TPU v7x, 32 devices: a whole 2x2x4 slice. The times are simulated.
32 devices in a mesh: dp: 16 (over z, y, core), mp: 2 (over x).
Axes of the slice: x: 2, y: 2, z: 4, core: 2. Of those that a mesh axis runs over, the one named last changes fastest.
Arguments:
- layer_input: bfloat16 [49152, 1024], P('dp'), may hold values from -11 to 11
- out_cotangent: bfloat16 [49152, 1024], P(('dp', 'mp')), may hold values from -6 to 6
- segment_ids: int32 [16, 3072], P('dp'), may hold values from 0 to 2, as said below
- qkv_weight: float32 [3, 1024, 1024], P(None, 'dp', 'mp'), may hold values from -0.1875 to 0.1875
- out_weight: float32 [1024, 1024], P('dp', 'mp'), may hold values from -6 to 6
- up_weight: float32 [1024, 4096], P('dp', 'mp'), may hold values from -0.1875 to 0.1875
- down_weight: float32 [1024, 4096], P('dp', 'mp'), may hold values from -0.09375 to 0.09375
- norm_gains: float32 [2, 1024], replicated, may hold values from 0.5 to 1.5
- bias_rows: float32 [6, 1024], replicated, may hold values from -4 to 4
- up_bias: float32 [4096], replicated, may hold values from -4 to 4
- qkv_moments: float32 [2, 3, 1024, 1024], P(None, None, 'dp', 'mp'), may hold values from -2 to 2, as said below
- out_moments: float32 [2, 1024, 1024], P(None, 'dp', 'mp'), may hold values from -2 to 2, as said below
- up_moments: float32 [2, 1024, 4096], P(None, 'dp', 'mp'), may hold values from -2 to 2, as said below
- down_moments: float32 [2, 1024, 4096], P(None, 'dp', 'mp'), may hold values from -2 to 2, as said below
- gain_moments: float32 [2, 2, 1024], replicated, may hold values from -2 to 2, as said below
- bias_moments: float32 [2, 6, 1024], replicated, may hold values from -2 to 2, as said below
- up_bias_moments: float32 [2, 4096], replicated, may hold values from -2 to 2, as said below
Outputs:
- layer_output: bfloat16 [49152, 1024], P(('dp', 'mp'))
- input_grad: float32 [49152, 1024], P(('dp', 'mp'))
- new_qkv: float32 [3, 1024, 1024], P(None, 'dp', 'mp')
- new_out: float32 [1024, 1024], P('dp', 'mp')
- new_up: float32 [1024, 4096], P('dp', 'mp')
- new_down: float32 [1024, 4096], P('dp', 'mp')
- new_gains: float32 [2, 1024], replicated
- new_biases: float32 [6, 1024], replicated
- new_up_bias: float32 [4096], replicated
- next_qkv_moments: float32 [2, 3, 1024, 1024], P(None, None, 'dp', 'mp')
- next_out_moments: float32 [2, 1024, 1024], P(None, 'dp', 'mp')
- next_up_moments: float32 [2, 1024, 4096], P(None, 'dp', 'mp')
- next_down_moments: float32 [2, 1024, 4096], P(None, 'dp', 'mp')
- next_gain_moments: float32 [2, 2, 1024], replicated
- next_bias_moments: float32 [2, 6, 1024], replicated
- next_up_bias_moments: float32 [2, 4096], replicated
Inputs may be any that keep to these rules, and one draw needn't show every extreme that they name: `segment_ids`: ids never fall along a sequence and start at 0; a sequence holds at most three documents, one of which begins within its first 384 tokens and ends within its last 384. `qkv_moments`: index 0 of the first dimension holds first moments, index 1 positive second moments. `out_moments`: index 0 of the first dimension holds first moments, index 1 positive second moments. `up_moments`: index 0 of the first dimension holds first moments, index 1 positive second moments. `down_moments`: index 0 of the first dimension holds first moments, index 1 positive second moments. `gain_moments`: index 0 of the first dimension holds first moments, index 1 positive second moments. `bias_moments`: index 0 of the first dimension holds first moments, index 1 positive second moments. `up_bias_moments`: index 0 of the first dimension holds first moments, index 1 positive second moments.
All inputs are finite; a program needn't handle non-finite values.
Results may differ from a plain program's by a relative error of at most 0.019.
The roundings to bfloat16 on the way count: a program that leaves them out, or rounds other values in their place, can miss the bound.
Values may be sent and summed in bfloat16 or wider, within the bound.
No kernel may reach another device: no remote copies, remote signals or barrier semaphores. Data moves between devices by JAX's collectives and lax.ppermute only.
A program may use at most 384 MiB of HBM per device.

v0:
```python
import jax
import jax.numpy as jnp
from jax import lax
from jax.sharding import PartitionSpec as P

HEADS = 16
HEAD_DIM = 64
ADAM_STEP = 5


very_low = -1e30
clip_tau = 5.0
learn_rate = 0.25
weight_decay = 0.1
moment_beta = 0.5
adam_epsilon = 1e-08


def norm_rows(values, gain_row, shift_row):
    center = values - jnp.mean(values, axis=-1, keepdims=True)
    spread = jnp.mean(center * center, axis=-1, keepdims=True)
    return center * lax.rsqrt(spread + 1e-05) * gain_row + shift_row


def gelu_exact(values):
    return jax.nn.gelu(values, approximate=False)


def times_transposed(left_side, right_side):
    return lax.dot_general(
        left_side, right_side, (((1,), (1,)), ((), ())), preferred_element_type=jnp.float32
    )


def transposed_times(left_side, right_side):
    return lax.dot_general(
        left_side, right_side, (((0,), (0,)), ((), ())), preferred_element_type=jnp.float32
    )


def adam_update(param, moments, grad, step_value):
    first_moment = moment_beta * moments[0] + (1.0 - moment_beta) * grad
    second_moment = moment_beta * moments[1] + (1.0 - moment_beta) * grad * grad
    correct = 1.0 - jnp.power(moment_beta, step_value)
    update = first_moment / correct / (jnp.sqrt(second_moment / correct) + adam_epsilon)
    return (
        param - learn_rate * (update + weight_decay * param),
        jnp.stack([first_moment, second_moment]),
    )


def place_columns(values, column_start, full_width):
    return lax.dynamic_update_slice_in_dim(
        jnp.zeros((full_width,), jnp.float32), values, column_start, 0
    )


def attention_forward(queries, keys_all, values_all, segment_ids, heads_local):
    token_total = queries.shape[0]
    seq_len = segment_ids.shape[1]
    block_rows = min(512, seq_len)
    score_scale = HEAD_DIM ** (-0.5)
    flat_ids = segment_ids.reshape(-1)

    def attention_one_block(block_index):
        row_first = block_index * block_rows
        query_block = lax.dynamic_slice_in_dim(queries, row_first, block_rows, 0).reshape(
            block_rows, heads_local, HEAD_DIM
        )
        key_heads = keys_all.reshape(seq_len, heads_local, HEAD_DIM)
        value_heads = values_all.reshape(seq_len, heads_local, HEAD_DIM)
        query_ids = lax.dynamic_slice_in_dim(flat_ids, row_first, block_rows, 0)
        scores = (
            jnp.einsum("qhd,khd->hqk", query_block, key_heads, preferred_element_type=jnp.float32)
            * score_scale
        )
        allowed = (query_ids[:, None] == flat_ids[None, :])[None]
        masked = jnp.where(allowed, scores, very_low)
        row_max = jnp.max(masked, axis=-1, keepdims=True)
        expd = jnp.exp(masked - row_max)
        row_total = jnp.sum(expd, axis=-1, keepdims=True)
        probs = (expd / row_total).astype(jnp.bfloat16)
        output = jnp.einsum("hqk,khd->qhd", probs, value_heads, preferred_element_type=jnp.float32)
        output = output.astype(jnp.bfloat16).reshape(block_rows, heads_local * HEAD_DIM)
        log_sum = (row_max + jnp.log(row_total))[..., 0]
        return (output, log_sum, jnp.max(row_max[..., 0], axis=1))

    outputs, log_sums, maxima = lax.map(attention_one_block, jnp.arange(token_total // block_rows))
    return (outputs.reshape(token_total, heads_local * HEAD_DIM), log_sums, jnp.max(maxima, axis=0))


def attention_backward(
    queries, keys_all, values_all, attended_grad, log_sums, segment_ids, heads_local
):
    seq_count = segment_ids.shape[0]
    seq_len = segment_ids.shape[1]
    block_rows = min(512, seq_len)
    per_seq = seq_len // block_rows
    width_local = heads_local * HEAD_DIM
    score_scale = HEAD_DIM ** (-0.5)
    flat_ids = segment_ids.reshape(-1)

    def one_sequence(seq_index):
        seq_first = seq_index * seq_len
        key_heads = keys_all.reshape(seq_len, heads_local, HEAD_DIM)
        value_heads = values_all.reshape(seq_len, heads_local, HEAD_DIM)

        def one_one_block(running, block_index):
            key_acc, value_acc = running
            row_first = seq_first + block_index * block_rows
            query_block = lax.dynamic_slice_in_dim(queries, row_first, block_rows, 0).reshape(
                block_rows, heads_local, HEAD_DIM
            )
            grad_block = lax.dynamic_slice_in_dim(attended_grad, row_first, block_rows, 0).reshape(
                block_rows, heads_local, HEAD_DIM
            )
            query_ids = lax.dynamic_slice_in_dim(flat_ids, row_first, block_rows, 0)
            log_block = lax.dynamic_index_in_dim(
                log_sums, seq_index * per_seq + block_index, 0, keepdims=False
            )
            scores = (
                jnp.einsum(
                    "qhd,khd->hqk", query_block, key_heads, preferred_element_type=jnp.float32
                )
                * score_scale
            )
            allowed = (query_ids[:, None] == flat_ids[None, :])[None]
            masked = jnp.where(allowed, scores, very_low)
            probs = jnp.exp(masked - log_block[:, :, None])
            prob_low = probs.astype(jnp.bfloat16)
            value_acc = value_acc + jnp.einsum(
                "hqk,qhd->khd", prob_low, grad_block, preferred_element_type=jnp.float32
            )
            prob_grad = jnp.einsum(
                "qhd,khd->hqk", grad_block, value_heads, preferred_element_type=jnp.float32
            )
            score_grad = probs * (prob_grad - jnp.sum(probs * prob_grad, axis=-1, keepdims=True))
            score_low = score_grad.astype(jnp.bfloat16)
            query_grad = (
                jnp.einsum("hqk,khd->qhd", score_low, key_heads, preferred_element_type=jnp.float32)
                * score_scale
            )
            key_acc = (
                key_acc
                + jnp.einsum(
                    "hqk,qhd->khd", score_low, query_block, preferred_element_type=jnp.float32
                )
                * score_scale
            )
            return ((key_acc, value_acc), query_grad.reshape(block_rows, width_local))

        zeros_heads = jnp.zeros((seq_len, heads_local, HEAD_DIM), jnp.float32)
        (key_acc, value_acc), query_blocks = lax.scan(
            one_one_block, (zeros_heads, zeros_heads), jnp.arange(per_seq)
        )
        return (
            query_blocks.reshape(seq_len, width_local),
            key_acc.reshape(seq_len, width_local),
            value_acc.reshape(seq_len, width_local),
        )

    query_grad, key_grad, value_grad = lax.map(one_sequence, jnp.arange(seq_count))
    total_rows = seq_count * seq_len
    return (
        query_grad.reshape(total_rows, width_local),
        key_grad.reshape(total_rows, width_local),
        value_grad.reshape(total_rows, width_local),
    )


def body(
    layer_input,
    out_cotangent,
    segment_ids,
    qkv_weight,
    out_weight,
    up_weight,
    down_weight,
    norm_gains,
    bias_rows,
    up_bias,
    qkv_moments,
    out_moments,
    up_moments,
    down_moments,
    gain_moments,
    bias_moments,
    up_bias_moments,
):
    group_size = lax.axis_size("mp")
    group_index = lax.axis_index("mp")
    heads_local = HEADS // group_size
    width_local = qkv_weight.shape[2]
    units_local = up_weight.shape[1]
    token_total = layer_input.shape[0]
    row_count = token_total // group_size
    row_start = group_index * row_count
    column_start = group_index * width_local
    unit_start = group_index * units_local
    qkv_full, out_full, up_full, down_full = (
        lax.all_gather(qkv_weight.astype(jnp.bfloat16), "dp", axis=1, tiled=True),
        lax.all_gather(out_weight.astype(jnp.bfloat16), "dp", axis=0, tiled=True),
        lax.all_gather(up_weight.astype(jnp.bfloat16), "dp", axis=0, tiled=True),
        lax.all_gather(down_weight.astype(jnp.bfloat16), "dp", axis=0, tiled=True),
    )
    query_bias = lax.dynamic_slice_in_dim(bias_rows[0], column_start, width_local)
    value_bias = lax.dynamic_slice_in_dim(bias_rows[1], column_start, width_local)
    projected = jnp.einsum("td,cde->cte", layer_input, qkv_full, preferred_element_type=jnp.float32)
    queries = (projected[0] + query_bias).astype(jnp.bfloat16)
    keys_all = projected[1].astype(jnp.bfloat16)
    values_all = (projected[2] + value_bias).astype(jnp.bfloat16)
    attended, log_sums, head_max = attention_forward(
        queries, keys_all, values_all, segment_ids, heads_local
    )
    row_piece = attended
    branch_rows = lax.psum_scatter(
        times_transposed(row_piece, out_full), "mp", scatter_dimension=0, tiled=True
    )
    input_rows = lax.dynamic_slice_in_dim(layer_input, row_start, row_count, 0).astype(jnp.float32)
    summed = input_rows + branch_rows + bias_rows[2]
    normed, first_norm_pull = jax.vjp(norm_rows, summed, norm_gains[0], bias_rows[4])
    normed_low = normed.astype(jnp.bfloat16)
    normed_all = lax.all_gather(normed_low, "mp", axis=0, tiled=True)
    unit_bias = lax.dynamic_slice_in_dim(up_bias, unit_start, units_local)
    pre_act = jnp.dot(normed_all, up_full, preferred_element_type=jnp.float32) + unit_bias
    hidden, gelu_pull = jax.vjp(gelu_exact, pre_act)
    hidden_low = hidden.astype(jnp.bfloat16)
    row_piece = hidden_low
    ffn_out = lax.psum_scatter(
        times_transposed(row_piece, down_full), "mp", scatter_dimension=0, tiled=True
    )
    total = normed + ffn_out + bias_rows[3]
    result, second_norm_pull = jax.vjp(norm_rows, total, norm_gains[1], bias_rows[5])
    total_grad, second_gain_grad, second_shift_grad = second_norm_pull(
        out_cotangent.astype(jnp.float32)
    )
    total_low = total_grad.astype(jnp.bfloat16)
    total_all = lax.all_gather(total_low, "mp", axis=0, tiled=True)
    down_grad = transposed_times(total_all, hidden_low)
    hidden_grad = jnp.dot(total_all, down_full, preferred_element_type=jnp.float32)
    pre_grad = gelu_pull(hidden_grad)[0]
    up_bias_grad = place_columns(jnp.sum(pre_grad, axis=0), unit_start, up_bias.shape[0])
    pre_low = pre_grad.astype(jnp.bfloat16)
    up_grad = transposed_times(normed_all, pre_low)
    row_piece = pre_low
    normed_grad = lax.psum_scatter(
        times_transposed(row_piece, up_full), "mp", scatter_dimension=0, tiled=True
    )
    summed_grad, first_gain_grad, first_shift_grad = first_norm_pull(normed_grad + total_grad)
    summed_low = summed_grad.astype(jnp.bfloat16)
    summed_all = lax.all_gather(summed_low, "mp", axis=0, tiled=True)
    out_grad = transposed_times(summed_all, attended)
    attended_grad = jnp.dot(summed_all, out_full, preferred_element_type=jnp.float32).astype(
        jnp.bfloat16
    )
    query_grad, key_grad, value_grad = attention_backward(
        queries, keys_all, values_all, attended_grad, log_sums, segment_ids, heads_local
    )
    stacked = jnp.stack(
        [
            query_grad.astype(jnp.bfloat16),
            key_grad.astype(jnp.bfloat16),
            value_grad.astype(jnp.bfloat16),
        ]
    )
    qkv_grad = jnp.einsum("td,cte->cde", layer_input, stacked, preferred_element_type=jnp.float32)
    row_piece = stacked
    input_grad = (
        lax.psum_scatter(
            jnp.einsum("cte,cde->td", row_piece, qkv_full, preferred_element_type=jnp.float32),
            "mp",
            scatter_dimension=0,
            tiled=True,
        )
        + summed_grad
    )
    width_full = bias_rows.shape[1]
    gain_grad = jnp.stack([first_gain_grad, second_gain_grad])
    bias_grad = jnp.stack(
        [
            place_columns(jnp.sum(query_grad, axis=0), column_start, width_full),
            place_columns(jnp.sum(value_grad, axis=0), column_start, width_full),
            jnp.sum(summed_grad, axis=0),
            jnp.sum(total_grad, axis=0),
            first_shift_grad,
            second_shift_grad,
        ]
    )
    gain_sum, bias_sum, unit_sum = lax.psum((gain_grad, bias_grad, up_bias_grad), ("dp", "mp"))
    local_max = lax.pmax(head_max, "dp")
    qkv_part, out_part, up_part, down_part = (
        lax.psum_scatter(qkv_grad, "dp", scatter_dimension=1, tiled=True),
        lax.psum_scatter(out_grad, "dp", scatter_dimension=0, tiled=True),
        lax.psum_scatter(up_grad, "dp", scatter_dimension=0, tiled=True),
        lax.psum_scatter(down_grad, "dp", scatter_dimension=0, tiled=True),
    )
    grad_scale = lax.rsqrt(jnp.float32(token_total * lax.axis_size("dp")))
    step_value = jnp.float32(ADAM_STEP)
    new_qkv, next_qkv = adam_update(qkv_weight, qkv_moments, qkv_part * grad_scale, step_value)
    new_out, next_out = adam_update(out_weight, out_moments, out_part * grad_scale, step_value)
    new_up, next_up = adam_update(up_weight, up_moments, up_part * grad_scale, step_value)
    new_down, next_down = adam_update(down_weight, down_moments, down_part * grad_scale, step_value)
    new_gains, next_gains = adam_update(norm_gains, gain_moments, gain_sum * grad_scale, step_value)
    new_biases, next_biases = adam_update(
        bias_rows, bias_moments, bias_sum * grad_scale, step_value
    )
    new_up_bias, next_up_bias = adam_update(
        up_bias, up_bias_moments, unit_sum * grad_scale, step_value
    )
    factor = jnp.sqrt(clip_tau / jnp.maximum(local_max, clip_tau))
    column = jnp.repeat(factor, HEAD_DIM)
    scales = jnp.stack([column, column, jnp.ones_like(column)])[:, None, :]
    new_qkv = new_qkv * scales
    return (
        result.astype(jnp.bfloat16),
        input_grad,
        new_qkv,
        new_out,
        new_up,
        new_down,
        new_gains,
        new_biases,
        new_up_bias,
        next_qkv,
        next_out,
        next_up,
        next_down,
        next_gains,
        next_biases,
        next_up_bias,
    )


def solution(mesh):
    placed = (
        P("dp", None),
        P(("dp", "mp"), None),
        P("dp", None),
        P(None, "dp", "mp"),
        P("dp", "mp"),
        P("dp", "mp"),
        P("dp", "mp"),
        P(),
        P(),
        P(),
        P(None, None, "dp", "mp"),
        P(None, "dp", "mp"),
        P(None, "dp", "mp"),
        P(None, "dp", "mp"),
        P(),
        P(),
        P(),
    )
    return jax.shard_map(
        body,
        mesh=mesh,
        in_specs=placed,
        out_specs=(
            P(("dp", "mp"), None),
            P(("dp", "mp"), None),
            P(None, "dp", "mp"),
            P("dp", "mp"),
            P("dp", "mp"),
            P("dp", "mp"),
            P(),
            P(),
            P(),
            P(None, None, "dp", "mp"),
            P(None, "dp", "mp"),
            P(None, "dp", "mp"),
            P(None, "dp", "mp"),
            P(),
            P(),
            P(),
        ),
        check_vma=False,
    )
```

profile of v0, /device:TPU:0, one launch (start us, length us, event | category | flops | bytes accessed | tf_op | source)
XLA Modules:
  0.0 2877.6 jit_solution(14402613618211470643)
XLA Ops:
  14.0 44.7 %all-gather.8.cloned.1.call-done = bf16[3,1024,512]{2,1,0:T(8,128)(2,1)} async-done(((bf16[3,64,512]{2,1,0:T(8,128)(2,1)}), bf16[3,1024,512]{2,1,0:T(8,128)(2,1)}) %all-gather.8.cloned.1.call-update) | async-done | bytes 3145744 | tf_op jit(solution)/shard_map/all_gather | solution.py:201
  81.1 434.1 %while.43 = (s32[]{:T(128)}, bf16[6,512,512]{2,1,0:T(8,128)(2,1)}, f32[6,8,512]{2,1,0:T(8,128)}, f32[6,8]{1,0:T(8,128)}, s32[6]{0:T(128)S(1)}, /*index=5*/s32[30...) while((s32[]{:T(128)}, bf16[6,512,512]{2,1,0:T(8,128)(2,1)}, ...), condition=%wide.region_4.5_spmd, body=%wide.region_0.4_spmd.sunk | while | flops 3386634240 | bytes 180504912 | solution.py:88
  84.6 22.6 fusion.133
  107.3 23.3 fusion.134
  130.5 20.1 fusion.135
  157.0 22.5 fusion.133
  179.5 23.3 fusion.134
  202.7 20.1 fusion.135
  229.2 22.5 fusion.133
  251.7 23.3 fusion.134
  275.0 20.1 fusion.135
  301.4 22.5 fusion.133
  324.0 23.3 fusion.134
  347.2 20.1 fusion.135
  373.7 22.5 fusion.133
  396.2 23.3 fusion.134
  419.5 20.1 fusion.135
  445.9 22.5 fusion.133
  468.4 23.3 fusion.134
  491.7 20.1 fusion.135
  527.9 141.1 %reduce-scatter.8.cloned.1.call-done = f32[1536,1024]{1,0:T(8,128)} async-done(((f32[3072,1024]{1,0:T(8,128)}), f32[1536,1024]{1,0:T(8,128)}) %reduce-scatter.8.cloned.1.call-update) | async-done | bytes 6291472 | tf_op jit(solution)/shard_map/reduce_scatter | solution.py:216
  679.7 42.5 %all-gather.14.cloned.1.call-done = bf16[1024,2048]{1,0:T(8,128)(2,1)} async-done(((bf16[64,2048]{1,0:T(8,128)(2,1)}), bf16[1024,2048]{1,0:T(8,128)(2,1)}) %all-gather.14.cloned.1.call-update) | async-done | bytes 4194320 | tf_op jit(solution)/shard_map/all_gather | solution.py:203
  722.2 80.9 %all-gather.12.cloned.1.call-done = bf16[3072,1024]{1,0:T(8,128)(2,1)} async-done(((bf16[1536,1024]{1,0:T(8,128)(2,1)}), bf16[3072,1024]{1,0:T(8,128)(2,1)}) %all-gather.12.cloned.1.call-update) | async-done | bytes 6291472 | tf_op jit(solution)/shard_map/all_gather | solution.py:223
  803.0 70.7 %multiply_convert_fusion.1 = (bf16[3072,2048]{1,0:T(8,128)(2,1)}, f32[3072,2048]{1,0:T(8,128)}, f32[3072,2048]{1,0:T(8,128)}) fusion(f32[2048]{0:T(1024)S(1)} %dynamic_slice.64, bf16[3072,1024]{1,0:T(8,128)(2,1)} %all-gather.12.cloned.1.call-done, bf16[1024,2048]{1,0:T(8,128)(2,1)} %all-gather.14.cloned.1.call-done), kind=kOutput, calls=%fused_computation.33 | convolution fusion | flops 13300137984 | bytes 73408512 | tf_op jit(solution)/shard_map/dot_general | solution.py:225
  873.8 19.2 fusion.78
  893.1 144.6 %reduce-scatter.10.cloned.1.call-done = f32[1536,1024]{1,0:T(8,128)} async-done(((f32[3072,1024]{1,0:T(8,128)}), f32[1536,1024]{1,0:T(8,128)}) %reduce-scatter.10.cloned.1.call-update) | async-done | bytes 6291472 | tf_op jit(solution)/shard_map/reduce_scatter | solution.py:229
  1059.1 80.5 %all-gather.18.cloned.1.call-done = bf16[3072,1024]{1,0:T(8,128)(2,1)} async-done(((bf16[1536,1024]{1,0:T(8,128)(2,1)}), bf16[3072,1024]{1,0:T(8,128)(2,1)}) %all-gather.18.cloned.1.call-update) | async-done | bytes 6291472 | tf_op jit(solution)/shard_map/all_gather | solution.py:238
  1139.6 34.5 %fusion.75 = (f32[2048]{0:T(1024)}, bf16[3072,2048]{1,0:T(8,128)(2,1)}) fusion(f32[3072,2048]{1,0:T(8,128)} %get-tuple-element.497, bf16[3072,1024]{1,0:T(8,128)(2,1)} %all-gather.18.cloned.1.call-done, bf16[1024,2048]{1,0:T(8,128)(2,1)} %all-gather.16.cloned.1.call-done, f32[3072,2048]{1,0:T(8,128)} %get-tuple-element.547, f32[2048]{0:T(1024)S(1)} %dynamic_slice.64), kind=kOutput, calls=%fused_computation.173 | convolution fusion | flops 12985563136 | bytes 73416704 | tf_op jit(solution)/shard_map/dot_general | solution.py:240
  1174.1 19.1 fusion.33
  1193.3 144.6 %reduce-scatter.12.cloned.1.call-done = f32[1536,1024]{1,0:T(8,128)} async-done(((f32[3072,1024]{1,0:T(8,128)}), f32[1536,1024]{1,0:T(8,128)}) %reduce-scatter.12.cloned.1.call-update) | async-done | bytes 6291472 | tf_op jit(solution)/shard_map/reduce_scatter | solution.py:246
  1356.8 19.0 fusion.80
  1387.0 17.2 fusion.31
  1404.3 32.9 %all-gather.20.cloned.1.call-done = bf16[3072,1024]{1,0:T(8,128)(2,1)} async-done(((bf16[1536,1024]{1,0:T(8,128)(2,1)}), bf16[3072,1024]{1,0:T(8,128)(2,1)}) %all-gather.20.cloned.1.call-update) | async-done | bytes 6291472 | tf_op jit(solution)/shard_map/all_gather | solution.py:251
  1444.9 985.9 %while.44 = (s32[]{:T(128)}, f32[3072,8,64]{0,2,1:T(8,128)}, f32[3072,8,64]{0,2,1:T(8,128)}, f32[6,512,512]{1,2,0:T(8,128)}, s32[6]{0:T(128)S(1)}, /*index=5*/bf...) while((s32[]{:T(128)}, f32[3072,8,64]{0,2,1:T(8,128)}, ...), condition=%wide.region_18.19_spmd.clone, body=%wide.region_16.18_spmd.clone.sunk | while | flops 8251502592 | bytes 426903808 | solution.py:153
  1452.4 23.6 fusion.146
  1476.0 23.9 bitcast_add_fusion.14
  1499.9 37.5 %multiply_reduce_fusion.6 = (f32[8,512]{1,0:T(8,128)S(1)}, f32[8,512,3072]{2,1,0:T(8,128)}) fusion(f32[8,512,3072]{2,1,0:T(8,128)} %fusion.146, f32[8,512]{1,0:T(8,128)S(1)} %dynamic-slice_bitcast_fusion.2, pred[512,3072]{1,0:T(8,128)(4,1)S(1)} %broadcast_compare_fusion.5, bf16[512,8,64]{0,2,1:T(8,128)(2,1)S(1)} %bitcast.275, ...), kind=kOutput, calls=%fused_computation.15.clone.1 | convolution fusion | flops 1673523200 | bytes 105938944 | tf_op jit(solution)/shard_map/while/body/eval_jaxpr/while/body/eval_jaxpr/qhd,khd->hqk/dot_general | solution.py:134
  1537.5 44.7 %multiply_convert_fusion.3 = bf16[8,512,3072]{2,1,0:T(8,128)(2,1)} fusion(f32[8,512,3072]{2,1,0:T(8,128)} %get-tuple-element.696, f32[8,512,3072]{2,1,0:T(8,128)} %fusion.146, f32[8,512]{1,0:T(8,128)S(1)} %get-tuple-element.697, f32[8,512]{1,0:T(8,128)S(1)} %dynamic-slice_bitcast_fusion.2, pred[512,3072]{1,0:T(8,128)(4,1)S(1)} %broadcast_compare_fusion.5), kind=kLoop, calls=%fused_computation.14.clone.1 | loop fusion | flops 75497472 | bytes 127434752 | tf_op jit(solution)/shard_map/while/body/eval_jaxpr/while/body/eval_jaxpr/convert_element_type | solution.py:138
  1619.4 21.9 fusion.146
  1641.3 25.7 bitcast_add_fusion.14
  1667.0 37.2 %multiply_reduce_fusion.6 = (f32[8,512]{1,0:T(8,128)S(1)}, f32[8,512,3072]{2,1,0:T(8,128)}) fusion(f32[8,512,3072]{2,1,0:T(8,128)} %fusion.146, f32[8,512]{1,0:T(8,128)S(1)} %dynamic-slice_bitcast_fusion.2, pred[512,3072]{1,0:T(8,128)(4,1)S(1)} %broadcast_compare_fusion.5, bf16[512,8,64]{0,2,1:T(8,128)(2,1)S(1)} %bitcast.275, ...), kind=kOutput, calls=%fused_computation.15.clone.1 | convolution fusion | flops 1673523200 | bytes 105938944 | tf_op jit(solution)/shard_map/while/body/eval_jaxpr/while/body/eval_jaxpr/qhd,khd->hqk/dot_general | solution.py:134
  1704.3 40.6 %multiply_convert_fusion.3 = bf16[8,512,3072]{2,1,0:T(8,128)(2,1)} fusion(f32[8,512,3072]{2,1,0:T(8,128)} %get-tuple-element.696, f32[8,512,3072]{2,1,0:T(8,128)} %fusion.146, f32[8,512]{1,0:T(8,128)S(1)} %get-tuple-element.697, f32[8,512]{1,0:T(8,128)S(1)} %dynamic-slice_bitcast_fusion.2, pred[512,3072]{1,0:T(8,128)(4,1)S(1)} %broadcast_compare_fusion.5), kind=kLoop, calls=%fused_computation.14.clone.1 | loop fusion | flops 75497472 | bytes 127434752 | tf_op jit(solution)/shard_map/while/body/eval_jaxpr/while/body/eval_jaxpr/convert_element_type | solution.py:138
  1783.7 21.2 fusion.146
  1805.0 25.6 bitcast_add_fusion.14
  1830.6 37.2 %multiply_reduce_fusion.6 = (f32[8,512]{1,0:T(8,128)S(1)}, f32[8,512,3072]{2,1,0:T(8,128)}) fusion(f32[8,512,3072]{2,1,0:T(8,128)} %fusion.146, f32[8,512]{1,0:T(8,128)S(1)} %dynamic-slice_bitcast_fusion.2, pred[512,3072]{1,0:T(8,128)(4,1)S(1)} %broadcast_compare_fusion.5, bf16[512,8,64]{0,2,1:T(8,128)(2,1)S(1)} %bitcast.275, ...), kind=kOutput, calls=%fused_computation.15.clone.1 | convolution fusion | flops 1673523200 | bytes 105938944 | tf_op jit(solution)/shard_map/while/body/eval_jaxpr/while/body/eval_jaxpr/qhd,khd->hqk/dot_general | solution.py:134
  1867.8 40.6 %multiply_convert_fusion.3 = bf16[8,512,3072]{2,1,0:T(8,128)(2,1)} fusion(f32[8,512,3072]{2,1,0:T(8,128)} %get-tuple-element.696, f32[8,512,3072]{2,1,0:T(8,128)} %fusion.146, f32[8,512]{1,0:T(8,128)S(1)} %get-tuple-element.697, f32[8,512]{1,0:T(8,128)S(1)} %dynamic-slice_bitcast_fusion.2, pred[512,3072]{1,0:T(8,128)(4,1)S(1)} %broadcast_compare_fusion.5), kind=kLoop, calls=%fused_computation.14.clone.1 | loop fusion | flops 75497472 | bytes 127434752 | tf_op jit(solution)/shard_map/while/body/eval_jaxpr/while/body/eval_jaxpr/convert_element_type | solution.py:138
  1947.2 21.2 fusion.146
  1968.5 25.6 bitcast_add_fusion.14
  1994.1 37.2 %multiply_reduce_fusion.6 = (f32[8,512]{1,0:T(8,128)S(1)}, f32[8,512,3072]{2,1,0:T(8,128)}) fusion(f32[8,512,3072]{2,1,0:T(8,128)} %fusion.146, f32[8,512]{1,0:T(8,128)S(1)} %dynamic-slice_bitcast_fusion.2, pred[512,3072]{1,0:T(8,128)(4,1)S(1)} %broadcast_compare_fusion.5, bf16[512,8,64]{0,2,1:T(8,128)(2,1)S(1)} %bitcast.275, ...), kind=kOutput, calls=%fused_computation.15.clone.1 | convolution fusion | flops 1673523200 | bytes 105938944 | tf_op jit(solution)/shard_map/while/body/eval_jaxpr/while/body/eval_jaxpr/qhd,khd->hqk/dot_general | solution.py:134
  2031.3 40.6 %multiply_convert_fusion.3 = bf16[8,512,3072]{2,1,0:T(8,128)(2,1)} fusion(f32[8,512,3072]{2,1,0:T(8,128)} %get-tuple-element.696, f32[8,512,3072]{2,1,0:T(8,128)} %fusion.146, f32[8,512]{1,0:T(8,128)S(1)} %get-tuple-element.697, f32[8,512]{1,0:T(8,128)S(1)} %dynamic-slice_bitcast_fusion.2, pred[512,3072]{1,0:T(8,128)(4,1)S(1)} %broadcast_compare_fusion.5), kind=kLoop, calls=%fused_computation.14.clone.1 | loop fusion | flops 75497472 | bytes 127434752 | tf_op jit(solution)/shard_map/while/body/eval_jaxpr/while/body/eval_jaxpr/convert_element_type | solution.py:138
  2085.2 17.1 bitcast_add_fusion.13
  2110.7 21.2 fusion.146
  2132.0 25.6 bitcast_add_fusion.14
  2157.5 37.2 %multiply_reduce_fusion.6 = (f32[8,512]{1,0:T(8,128)S(1)}, f32[8,512,3072]{2,1,0:T(8,128)}) fusion(f32[8,512,3072]{2,1,0:T(8,128)} %fusion.146, f32[8,512]{1,0:T(8,128)S(1)} %dynamic-slice_bitcast_fusion.2, pred[512,3072]{1,0:T(8,128)(4,1)S(1)} %broadcast_compare_fusion.5, bf16[512,8,64]{0,2,1:T(8,128)(2,1)S(1)} %bitcast.275, ...), kind=kOutput, calls=%fused_computation.15.clone.1 | convolution fusion | flops 1673523200 | bytes 105938944 | tf_op jit(solution)/shard_map/while/body/eval_jaxpr/while/body/eval_jaxpr/qhd,khd->hqk/dot_general | solution.py:134
  2194.8 40.6 %multiply_convert_fusion.3 = bf16[8,512,3072]{2,1,0:T(8,128)(2,1)} fusion(f32[8,512,3072]{2,1,0:T(8,128)} %get-tuple-element.696, f32[8,512,3072]{2,1,0:T(8,128)} %fusion.146, f32[8,512]{1,0:T(8,128)S(1)} %get-tuple-element.697, f32[8,512]{1,0:T(8,128)S(1)} %dynamic-slice_bitcast_fusion.2, pred[512,3072]{1,0:T(8,128)(4,1)S(1)} %broadcast_compare_fusion.5), kind=kLoop, calls=%fused_computation.14.clone.1 | loop fusion | flops 75497472 | bytes 127434752 | tf_op jit(solution)/shard_map/while/body/eval_jaxpr/while/body/eval_jaxpr/convert_element_type | solution.py:138
  2274.2 21.2 fusion.146
  2295.4 25.6 bitcast_add_fusion.14
  2321.0 37.2 %multiply_reduce_fusion.6 = (f32[8,512]{1,0:T(8,128)S(1)}, f32[8,512,3072]{2,1,0:T(8,128)}) fusion(f32[8,512,3072]{2,1,0:T(8,128)} %fusion.146, f32[8,512]{1,0:T(8,128)S(1)} %dynamic-slice_bitcast_fusion.2, pred[512,3072]{1,0:T(8,128)(4,1)S(1)} %broadcast_compare_fusion.5, bf16[512,8,64]{0,2,1:T(8,128)(2,1)S(1)} %bitcast.275, ...), kind=kOutput, calls=%fused_computation.15.clone.1 | convolution fusion | flops 1673523200 | bytes 105938944 | tf_op jit(solution)/shard_map/while/body/eval_jaxpr/while/body/eval_jaxpr/qhd,khd->hqk/dot_general | solution.py:134
  2358.3 40.6 %multiply_convert_fusion.3 = bf16[8,512,3072]{2,1,0:T(8,128)(2,1)} fusion(f32[8,512,3072]{2,1,0:T(8,128)} %get-tuple-element.696, f32[8,512,3072]{2,1,0:T(8,128)} %fusion.146, f32[8,512]{1,0:T(8,128)S(1)} %get-tuple-element.697, f32[8,512]{1,0:T(8,128)S(1)} %dynamic-slice_bitcast_fusion.2, pred[512,3072]{1,0:T(8,128)(4,1)S(1)} %broadcast_compare_fusion.5), kind=kLoop, calls=%fused_computation.14.clone.1 | loop fusion | flops 75497472 | bytes 127434752 | tf_op jit(solution)/shard_map/while/body/eval_jaxpr/while/body/eval_jaxpr/convert_element_type | solution.py:138
  2507.7 35.0 %pmax.7 = f32[8]{0:T(128)S(1)} all-reduce(f32[8]{0:T(128)S(1)} %reduce_max.27), channel_id=1, replica_groups=mesh['dp'=16,'mp'=2] {'dp'}, use_global_device_ids=true, to_apply=%region_22.23 | all-reduce | flops 8 | bytes 64 | tf_op jit(solution)/shard_map/pmax | solution.py:290
  2550.6 38.1 %all-reduce.1 = (f32[2,1024]{1,0:T(2,128)S(1)}, f32[6,1024]{1,0:T(8,128)S(1)}, f32[4096]{0:T(1024)S(1)}) all-reduce(f32[2,1024]{1,0:T(2,128)S(1)} %pad_maximum_fusion.12, f32[6,1024]{1,0:T(8,128)S(1)} %stack.104, f32[4096]{0:T(1024)S(1)} %dynamic_update_slice.40), channel_id=1, replica_groups=mesh['dp'=16,'mp'=2] {'dp','mp'}, use_global_device_ids=true, to_apply=%region_28.29 | all-reduce | flops 12288 | bytes 98304 | tf_op jit(solution)/shard_map/psum | solution.py:289
  2592.7 58.5 %all-reduce.4.cloned.1.call-done = f32[3,1024,512]{2,0,1:T(4,128)} async-done(((f32[3,1024,512]{2,0,1:T(4,128)}), f32[3,1024,512]{2,0,1:T(4,128)}) %all-reduce.4.cloned.1.call-update) | async-done | bytes 6291472
  2655.6 61.7 %reduce-scatter.16.cloned.1.call-done = f32[64,512]{1,0:T(8,128)} async-done(((f32[1024,512]{1,0:T(8,128)}), f32[64,512]{1,0:T(8,128)}) %reduce-scatter.16.cloned.1.call-update) | async-done | bytes 131088 | tf_op jit(solution)/shard_map/reduce_scatter | solution.py:293
  2719.7 143.2 %reduce-scatter.14.cloned.1.call-done = f32[1536,1024]{1,0:T(8,128)} async-done(((f32[3072,1024]{1,0:T(8,128)}), f32[1536,1024]{1,0:T(8,128)}) %reduce-scatter.14.cloned.1.call-update) | async-done | bytes 6291472 | tf_op jit(solution)/shard_map/reduce_scatter | solution.py:269
  (354 shorter events, 446.4 us)
Async XLA Ops:
  7.2 51.5 %all-gather.8.cloned.1.call-start = ((), (), s32[]{:S(2)}) async-start(), calls=%async_computation.7 | async-start | bytes 3342336 | tf_op jit(solution)/shard_map/all_gather | solution.py:201
  8.9 506.3 %all-gather.10.cloned.1.call-start = ((), (), s32[]{:S(2)}) async-start(), calls=%async_computation.8 | async-start | bytes 1114112 | tf_op jit(solution)/shard_map/all_gather | solution.py:202
  10.6 658.4 %reduce-scatter.8.cloned.1.call-start = ((), (), s32[]{:S(2)}) async-start(), calls=%async_computation.9 | async-start | bytes 18874368 | tf_op jit(solution)/shard_map/reduce_scatter | solution.py:216
  71.9 9.2 copy-start.3
  74.3 6.8 copy-start.11
  107.2 23.3 copy-start.5
  179.5 23.3 copy-start.5
  251.7 23.3 copy-start.5
  323.9 23.3 copy-start.5
  396.2 23.3 copy-start.5
  468.4 23.3 copy-start.5
  525.4 143.6 %copy-start.42 = (f32[1,1024]{1,0:T(1,128)S(1)}, f32[1,1024]{1,0:T(1,128)}, u32[]{:S(2)}) copy-start(f32[1,1024]{1,0:T(1,128)} %get-tuple-element.539) | copy-start | bytes 12292
  525.4 196.8 %all-gather.14.cloned.1.call-start = ((), (), s32[]{:S(2)}) async-start(), calls=%async_computation.11 | async-start | bytes 4456448 | tf_op jit(solution)/shard_map/all_gather | solution.py:203
  527.2 275.9 %all-gather.12.cloned.1.call-start = ((), (), s32[]{:S(2)}) async-start(), calls=%async_computation.10 | async-start | bytes 9437184 | tf_op jit(solution)/shard_map/all_gather | solution.py:223
  527.9 147.2 %copy-start.21 = (f32[1,1024]{1,0:T(1,128)}, f32[1,1024]{1,0:T(1,128)S(1)}, u32[]{:S(2)}) copy-start(f32[1,1024]{1,0:T(1,128)S(1)} %get-tuple-element.546) | copy-start | bytes 12292
  673.6 2.7 copy-start
  673.6 2.7 copy-start.32
  673.6 2.7 copy-start.16
  676.3 3.4 copy-start.30
  678.8 195.0 %all-gather.16.cloned.1.call-start = ((), (), s32[]{:S(2)}) async-start(), calls=%async_computation.12 | async-start | bytes 4456448 | tf_op jit(solution)/shard_map/all_gather | solution.py:204
  679.6 358.0 %reduce-scatter.10.cloned.1.call-start = ((), (), s32[]{:S(2)}) async-start(), calls=%async_computation.13 | async-start | bytes 18874368 | tf_op jit(solution)/shard_map/reduce_scatter | solution.py:229
  893.0 144.7 %copy-start.17 = (f32[1536]{0:T(1024)S(1)}, f32[1536]{0:T(1024)}, u32[]{:S(2)}) copy-start(f32[1536]{0:T(1024)} %copy-done.16) | copy-start | bytes 18436
  893.0 144.7 %copy-start.20 = (f32[1536]{0:T(1024)S(1)}, f32[1536]{0:T(1024)}, u32[]{:S(2)}) copy-start(f32[1536]{0:T(1024)} %copy-done.19) | copy-start | bytes 18436
  893.0 144.7 %copy-start.22 = (f32[1,1024]{1,0:T(1,128)S(1)}, f32[1,1024]{1,0:T(1,128)}, u32[]{:S(2)}) copy-start(f32[1,1024]{1,0:T(1,128)} %copy-done.21) | copy-start | bytes 12292
  893.0 144.7 %copy-start.33 = (f32[1,1024]{1,0:T(1,128)S(1)}, f32[1,1024]{1,0:T(1,128)}, u32[]{:S(2)}) copy-start(f32[1,1024]{1,0:T(1,128)} %get-tuple-element.538) | copy-start | bytes 12292
  893.0 144.7 %copy-start.46 = (f32[1,1024]{1,0:T(1,128)S(1)}, f32[1,1024]{1,0:T(1,128)}, u32[]{:S(2)}) copy-start(f32[1,1024]{1,0:T(1,128)} %get-tuple-element.537) | copy-start | bytes 12292
  893.0 246.6 %all-gather.18.cloned.1.call-start = ((), (), s32[]{:S(2)}) async-start(), calls=%async_computation.14 | async-start | bytes 9437184 | tf_op jit(solution)/shard_map/all_gather | solution.py:238
  1044.6 4.8 copy-start.41
  1059.1 278.8 %reduce-scatter.12.cloned.1.call-start = ((), (), s32[]{:S(2)}) async-start(), calls=%async_computation.15 | async-start | bytes 18874368 | tf_op jit(solution)/shard_map/reduce_scatter | solution.py:246
  1193.2 153.5 %copy-start.27 = (f32[1536]{0:T(1024)S(1)}, f32[1536]{0:T(1024)}, u32[]{:S(2)}) copy-start(f32[1536]{0:T(1024)} %copy-done.26) | copy-start | bytes 18436
  1193.3 244.0 %all-gather.20.cloned.1.call-start = ((), (), s32[]{:S(2)}) async-start(), calls=%async_computation.16 | async-start | bytes 9437184 | tf_op jit(solution)/shard_map/all_gather | solution.py:251
  1351.2 2.7 copy-start.1
  1351.2 5.5 copy-start.24
  1356.7 1186.5 %reduce-scatter.20.cloned.1.call-start = ((), (), s32[]{:S(2)}) async-start(), calls=%async_computation.20 | async-start | bytes 8912896 | tf_op jit(solution)/shard_map/reduce_scatter | solution.py:295
  1375.8 1170.8 %reduce-scatter.18.cloned.1.call-start = ((), (), s32[]{:S(2)}) async-start(), calls=%async_computation.19 | async-start | bytes 8912896 | tf_op jit(solution)/shard_map/reduce_scatter | solution.py:294
  1376.5 10.5 slice-start.1
  1381.6 2.8 slice-start
  1381.6 5.4 slice-start.2
  1404.2 33.0 %copy-start.50 = (bf16[1024,512]{1,0:T(8,128)(2,1)S(1)}, bf16[1024,512]{1,0:T(8,128)(2,1)}, u32[]{:S(2)}) copy-start(bf16[1024,512]{1,0:T(8,128)(2,1)} %all-gather.10.cloned.1.call-done) | copy-start | bytes 3145732
  1404.3 40.6 %copy-start.12 = (s32[1,3072]{1,0:T(1,128)S(1)}, s32[1,3072]{1,0:T(1,128)}, u32[]{:S(2)}) copy-start(s32[1,3072]{1,0:T(1,128)} %param.23) | copy-start | bytes 36868
  1404.3 1246.9 %all-reduce.4.cloned.1.call-start = ((), (), s32[]{:S(2)}) async-start(), calls=%async_computation.21 | async-start | bytes 16777216
  2479.5 8.7 copy-start.6
  2479.5 237.8 %reduce-scatter.16.cloned.1.call-start = ((), (), s32[]{:S(2)}) async-start(), calls=%async_computation.18 | async-start | bytes 2228224 | tf_op jit(solution)/shard_map/reduce_scatter | solution.py:293
  2488.2 374.8 %reduce-scatter.14.cloned.1.call-start = ((), (), s32[]{:S(2)}) async-start(), calls=%async_computation.17 | async-start | bytes 18874368 | tf_op jit(solution)/shard_map/reduce_scatter | solution.py:269
  2504.1 2.7 copy-start.36
  2504.1 2.8 copy-start.49
  2504.1 38.8 %copy-start.48 = (f32[2048]{0:T(1024)S(1)}, f32[2048]{0:T(1024)}, u32[]{:S(2)}) copy-start(f32[2048]{0:T(1024)} %get-tuple-element.548) | copy-start | bytes 24580
  2504.2 39.1 %copy-start.8 = (f32[64,2048]{1,0:T(8,128)S(1)}, f32[64,2048]{1,0:T(8,128)}, u32[]{:S(2)}) copy-start(f32[64,2048]{1,0:T(8,128)} %param.27) | copy-start | bytes 1572868
  2504.2 39.1 %copy-start.14 = (f32[2,64,2048]{2,1,0:T(8,128)S(1)}, f32[2,64,2048]{2,1,0:T(8,128)}, u32[]{:S(2)}) copy-start(f32[2,64,2048]{2,1,0:T(8,128)} %param.34) | copy-start | bytes 3145732
  2504.2 42.4 %copy-start.10 = (f32[64,2048]{1,0:T(8,128)S(1)}, f32[64,2048]{1,0:T(8,128)}, u32[]{:S(2)}) copy-start(f32[64,2048]{1,0:T(8,128)} %param.26) | copy-start | bytes 1572868
  2505.5 44.9 %copy-start.43 = (f32[1024]{0:T(1024)S(1)}, f32[1024]{0:T(1024)}, u32[]{:S(2)}) copy-start(f32[1024]{0:T(1024)} %get-tuple-element.433) | copy-start | bytes 12292
  2505.5 44.9 %copy-start.44 = (f32[1024]{0:T(1024)S(1)}, f32[1024]{0:T(1024)}, u32[]{:S(2)}) copy-start(f32[1024]{0:T(1024)} %get-tuple-element.431) | copy-start | bytes 12292
  2505.5 45.0 %copy-start.37 = (f32[1024]{0:T(1024)S(1)}, f32[1024]{0:T(1024)}, u32[]{:S(2)}) copy-start(f32[1024]{0:T(1024)} %get-tuple-element.510) | copy-start | bytes 12292
  2505.5 45.0 %copy-start.38 = (f32[1024]{0:T(1024)S(1)}, f32[1024]{0:T(1024)}, u32[]{:S(2)}) copy-start(f32[1024]{0:T(1024)} %get-tuple-element.512) | copy-start | bytes 12292
  2505.5 45.0 %copy-start.39 = (f32[1024]{0:T(1024)S(1)}, f32[1024]{0:T(1024)}, u32[]{:S(2)}) copy-start(f32[1024]{0:T(1024)} %get-tuple-element.436) | copy-start | bytes 12292
  2505.5 45.0 %copy-start.40 = (f32[1024]{0:T(1024)S(1)}, f32[1024]{0:T(1024)}, u32[]{:S(2)}) copy-start(f32[1024]{0:T(1024)} %get-tuple-element.435) | copy-start | bytes 12292
  2506.8 82.0 %copy-start.23 = (f32[6,1024]{1,0:T(8,128)S(1)}, f32[6,1024]{1,0:T(8,128)}, u32[]{:S(2)}) copy-start(f32[6,1024]{1,0:T(8,128)} %param.29) | copy-start | bytes 73732
  2506.8 83.3 %copy-start.35 = (f32[2,1024]{1,0:T(2,128)S(1)}, f32[2,1024]{1,0:T(2,128)}, u32[]{:S(2)}) copy-start(f32[2,1024]{1,0:T(2,128)} %param.28) | copy-start | bytes 24580
  2506.9 83.3 %copy-start.45 = (f32[2,2,1024]{2,1,0:T(2,128)S(1)}, f32[2,2,1024]{2,1,0:T(2,128)}, u32[]{:S(2)}) copy-start(f32[2,2,1024]{2,1,0:T(2,128)} %param.35) | copy-start | bytes 49156
  2506.9 84.5 %copy-start.31 = (f32[4096]{0:T(1024)S(1)}, f32[4096]{0:T(1024)}, u32[]{:S(2)}) copy-start(f32[4096]{0:T(1024)} %param.30) | copy-start | bytes 49156
  2506.9 144.3 %copy-start.13 = (f32[3,64,512]{2,1,0:T(8,128)S(1)}, f32[3,64,512]{2,1,0:T(8,128)}, u32[]{:S(2)}) copy-start(f32[3,64,512]{2,1,0:T(8,128)} %param.24) | copy-start | bytes 1179652
  2549.3 168.0 %copy-start.15 = (f32[64,512]{1,0:T(8,128)S(1)}, f32[64,512]{1,0:T(8,128)}, u32[]{:S(2)}) copy-start(f32[64,512]{1,0:T(8,128)} %param.25) | copy-start | bytes 393220
  2549.3 168.0 %copy-start.18 = (f32[2,64,512]{2,1,0:T(8,128)S(1)}, f32[2,64,512]{2,1,0:T(8,128)}, u32[]{:S(2)}) copy-start(f32[2,64,512]{2,1,0:T(8,128)} %param.32) | copy-start | bytes 786436
  2549.3 313.6 %copy-start.25 = (f32[1536]{0:T(1024)S(1)}, f32[1536]{0:T(1024)}, u32[]{:S(2)}) copy-start(f32[1536]{0:T(1024)} %copy-done.24) | copy-start | bytes 18436
  (11 other events, 16.9 us)
Sparse Core Ops, SparseCore 0:
  10.8 47.9 all-gather.7
  61.5 36.7 all-gather.9
  525.5 143.3 reduce-scatter.7
  671.6 50.5 all-gather.13
  724.1 78.8 all-gather.11
  805.6 50.5 all-gather.15
  893.2 144.4 reduce-scatter.9
  1059.2 80.3 all-gather.17
  1193.4 144.4 reduce-scatter.11
  1356.8 80.3 all-gather.19
  1441.3 104.6 reduce-scatter.19
  1550.0 104.4 reduce-scatter.17
  2479.6 171.5 all-reduce.3
  2655.8 61.4 reduce-scatter.15
  2719.5 143.4 reduce-scatter.13
where the time goes:
time: 2890 us; the launch traced here: 2880 us
  matrix products  1200 us (42%)
  waiting for transfers between devices  975 us (34%)
  other arithmetic  494 us (17%)
  local copies, waits for them, and re-layouts  102 us (4%)
  blocking collectives  73.2 us (3%)
    convert_element_type x6, other arithmetic, one_one_block(): score_low = score_grad.astype(jnp.bfloat16)  248 us
    dot_general x6, matrix products, one_one_block(): jnp.einsum('qhd,khd->hqk', grad_block, value_heads, preferred_element_typ...  224 us
    dot_general x6, matrix products, one_one_block(): jnp.einsum('hqk,qhd->khd', prob_low, grad_block, preferred_element_type=j...  152 us
    reduce_scatter x1, waiting for transfers between devices, body(): lax.psum_scatter(times_transposed(row_piece, down_full), 'mp', scatter_di...  145 us
    reduce_scatter x1, waiting for transfers between devices, body(): lax.psum_scatter(times_transposed(row_piece, up_full), 'mp', scatter_dime...  145 us
    reduce_scatter x1, waiting for transfers between devices, body(): lax.psum_scatter(jnp.einsum('cte,cde->td', row_piece, qkv_full, preferred...  143 us
    reduce_scatter x1, waiting for transfers between devices, body(): lax.psum_scatter(times_transposed(row_piece, out_full), 'mp', scatter_dim...  141 us
    reduce_max x6, other arithmetic, attention_one_block(): return (output, log_sum, jnp.max(row_max[..., 0], axis=1))  140 us
  transfers between devices with their start and end apart: 15, of which 11 were waited for; matrix products, arithmetic and copies ran while one was open for 57% of the time, Pallas kernels for 0%

commit v1 on v0

v1 whole, which is shorter than its diff:
```python
import functools

import jax
import jax.numpy as jnp
from jax import lax
from jax.experimental import pallas as pl
from jax.experimental.pallas import tpu as pltpu
from jax.sharding import PartitionSpec as P

HEADS = 16
HEAD_DIM = 64
ADAM_STEP = 5
PAIR = 2 * HEAD_DIM
LOG2E = 1.4426950408889634

very_low = -1e30
clip_tau = 5.0
learn_rate = 0.25
weight_decay = 0.1
moment_beta = 0.5
adam_epsilon = 1e-08


def norm_rows(values, gain_row, shift_row):
    center = values - jnp.mean(values, axis=-1, keepdims=True)
    spread = jnp.mean(center * center, axis=-1, keepdims=True)
    return center * lax.rsqrt(spread + 1e-05) * gain_row + shift_row


def gelu_exact(values):
    return jax.nn.gelu(values, approximate=False)


def times_transposed(left_side, right_side):
    return lax.dot_general(
        left_side, right_side, (((1,), (1,)), ((), ())), preferred_element_type=jnp.float32
    )


def transposed_times(left_side, right_side):
    return lax.dot_general(
        left_side, right_side, (((0,), (0,)), ((), ())), preferred_element_type=jnp.float32
    )


def adam_update(param, moments, grad, step_value):
    first_moment = moment_beta * moments[0] + (1.0 - moment_beta) * grad
    second_moment = moment_beta * moments[1] + (1.0 - moment_beta) * grad * grad
    correct = 1.0 - jnp.power(moment_beta, step_value)
    update = first_moment / correct / (jnp.sqrt(second_moment / correct) + adam_epsilon)
    return (
        param - learn_rate * (update + weight_decay * param),
        jnp.stack([first_moment, second_moment]),
    )


def place_columns(values, column_start, full_width):
    return lax.dynamic_update_slice_in_dim(
        jnp.zeros((full_width,), jnp.float32), values, column_start, 0
    )


bf=jnp.bfloat16
f32=jnp.float32
NN=(((1,),(0,)),((),()))
def dot(a,b): return lax.dot_general(a,b,NN,preferred_element_type=f32)

def fwd_kernel(BQ,CH,T, k_cur,k_nxt,q_cur,q_nxt,sq_cur,sq_nxt,vT, p_ref,o_ref,l_ref,m_ref, sA,sB,mA,mB):
    i=pl.program_id(0)
    zeros=jnp.zeros((64,BQ),bf)
    C1=f32(LOG2E*HEAD_DIM**-0.5)
    def aug(q_ref,sq,h):
        q=q_ref[h*64:(h+1)*64,:]
        parts=[q,zeros] if h==0 else [zeros,q]
        return jnp.concatenate(parts+[sq[...]],axis=0)
    def scores(ks,qa,s_ref,c,mx):
        st=dot(ks[c*CH:(c+1)*CH,:],qa)
        s_ref[c*CH:(c+1)*CH,:]=st
        return jnp.maximum(mx,jnp.max(st.reshape(CH//8,8,BQ),axis=0))
    def finish(mx,m_s):
        m_s[...]=jnp.broadcast_to(jnp.max(mx,axis=0,keepdims=True),(8,BQ))
    neg=jnp.full((8,BQ),-3e38,f32)
    n=T//CH
    @pl.when(i==0)
    def _():
        qa=aug(q_cur,sq_cur,0)
        mx=neg
        for c in range(n): mx=scores(k_cur,qa,sA,c,mx)
        finish(mx,mA)
    def phase(h,s_in,m_in,ks,qa,s_out,m_out):
        m=m_in[...]
        m1=m[0:1]
        mx=neg
        ls=jnp.zeros((8,BQ),f32)
        acc=jnp.zeros((64,BQ),f32)
        for c in range(n):
            mx=scores(ks,qa,s_out,c,mx)
            p=jnp.exp2((s_in[c*CH:(c+1)*CH,:]-m1)*C1)
            ls=ls+jnp.sum(p.reshape(CH//8,8,BQ),axis=0)
            pb=p.astype(bf)
            p_ref[0,h,0,c*CH:(c+1)*CH,:]=pb
            acc=acc+dot(vT[h*64:(h+1)*64,c*CH:(c+1)*CH],pb)
        finish(mx,m_out)
        l=jnp.sum(ls,axis=0,keepdims=True)
        o_ref[h*64:(h+1)*64,:]=acc/l
        l_ref[0,h:h+1,:]=l
        m_ref[0,h:h+1,:]=m1
    phase(0,sA,mA,k_cur,aug(q_cur,sq_cur,1),sB,mB)
    phase(1,sB,mB,k_nxt,aug(q_nxt,sq_nxt,0),sA,mA)

def attention_fwd(kaug,qT,sq,vT,BQ=256,CH=512):
    pairs,T,_=kaug.shape
    nq=T//BQ
    N=pairs*nq
    cur=lambda i:i
    nxt=lambda i:jnp.minimum(i+1,N-1)
    def km(f): return pl.BlockSpec((None,T,256),lambda i:(f(i)//nq,0,0))
    def qm(f): return pl.BlockSpec((128,BQ),lambda i:(f(i)//nq,f(i)%nq))
    def sm(f): return pl.BlockSpec((128,BQ),lambda i:(0,f(i)%nq))
    H=2*pairs
    return pl.pallas_call(
        functools.partial(fwd_kernel,BQ,CH,T),
        grid=(N,),
        in_specs=[km(cur),km(nxt),qm(cur),qm(nxt),sm(cur),sm(nxt),pl.BlockSpec((128,T),lambda i:(i//nq,0))],
        out_specs=[pl.BlockSpec((1,2,1,T,BQ),lambda i:(i//nq,0,i%nq,0,0)),
                   pl.BlockSpec((128,BQ),lambda i:(i//nq,i%nq)),
                   pl.BlockSpec((1,2,BQ),lambda i:(i//nq,0,i%nq)),
                   pl.BlockSpec((1,2,BQ),lambda i:(i//nq,0,i%nq))],
        out_shape=[jax.ShapeDtypeStruct((pairs,2,nq,T,BQ),bf),
                   jax.ShapeDtypeStruct((pairs*128,T),f32),
                   jax.ShapeDtypeStruct((pairs,2,T),f32),
                   jax.ShapeDtypeStruct((pairs,2,T),f32)],
        scratch_shapes=[pltpu.VMEM((T,BQ),f32),pltpu.VMEM((T,BQ),f32),pltpu.VMEM((8,BQ),f32),pltpu.VMEM((8,BQ),f32)],
        compiler_params=pltpu.CompilerParams(vmem_limit_bytes=58*2**20,dimension_semantics=("arbitrary",)),
        cost_estimate=pl.CostEstimate(flops=4*H*T*T*64*4,bytes_accessed=2*H*T*T,transcendentals=H*T*T),
    )(kaug,kaug,qT,qT,sq,sq,vT)

def bwd_kernel(BQ,CH,T, p_ref,doT,do,q,v,kT,dl, dq_ref,dk_ref,dv_ref):
    j=pl.program_id(0)
    @pl.when(j==0)
    def _():
        dk_ref[...]=jnp.zeros_like(dk_ref)
        dv_ref[...]=jnp.zeros_like(dv_ref)
    zeros=jnp.zeros((64,BQ),bf)
    zl=jnp.zeros((BQ,64),bf)
    def diag(x):
        x=x[...]
        lane=lax.broadcasted_iota(jnp.int32,(BQ,128),1)
        zz=jnp.zeros_like(x)
        return jnp.concatenate([jnp.where(lane<64,x,zz),jnp.where(lane>=64,x,zz)],axis=0)
    dod=diag(do); qd=diag(q)
    doTs=[jnp.concatenate([doT[0:64,:],zeros],0),jnp.concatenate([zeros,doT[64:128,:]],0)]
    dls=[dl[0,0:1,:],dl[0,1:2,:]]
    dqs=[jnp.zeros((64,BQ),f32) for _ in range(2)]
    for c in range(T//CH):
        sl=slice(c*CH,(c+1)*CH)
        vc=v[sl,:]
        ps=[];dss=[]
        for h in range(2):
            dp=dot(vc,doTs[h])
            p=p_ref[0,h,0,sl,:]
            ds=(p.astype(f32)*(dp-dls[h])).astype(bf)
            ps.append(p);dss.append(ds)
            dqs[h]=dqs[h]+dot(kT[h*64:(h+1)*64,sl],ds)
        dv_ref[sl,:]+=dot(jnp.concatenate(ps,1),dod)
        dk_ref[sl,:]+=dot(jnp.concatenate(dss,1),qd)
    for h in range(2):
        dq_ref[h*64:(h+1)*64,:]=dqs[h]*f32(HEAD_DIM**-0.5)
    @pl.when(j==pl.num_programs(0)-1)
    def _():
        dk_ref[...]=dk_ref[...]*f32(HEAD_DIM**-0.5)

def attention_bwd(p,doT,do,q,v,kT,dl,at,CH=1536):
    _,_,nq,T,BQ=p.shape
    CH=min(CH,T)
    return pl.pallas_call(
        functools.partial(bwd_kernel,BQ,CH,T),
        grid=(nq,),
        in_specs=[pl.BlockSpec((1,2,1,T,BQ),lambda j:(at,0,j,0,0)),
                  pl.BlockSpec((128,BQ),lambda j:(0,j)),
                  pl.BlockSpec((BQ,128),lambda j:(j,0)),
                  pl.BlockSpec((BQ,128),lambda j:(j,0)),
                  pl.BlockSpec((T,128),lambda j:(0,0)),
                  pl.BlockSpec((128,T),lambda j:(0,0)),
                  pl.BlockSpec((1,2,BQ),lambda j:(0,0,j))],
        out_specs=[pl.BlockSpec((128,BQ),lambda j:(0,j)),
                   pl.BlockSpec((T,128),lambda j:(0,0)),
                   pl.BlockSpec((T,128),lambda j:(0,0))],
        out_shape=[jax.ShapeDtypeStruct((128,T),f32),
                   jax.ShapeDtypeStruct((T,128),f32),
                   jax.ShapeDtypeStruct((T,128),f32)],
        compiler_params=pltpu.CompilerParams(vmem_limit_bytes=58*2**20,dimension_semantics=("arbitrary",)),
        cost_estimate=pl.CostEstimate(flops=8*2*T*T*64*4,bytes_accessed=2*2*T*T,transcendentals=0),
    )(p,doT,do,q,v,kT,dl)


def bits_of(size):
    return size.bit_length() - 1


def swap(value, axis_name, mask):
    size = lax.axis_size(axis_name)
    return lax.ppermute(value, axis_name, [(i, i ^ mask) for i in range(size)])


def pick(value, index, axis):
    return lax.dynamic_index_in_dim(value, index, axis, keepdims=False)


def halve(value, axis_name, bit, axis):
    mine = (lax.axis_index(axis_name) >> bit) & 1
    got = swap(pick(value, 1 - mine, axis).astype(jnp.bfloat16), axis_name, 1 << bit)
    return pick(value, mine, axis) + got.astype(jnp.float32)


def core_first(rows_t, right, add_axis=None):
    dp = lax.axis_size("dp")
    core = lax.axis_index("dp") & 1
    tokens = rows_t.shape[1]
    split = rows_t.reshape(dp // 2, 2, -1, tokens)
    other = pick(split, 1 - core, 1).reshape(-1, tokens)
    own = pick(split, core, 1).reshape(-1, tokens)
    sent = jnp.dot(other, right, preferred_element_type=jnp.float32).astype(jnp.bfloat16)
    got = swap(sent, "dp", 1)
    return jnp.dot(own, right, preferred_element_type=jnp.float32) + got.astype(jnp.float32)


def rest_of_dp(value):
    steps = bits_of(lax.axis_size("dp")) - 1
    width = value.shape[1]
    value = value.reshape((2,) * steps + (-1, width))
    for step in range(steps):
        value = halve(value, "dp", step + 1, steps - 1 - step)
    return value


def over_mp(value):
    steps = bits_of(lax.axis_size("mp"))
    rows, _, width = value.shape
    value = value.reshape((rows,) + (2,) * steps + (width,))
    for step in range(steps):
        value = halve(value, "mp", step, steps - step)
    return value


def over_mp_relative(blocks):
    blocks = list(blocks)
    for step in reversed(range(bits_of(len(blocks)))):
        size = 1 << step
        blocks = [
            blocks[j] + swap(blocks[j + size].astype(jnp.bfloat16), "mp", size).astype(jnp.float32)
            for j in range(size)
        ]
    return blocks[0]


def all_sum(value):
    for name in ("dp", "mp"):
        for step in range(bits_of(lax.axis_size(name))):
            value = value + swap(value, name, 1 << step)
    return value


def body(
    layer_input,
    out_cotangent,
    segment_ids,
    qkv_weight,
    out_weight,
    up_weight,
    down_weight,
    norm_gains,
    bias_rows,
    up_bias,
    qkv_moments,
    out_moments,
    up_moments,
    down_moments,
    gain_moments,
    bias_moments,
    up_bias_moments,
):
    mp = lax.axis_size("mp")
    me = lax.axis_index("mp")
    dp = lax.axis_size("dp")
    dp_me = lax.axis_index("dp")
    width = qkv_weight.shape[2]
    units = up_weight.shape[1]
    tokens, dim = layer_input.shape
    rows = tokens // mp
    pairs = width // PAIR
    heads_local = width // HEAD_DIM
    low = jnp.bfloat16
    block = min(512, tokens)
    column_start = me * width

    def relative(value, axis):
        shape = value.shape
        value = value.reshape(shape[:axis] + (mp, rows) + shape[axis + 1 :])
        parts = [pick(value, me ^ j, axis) for j in range(mp)]
        return jnp.concatenate(parts, axis=axis)

    qkv_low = qkv_weight.astype(low)
    qkv_full = lax.all_gather(qkv_low, "dp", axis=1, tiled=True)
    first_set = jnp.concatenate([out_weight.astype(low), up_weight.astype(low)], axis=1)
    second_set = jnp.concatenate(
        [down_weight.astype(low), qkv_low.transpose(1, 0, 2).reshape(-1, 3 * width)], axis=1
    )
    inputs = relative(layer_input, 0)
    inputs_t = inputs.T
    ids = relative(segment_ids.reshape(-1), 0)

    projected = jnp.einsum("td,cde->cte", inputs, qkv_full, preferred_element_type=jnp.float32)
    query_bias = lax.dynamic_slice_in_dim(bias_rows[0], column_start, width)
    value_bias = lax.dynamic_slice_in_dim(bias_rows[1], column_start, width)
    queries = (projected[0] + query_bias).astype(low)
    keys_all = projected[1].astype(low)
    values_all = (projected[2] + value_bias).astype(low)
    queries_t = queries.T
    keys_t = keys_all.T
    values_t = values_all.T
    first_all = lax.all_gather(first_set, ("mp", "dp"), axis=0, tiled=True).reshape(mp, dim, -1)
    second_all = lax.all_gather(second_set, ("mp", "dp"), axis=0, tiled=True).reshape(mp, dim, -1)
    document = jnp.arange(PAIR, dtype=jnp.int32)
    same = ids[:, None] == document[None, :]
    key_marks = jnp.where(same | (document[None, :] > 2), 0.0, very_low).astype(low)
    query_marks = same.T.astype(low)
    key_rows = jnp.concatenate(
        [
            keys_all.reshape(tokens, pairs, PAIR).transpose(1, 0, 2),
            jnp.broadcast_to(key_marks[None], (pairs, tokens, PAIR)),
        ],
        axis=-1,
    )

    calls = 2 if pairs % 2 == 0 else 1
    per_call = pairs // calls
    probs, attended_t, totals, attended_rel = [], [], [], [[] for _ in range(mp)]
    tops = []
    for call in range(calls):
        span = slice(call * per_call * PAIR, (call + 1) * per_call * PAIR)
        call_probs, call_out, call_total, call_max = attention_fwd(
            key_rows[call * per_call : (call + 1) * per_call],
            queries_t[span],
            query_marks,
            values_t[span],
            BQ=block,
        )
        probs.append(call_probs)
        attended_t.append(call_out)
        totals.append(call_total)
        tops.append(jnp.max(call_max, axis=2).reshape(-1))
        call_low = call_out.astype(low)
        for j in range(mp):
            piece = call_low[:, j * rows : (j + 1) * rows]
            attended_rel[j].append(piece if j == 0 else swap(piece, "mp", j))
    head_max = jnp.concatenate(tops) * HEAD_DIM ** (-0.5)
    attended_rel = [jnp.concatenate(parts, axis=0) for parts in attended_rel]

    out_full, up_full = first_all[:, :, :width], first_all[:, :, width:]
    down_full, qkv_other = second_all[:, :, :units], second_all[:, :, units:]
    out_rel = [pick(out_full, me ^ j, 0) for j in range(mp)]
    branch = 0.0
    for j in range(mp):
        branch = branch + lax.dot_general(
            attended_rel[j],
            out_rel[j],
            (((0,), (1,)), ((), ())),
            preferred_element_type=jnp.float32,
        )
    summed = inputs[:rows].astype(jnp.float32) + branch + bias_rows[2]
    normed, first_norm_pull = jax.vjp(norm_rows, summed, norm_gains[0], bias_rows[4])
    normed_low = normed.astype(low)
    pre_act = jnp.concatenate(
        [jnp.dot(normed_low, up_full[m], preferred_element_type=jnp.float32) for m in range(mp)],
        axis=1,
    )
    pre_act = pre_act + up_bias
    hidden, gelu_pull = jax.vjp(gelu_exact, pre_act)
    hidden_low = hidden.astype(low)
    ffn_out = 0.0
    for m in range(mp):
        ffn_out = ffn_out + times_transposed(
            hidden_low[:, m * units : (m + 1) * units], down_full[m]
        )
    total = normed + ffn_out + bias_rows[3]
    result, second_norm_pull = jax.vjp(norm_rows, total, norm_gains[1], bias_rows[5])
    total_grad, second_gain_grad, second_shift_grad = second_norm_pull(
        out_cotangent.astype(jnp.float32)
    )
    total_low = total_grad.astype(low)
    down_part = core_first(total_low.T, hidden_low)
    hidden_grad = jnp.concatenate(
        [jnp.dot(total_low, down_full[m], preferred_element_type=jnp.float32) for m in range(mp)],
        axis=1,
    )
    pre_grad = gelu_pull(hidden_grad)[0]
    up_bias_grad = jnp.sum(pre_grad, axis=0)
    pre_low = pre_grad.astype(low)
    up_part = core_first(normed_low.T, pre_low)
    normed_grad = total_grad
    for m in range(mp):
        normed_grad = normed_grad + times_transposed(
            pre_low[:, m * units : (m + 1) * units], up_full[m]
        )
    summed_grad, first_gain_grad, first_shift_grad = first_norm_pull(normed_grad)
    summed_low = summed_grad.astype(low)
    grad_rel = []
    for j in range(mp):
        piece = jnp.dot(summed_low, out_rel[j], preferred_element_type=jnp.float32).astype(low)
        grad_rel.append(piece if j == 0 else swap(piece, "mp", j))
    attended_grad = jnp.concatenate(grad_rel, axis=0)
    out_part = core_first(summed_low.T, jnp.concatenate(attended_rel, axis=0).T)

    down_sum = over_mp(rest_of_dp(down_part).reshape(-1, mp, units))
    up_sum = over_mp(rest_of_dp(up_part).reshape(-1, mp, units))
    out_sum = rest_of_dp(out_part)
    out_sum = over_mp_relative([out_sum[:, j * width : (j + 1) * width] for j in range(mp)])

    slots = lax.dynamic_update_slice_in_dim(
        jnp.zeros((dp * mp, heads_local), jnp.float32),
        head_max[None],
        dp_me * mp + me,
        0,
    )
    early = all_sum(
        jnp.concatenate(
            [
                first_gain_grad,
                second_gain_grad,
                jnp.sum(summed_grad, axis=0),
                jnp.sum(total_grad, axis=0),
                first_shift_grad,
                second_shift_grad,
                up_bias_grad,
                slots.reshape(-1),
            ]
        )
    )
    gain_sum = early[: 2 * dim].reshape(2, dim)
    late_biases = early[2 * dim : 6 * dim].reshape(4, dim)
    unit_sum = early[6 * dim : 6 * dim + units * mp]
    group_max = jnp.max(early[6 * dim + units * mp :].reshape(dp, mp, heads_local), axis=0)
    local_max = pick(group_max, me, 0)

    inverse = 1.0 / jnp.concatenate(totals, axis=0).reshape(heads_local, tokens)
    grad_t = attended_grad.T
    scaled = (
        attended_grad.astype(jnp.float32).reshape(tokens, heads_local, HEAD_DIM)
        * inverse.T[:, :, None]
    )
    scaled = scaled.reshape(tokens, width).astype(low)
    scaled_t = scaled.T
    delta = jnp.sum(
        (grad_t.astype(jnp.float32) * jnp.concatenate(attended_t, axis=0)).reshape(
            heads_local, HEAD_DIM, tokens
        ),
        axis=1,
    )
    delta = (delta * inverse).reshape(pairs, 2, tokens)
    own_rows, got_rows = [], [[] for _ in range(mp - 1)]
    qkv_pieces, bias_pieces = [], []
    for pair in range(pairs):
        span = slice(pair * PAIR, (pair + 1) * PAIR)
        call, at = pair // per_call, pair % per_call
        query_grad, key_grad, value_grad = attention_bwd(
            probs[call],
            scaled_t[span],
            scaled[:, span],
            queries[:, span],
            values_all[:, span],
            keys_t[span],
            delta[pair : pair + 1],
            at,
        )
        bias_pieces.append(jnp.stack([jnp.sum(query_grad, axis=1), jnp.sum(value_grad, axis=0)]))
        grads_low = jnp.concatenate(
            [query_grad.T.astype(low), key_grad.astype(low), value_grad.astype(low)], axis=1
        )
        own_rows.append(grads_low[:rows])
        for j in range(1, mp):
            got_rows[j - 1].append(swap(grads_low[j * rows : (j + 1) * rows], "mp", j))
        qkv_pieces.append(core_first(inputs_t, grads_low))
    qkv_sums = [rest_of_dp(piece) for piece in qkv_pieces]

    def by_pair(weights):
        weights = weights.reshape(dim, 3, pairs, PAIR).transpose(0, 2, 1, 3)
        return weights.reshape(dim, 3 * width)

    input_grad = summed_grad + times_transposed(
        jnp.concatenate(own_rows, axis=1), by_pair(qkv_full.transpose(1, 0, 2))
    )
    for j in range(1, mp):
        input_grad = input_grad + times_transposed(
            jnp.concatenate(got_rows[j - 1], axis=1), by_pair(pick(qkv_other, me ^ j, 0))
        )
    qkv_sum = jnp.concatenate(
        [piece.reshape(-1, 3, 1, PAIR) for piece in qkv_sums], axis=2
    ).reshape(-1, 3, width)
    qkv_sum = qkv_sum.transpose(1, 0, 2)
    head_biases = jnp.concatenate(bias_pieces, axis=1)
    head_biases = lax.dynamic_update_slice_in_dim(
        jnp.zeros((2, width * mp), jnp.float32), head_biases, column_start, 1
    )
    bias_sum = jnp.concatenate([all_sum(head_biases), late_biases], axis=0)

    grad_scale = lax.rsqrt(jnp.float32(tokens * dp))
    step_value = jnp.float32(ADAM_STEP)
    new_qkv, next_qkv = adam_update(qkv_weight, qkv_moments, qkv_sum * grad_scale, step_value)
    new_out, next_out = adam_update(out_weight, out_moments, out_sum * grad_scale, step_value)
    new_up, next_up = adam_update(up_weight, up_moments, up_sum * grad_scale, step_value)
    new_down, next_down = adam_update(down_weight, down_moments, down_sum * grad_scale, step_value)
    new_gains, next_gains = adam_update(norm_gains, gain_moments, gain_sum * grad_scale, step_value)
    new_biases, next_biases = adam_update(
        bias_rows, bias_moments, bias_sum * grad_scale, step_value
    )
    new_up_bias, next_up_bias = adam_update(
        up_bias, up_bias_moments, unit_sum * grad_scale, step_value
    )
    factor = jnp.sqrt(clip_tau / jnp.maximum(local_max, clip_tau))
    column = jnp.repeat(factor, HEAD_DIM)
    scales = jnp.stack([column, column, jnp.ones_like(column)])[:, None, :]
    new_qkv = new_qkv * scales
    return (
        result.astype(jnp.bfloat16),
        input_grad,
        new_qkv,
        new_out,
        new_up,
        new_down,
        new_gains,
        new_biases,
        new_up_bias,
        next_qkv,
        next_out,
        next_up,
        next_down,
        next_gains,
        next_biases,
        next_up_bias,
    )


def solution(mesh):
    placed = (
        P("dp", None),
        P(("dp", "mp"), None),
        P("dp", None),
        P(None, "dp", "mp"),
        P("dp", "mp"),
        P("dp", "mp"),
        P("dp", "mp"),
        P(),
        P(),
        P(),
        P(None, None, "dp", "mp"),
        P(None, "dp", "mp"),
        P(None, "dp", "mp"),
        P(None, "dp", "mp"),
        P(),
        P(),
        P(),
    )
    return jax.shard_map(
        body,
        mesh=mesh,
        in_specs=placed,
        out_specs=(
            P(("dp", "mp"), None),
            P(("dp", "mp"), None),
            P(None, "dp", "mp"),
            P("dp", "mp"),
            P("dp", "mp"),
            P("dp", "mp"),
            P(),
            P(),
            P(),
            P(None, None, "dp", "mp"),
            P(None, "dp", "mp"),
            P(None, "dp", "mp"),
            P(None, "dp", "mp"),
            P(),
            P(),
            P(),
        ),
        check_vma=False,
    )
```

time: 2890 us -> 1200 us (0.42)
  matrix products: 1200 us -> 216 us
  waiting for transfers between devices: 975 us -> 225 us
  other arithmetic: 494 us -> 189 us
  Pallas kernels: 0 us -> 295 us
  local copies, waits for them, and re-layouts: 102 us -> 206 us
  blocking collectives: 73.2 us -> 0 us
  starting transfers between devices: 0.63 us -> 37.4 us
    dot_general x51 -> x23, matrix products: 1150 us -> 148 us  [the longest x7 35.9 us: core_first(): jnp.dot(other, right, preferred_element_type=jnp.float32)]
    reduce_scatter x7 -> x0, waiting for transfers between devices: 635 us -> none  [the longest x1 145 us: body(): lax.psum_scatter(times_transposed(row_piece, down_full), 'mp', scatter_di...]
    pallas_call x0 -> x6, Pallas kernels: none -> 295 us  [the longest x4 173 us: attention_bwd(): pl.pallas_call(functools.partial(bwd_kernel, BQ, CH, T), grid=(nq,), in_s...]
    all_gather x7 -> x3, waiting for transfers between devices: 281 us -> 12.9 us  [the longest x1 12.9 us: body(): qkv_full = lax.all_gather(qkv_low, 'dp', axis=1, tiled=True)]
    ppermute x0 -> x48, waiting for transfers between devices: none -> 212 us  [swap(): return lax.ppermute(value, axis_name, [(i, i ^ mask) for i in range(size)])]
    convert_element_type x14 -> x15, other arithmetic: 265 us -> 85.4 us  [the longest x1 56.8 us: body(): hidden_low = hidden.astype(low)]
    reduce_max x7 -> x3, other arithmetic: 140 us -> 0.26 us  [the longest x2 0.23 us: body(): tops.append(jnp.max(call_max, axis=2).reshape(-1))]
    unnamed x16 -> x3, waiting for transfers between devices: 58.8 us -> 0.05 us
  transfers between devices with their start and end apart: 15 -> 51, of which waited for: 11 -> 29; matrix products, arithmetic and copies ran while one was open for 57% -> 38% of each run, Pallas kernels for 0% -> 25%
where the time goes in v1:
time: 1200 us; the launch traced here: 1180 us
  Pallas kernels  295 us (25%)
  waiting for transfers between devices  225 us (19%)
  matrix products  216 us (18%)
  local copies, waits for them, and re-layouts  206 us (17%)
  other arithmetic  189 us (16%)
  starting transfers between devices  37.4 us (3%)
  between operations  16.1 us (1%)
    ppermute x48, waiting for transfers between devices, swap(): return lax.ppermute(value, axis_name, [(i, i ^ mask) for i in range(size)])  212 us
    pallas_call x4, Pallas kernels, attention_bwd(): pl.pallas_call(functools.partial(bwd_kernel, BQ, CH, T), grid=(nq,), in_s...  173 us
    pallas_call x2, Pallas kernels, attention_fwd(): pl.pallas_call(functools.partial(fwd_kernel, BQ, CH, T), grid=(N,), in_sp...  122 us
    dot_general x6, matrix products, times_transposed(): lax.dot_general(left_side, right_side, (((1,), (1,)), ((), ())), preferre...  68.1 us
    convert_element_type x1, other arithmetic, body(): hidden_low = hidden.astype(low)  56.8 us
    ppermute x48, starting transfers between devices, swap(): return lax.ppermute(value, axis_name, [(i, i ^ mask) for i in range(size)])  37.2 us
    dot_general x7, matrix products, core_first(): jnp.dot(other, right, preferred_element_type=jnp.float32)  35.9 us
    dot_general x7, matrix products, core_first(): jnp.dot(own, right, preferred_element_type=jnp.float32)  35 us
  transfers between devices with their start and end apart: 51, of which 29 were waited for; matrix products, arithmetic and copies ran while one was open for 38% of the time, Pallas kernels for 25%

profile of v1, /device:TPU:0, one launch (start us, length us, event | category | flops | bytes accessed | tf_op | source)
XLA Modules:
  0.0 1183.9 jit_solution(998364567725290514)
XLA Ops:
  30.5 8.7 copy.260
  39.8 6.1 constant_dynamic-slice_fusion.26
  45.9 12.9 %all-gather.4.cloned.1.call-done = bf16[3,1024,512]{2,1,0:T(8,128)(2,1)} async-done(((bf16[3,64,512]{2,1,0:T(8,128)(2,1)}), bf16[3,1024,512]{2,1,0:T(8,128)(2,1)}) %all-gather.4.cloned.1.call-update) | async-done | bytes 3145744 | tf_op jit(solution)/shard_map/all_gather | solution.py:304
  58.8 16.2 %convolution_bitcast_fusion = f32[3,3072,512]{1,2,0:T(8,128)} fusion(bf16[3,1024,512]{2,1,0:T(8,128)(2,1)} %all-gather.4.cloned.1.call-done, bf16[1536,1024]{1,0:T(8,128)(2,1)} %copy-done.10, bf16[1536,1024]{1,0:T(8,128)(2,1)S(1)} %get-tuple-element.150), kind=kOutput, calls=%fused_computation.26 | convolution fusion | flops 9676259328 | bytes 28311552 | tf_op jit(solution)/shard_map/td,cde->cte/dot_general | solution.py:313
  78.3 4.9 slice.550
  83.2 4.6 copy.229
  87.9 5.7 fusion.21
  105.4 61.0 %shard_map.288 = (bf16[2,2,6,3072,512]{4,3,2,1,0:T(8,128)(2,1)}, f32[256,3072]{1,0:T(8,128)}, f32[2,2,3072]{2,1,0:T(2,128)}, f32[2,2,3072]{2,1,0:T(2,128)}) custom-call(bf16[2,3072,256]{2,1,0:T(8,128)(2,1)} %get-tuple-element.148.k_cur.k_nxt, bf16[2,3072,256]{2,1,0:T(8,128)(2,1)} %get-tuple-element.148.k_cur.k_nxt, ...), custom_call_target="tpu_custom_call" | custom-call | flops 38654705664 | bytes 75497472 | tf_op jit(solution)/shard_map/pallas_call | solution.py:121
  173.2 60.9 %shard_map.289 = (bf16[2,2,6,3072,512]{4,3,2,1,0:T(8,128)(2,1)}, f32[256,3072]{1,0:T(8,128)}, f32[2,2,3072]{2,1,0:T(2,128)}, f32[2,2,3072]{2,1,0:T(2,128)}) custom-call(bf16[2,3072,256]{2,1,0:T(8,128)(2,1)} %get-tuple-element.149.k_cur.k_nxt, bf16[2,3072,256]{2,1,0:T(8,128)(2,1)} %get-tuple-element.149.k_cur.k_nxt, ...), custom_call_target="tpu_custom_call" | custom-call | flops 38654705664 | bytes 75497472 | tf_op jit(solution)/shard_map/pallas_call | solution.py:121
  241.0 5.6 reshape.501
  246.6 15.2 %copy.257 = bf16[1024,3,4,128]{0,3,1,2:T(8,128)(2,1)} copy(bf16[1024,3,4,128]{3,2,0,1:T(4,128)(2,1)} %reshape.501) | data formatting | bytes 6291456 | tf_op jit(solution)/shard_map/reshape | solution.py:487
  292.3 6.5 copy.237
  302.3 4.0 fusion.56
  306.4 13.6 %collective-permute-done.1 = bf16[256,1536]{1,0:T(8,128)(2,1)} collective-permute-done((bf16[256,1536]{1,0:T(8,128)(2,1)}, bf16[256,1536]{1,0:T(8,128)(2,1)}, u32[]{:S(2)}, u32[]{:S(2)}) %collective-permute-start.1) | collective-permute-done | bytes 786464 | tf_op jit(solution)/shard_map/ppermute | solution.py:203
  320.0 4.1 fusion.171
  336.4 8.8 fusion.50
  345.2 15.1 %fusion.49 = f32[1536,2048]{1,0:T(8,128)} fusion(bf16[2,1024,2560]{2,1,0:T(8,128)(2,1)} %bitcast.539, f32[1536,1024]{1,0:T(8,128)S(1)} %copy-done.1, f32[1024]{0:T(1024)S(1)} %bitcast.560, f32[1024]{0:T(1024)S(1)} %bitcast.553, f32[1536]{0:T(1024)S(1)} %fusion.120, f32[1536]{0:T(1024)S(1)} %broadcast_multiply_fusion.1), kind=kOutput, calls=%fused_computation.97 | convolution fusion | flops 6450315264 | bytes 23089152 | tf_op jit(solution)/shard_map/dot_general | solution.py:375
  360.3 56.8 %multiply_convert_fusion = (bf16[1536,4096]{1,0:T(8,128)(2,1)}, f32[1536,4096]{1,0:T(8,128)}) fusion(f32[1536,2048]{1,0:T(8,128)S(1)} %fusion.50, f32[1536,2048]{1,0:T(8,128)} %fusion.49, f32[4096]{0:T(1024)S(1)} %copy-done.59), kind=kLoop, calls=%fused_computation.5 | loop fusion | flops 421527552 | bytes 62930944 | tf_op jit(solution)/shard_map/convert_element_type | solution.py:380
  417.2 10.1 fusion.16
  427.3 11.9 %fusion.172 = (f32[1536]{0:T(1024)S(1)}, f32[1536,1024]{1,0:T(8,128)S(1)}) fusion(f32[1024]{0:T(1024)S(1)} %bitcast.580, f32[1536,1024]{1,0:T(8,128)S(1)} %fusion.16, bf16[2,1024,3584]{2,1,0:T(8,128)(2,1)} %bitcast.515, bf16[1536,4096]{1,0:T(8,128)(2,1)} %get-tuple-element.137, f32[1024]{0:T(1024)S(1)} %bitcast.561, f32[1024]{0:T(1024)S(1)} %bitcast.554, ...), kind=kOutput, calls=%fused_computation.397 | convolution fusion | flops 6455032320 | bytes 29390848 | tf_op jit(solution)/shard_map/dot_general | solution.py:35
  444.5 4.3 fusion.149
  451.4 11.2 fusion.52
  462.6 11.1 fusion.51
  480.2 12.9 %convolution_convert_fusion = bf16[512,4096]{1,0:T(8,128)(2,1)} fusion(bf16[512,1536]{1,0:T(8,128)(2,1)S(1)} %bitcast.524, bf16[1536,4096]{1,0:T(8,128)(2,1)} %get-tuple-element.137), kind=kOutput, calls=%fused_computation.65 | convolution fusion | flops 6444548096 | bytes 18350080 | tf_op jit(solution)/shard_map/dot_general | solution.py:223
  493.1 30.2 %fusion.147 = (f32[4096]{0:T(1024)S(1)}, bf16[1536,4096]{1,0:T(8,128)(2,1)}) fusion(f32[1536,4096]{1,0:T(8,128)} %get-tuple-element.138, f32[1536,2048]{1,0:T(8,128)} %fusion.52, f32[1536,2048]{1,0:T(8,128)} %fusion.51, f32[4096]{0:T(1024)S(1)} %copy-done.59, f32[1536,2048]{1,0:T(8,128)} %copy-done.2, f32[1536,2048]{1,0:T(8,128)} %fusion.49), kind=kLoop, calls=%fused_computation.373 | loop fusion | flops 113242112 | bytes 88113152 | tf_op jit(solution)/shard_map/reduce_sum | solution.py:398
  523.3 11.7 fusion.12
  535.0 16.3 %multiply_reduce_fusion = (f32[1024]{0:T(1024)S(1)}, f32[1536]{0:T(1024)S(1)}, f32[1024]{0:T(1024)S(1)}, f32[1536,1024]{1,0:T(8,128)}) fusion(f32[1536,1024]{1,0:T(8,128)S(1)} %bitcast.464, f32[1536]{0:T(1024)S(1)} %fusion.120, f32[1536]{0:T(1024)S(1)} %broadcast_multiply_fusion.1, f32[1024]{0:T(1024)S(1)} %bitcast.555, f32[1536,1024]{1,0:T(8,128)} %fusion.12, ...), kind=kOutput, calls=%fused_computation.55 | convolution fusion | flops 6459748864 | bytes 35688448 | tf_op jit(solution)/shard_map/dot_general | solution.py:35
  551.3 4.6 fusion.148
  574.6 8.3 convolution_convert_fusion.1
  584.4 4.7 copy.275
  597.1 4.0 copy.259
  601.9 4.3 convolution_convert_fusion.4
  606.2 14.7 %collective-permute-done.27 = f32[10496]{0:T(1024)S(1)} collective-permute-done((f32[10496]{0:T(1024)S(1)}, f32[10496]{0:T(1024)S(1)}, u32[]{:S(2)}, u32[]{:S(2)}) %collective-permute-start.27) | collective-permute-done | bytes 42016 | tf_op jit(solution)/shard_map/ppermute | solution.py:203
  626.7 4.1 convert_add_fusion.2
  634.0 5.4 fusion.10
  639.4 6.6 copy.240
  650.2 4.3 fusion.9
  661.7 43.3 %shard_map.291 = (f32[128,3072]{1,0:T(8,128)}, f32[3072,128]{1,0:T(8,128)}, f32[3072,128]{1,0:T(8,128)}) custom-call(bf16[2,2,6,3072,512]{4,3,2,1,0:T(8,128)(2,1)} %get-tuple-element.38.p_ref, bf16[128,3072]{1,0:T(8,128)(2,1)} %copy.245.doT, bf16[3072,128]{1,0:T(8,128)(2,1)} %get-tuple-element.173.do, bf16[3072,128]{1,0:T(8,128)(2,1)} %copy.246.q, ...), custom_call_target="tpu_custom_call" | custom-call | flops 38654705664 | bytes 37748736 | tf_op jit(solution)/shard_map/pallas_call | solution.py:176
  714.7 43.1 %shard_map.293 = (f32[128,3072]{1,0:T(8,128)}, f32[3072,128]{1,0:T(8,128)}, f32[3072,128]{1,0:T(8,128)}) custom-call(bf16[2,2,6,3072,512]{4,3,2,1,0:T(8,128)(2,1)} %get-tuple-element.47.p_ref, bf16[128,3072]{1,0:T(8,128)(2,1)} %copy.253.doT, bf16[3072,128]{1,0:T(8,128)(2,1)} %get-tuple-element.171.do, bf16[3072,128]{1,0:T(8,128)(2,1)} %copy.254.q, ...), custom_call_target="tpu_custom_call" | custom-call | flops 38654705664 | bytes 37748736 | tf_op jit(solution)/shard_map/pallas_call | solution.py:176
  765.1 43.2 %shard_map.290 = (f32[128,3072]{1,0:T(8,128)}, f32[3072,128]{1,0:T(8,128)}, f32[3072,128]{1,0:T(8,128)}) custom-call(bf16[2,2,6,3072,512]{4,3,2,1,0:T(8,128)(2,1)} %get-tuple-element.38.p_ref, bf16[128,3072]{1,0:T(8,128)(2,1)} %copy.241.doT, bf16[3072,128]{1,0:T(8,128)(2,1)} %get-tuple-element.170.do, bf16[3072,128]{1,0:T(8,128)(2,1)} %copy.242.q, ...), custom_call_target="tpu_custom_call" | custom-call | flops 38654705664 | bytes 37748736 | tf_op jit(solution)/shard_map/pallas_call | solution.py:176
  808.3 43.4 %shard_map.292 = (f32[128,3072]{1,0:T(8,128)}, f32[3072,128]{1,0:T(8,128)}, f32[3072,128]{1,0:T(8,128)}) custom-call(bf16[2,2,6,3072,512]{4,3,2,1,0:T(8,128)(2,1)} %get-tuple-element.47.p_ref, bf16[128,3072]{1,0:T(8,128)(2,1)} %copy.249.doT, bf16[3072,128]{1,0:T(8,128)(2,1)} %get-tuple-element.172.do, bf16[3072,128]{1,0:T(8,128)(2,1)} %copy.250.q, ...), custom_call_target="tpu_custom_call" | custom-call | flops 38654705664 | bytes 37748736 | tf_op jit(solution)/shard_map/pallas_call | solution.py:176
  864.9 4.2 convolution_convert_fusion.5
  883.8 7.0 fusion.26
  909.7 6.2 collective-permute-done.31
  920.8 35.1 %collective-permute-done.32 = bf16[64,512]{1,0:T(8,128)(2,1)S(1)} collective-permute-done((bf16[64,512]{1,0:T(8,128)(2,1)S(1)}, bf16[64,512]{1,0:T(8,128)(2,1)S(1)}, u32[]{:S(2)}, u32[]{:S(2)}) %collective-permute-start.32) | collective-permute-done | bytes 65568 | tf_op jit(solution)/shard_map/ppermute | solution.py:203
  963.5 4.5 collective-permute-done.12
  969.1 5.6 collective-permute-done.20
  975.9 4.5 collective-permute-done.16
  980.6 4.4 collective-permute-done.9
  985.2 5.2 collective-permute-done.13
  990.6 4.9 collective-permute-done.21
  995.6 4.6 collective-permute-done.17
  1000.6 4.5 collective-permute-done.10
  1005.6 4.5 collective-permute-done.14
  1010.6 4.5 collective-permute-done.22
  1015.7 4.3 collective-permute-done.18
  1024.4 12.9 %convert_add_fusion = f32[512,4096]{1,0:T(8,128)} fusion(bf16[512,4096]{1,0:T(8,128)(2,1)} %collective-permute-done.38, bf16[512,1536]{1,0:T(8,128)(2,1)} %bitcast.520, bf16[1536,4096]{1,0:T(8,128)(2,1)} %get-tuple-element.137), kind=kOutput, calls=%fused_computation.24 | convolution fusion | flops 6446645248 | bytes 26738688 | tf_op jit(solution)/shard_map/dot_general | solution.py:225
  1037.3 3.9 fusion.55
  1043.2 10.7 convert_add_fusion.1
  1060.3 11.1 add_add_fusion.2
  1071.4 18.7 %collective-permute-done.39 = bf16[2,2,64,4096]{3,2,0,1:T(8,128)(2,1)} collective-permute-done((bf16[2,2,64,4096]{3,2,0,1:T(8,128)(2,1)}, bf16[2,2,64,4096]{3,2,0,1:T(8,128)(2,1)}, u32[]{:S(2)}, u32[]{:S(2)}) %collective-permute-start.39) | collective-permute-done | bytes 2097184 | tf_op jit(solution)/shard_map/ppermute | solution.py:203
  1092.5 27.5 %collective-permute-done.34 = bf16[2,2,64,4096]{3,2,0,1:T(8,128)(2,1)S(1)} collective-permute-done((bf16[2,2,64,4096]{3,2,0,1:T(8,128)(2,1)S(1)}, bf16[2,2,64,4096]{3,2,0,1:T(8,128)(2,1)S(1)}, u32[]{:S(2)}, u32[]{:S(2)}) %collective-permute-start.34) | collective-permute-done | bytes 2097184 | tf_op jit(solution)/shard_map/ppermute | solution.py:203
  1126.0 20.9 %collective-permute-done.35 = bf16[2,64,4096]{2,1,0:T(8,128)(2,1)S(1)} collective-permute-done((bf16[2,64,4096]{2,1,0:T(8,128)(2,1)S(1)}, bf16[2,64,4096]{2,1,0:T(8,128)(2,1)S(1)}, u32[]{:S(2)}, u32[]{:S(2)}) %collective-permute-start.35) | collective-permute-done | bytes 1048608 | tf_op jit(solution)/shard_map/ppermute | solution.py:203
  1157.6 7.8 collective-permute-done.36
  (528 shorter events, 285.4 us)
Async XLA Ops:
  7.2 51.5 %all-gather.4.cloned.1.call-start = ((), (), s32[]{:S(2)}) async-start(), calls=%async_computation | async-start | bytes 3342336 | tf_op jit(solution)/shard_map/all_gather | solution.py:304
  9.0 291.6 %all-gather.6.cloned.1.call-start = ((), (), s32[]{:S(2)}) async-start(), calls=%async_computation.1 | async-start | bytes 10813440 | tf_op jit(solution)/shard_map/all_gather | solution.py:322
  11.8 405.4 %all-gather.8.cloned.1.call-start = ((), (), s32[]{:S(2)}) async-start(), calls=%async_computation.2 | async-start | bytes 15138816 | tf_op jit(solution)/shard_map/all_gather | solution.py:323
  25.4 33.4 %copy-start.8 = (bf16[1536,1024]{1,0:T(8,128)(2,1)}, bf16[1536,1024]{1,0:T(8,128)(2,1)S(1)}, u32[]{:S(2)}) copy-start(bf16[1536,1024]{1,0:T(8,128)(2,1)S(1)} %get-tuple-element.150) | copy-start | bytes 9437188
  283.1 23.3 %collective-permute-start = (bf16[256,1536]{1,0:T(8,128)(2,1)}, bf16[256,1536]{1,0:T(8,128)(2,1)}, u32[]{:S(2)}, u32[]{:S(2)}) collective-permute-start(bf16[256,1536]{1,0:T(8,128)(2,1)} %get-tuple-element.206), channel_id=1, source_target_pairs={{0,1},{1,0},{2,3},{3,2},{4,5},{5,4},{6,7},{7,6},{8,9},{9,8},{10,11... | collective-permute-start | bytes 2359304 | tf_op jit(solution)/shard_map/ppermute | solution.py:203
  288.4 31.6 %collective-permute-start.1 = (bf16[256,1536]{1,0:T(8,128)(2,1)}, bf16[256,1536]{1,0:T(8,128)(2,1)}, u32[]{:S(2)}, u32[]{:S(2)}) collective-permute-start(bf16[256,1536]{1,0:T(8,128)(2,1)} %get-tuple-element.208), channel_id=1, source_target_pairs={{0,1},{1,0},{2,3},{3,2},{4,5},{5,4},{6,7},{7,6},{8,9},{9,8},{10,11... | collective-permute-start | bytes 2359304 | tf_op jit(solution)/shard_map/ppermute | solution.py:203
  480.2 54.8 %slice-start = ((s8[6291456]{0:T(1024)(128)(4,1)}), s8[4194304]{0:T(1024)(128)(4,1)S(1)}, s32[]{:S(2)}) async-start(s8[6291456]{0:T(1024)(128)(4,1)} %bitcast.463), calls=%async_computation.3 | async-start | bytes 8388608
  493.1 41.9 %slice-start.1 = ((s8[6291456]{0:T(1024)(128)(4,1)}), s8[2097152]{0:T(1024)(128)(4,1)S(1)}, s32[]{:S(2)}) async-start(s8[6291456]{0:T(1024)(128)(4,1)} %bitcast.463), calls=%async_computation.4 | async-start | bytes 4194304
  558.9 9.8 collective-permute-start.23
  568.7 4.1 collective-permute-start.24
  571.3 452.2 %collective-permute-start.38 = (bf16[512,4096]{1,0:T(8,128)(2,1)}, bf16[512,4096]{1,0:T(8,128)(2,1)}, u32[]{:S(2)}, u32[]{:S(2)}) collective-permute-start(bf16[512,4096]{1,0:T(8,128)(2,1)} %convolution_convert_fusion), channel_id=1, source_target_pairs={{0,2},{2,0},{4,6},{6,4},{8,10},{10,8},{12,14},{14,12},{16,18},{18,... | collective-permute-start | bytes 12582920 | tf_op jit(solution)/shard_map/ppermute | solution.py:203
  572.8 16.3 %collective-permute-start.25 = (f32[10496]{0:T(1024)S(1)}, f32[10496]{0:T(1024)S(1)}, u32[]{:S(2)}, u32[]{:S(2)}) collective-permute-start(f32[10496]{0:T(1024)S(1)} %add.537), channel_id=1, source_target_pairs={{0,8},{2,10},{4,12},{6,14},{8,0},{10,2},{12,4},{14,6},{16,24},{18,... | collective-permute-start | bytes 125960 | tf_op jit(solution)/shard_map/ppermute | solution.py:203
  582.9 458.3 %collective-permute-start.33 = (bf16[512,4096]{1,0:T(8,128)(2,1)}, bf16[512,4096]{1,0:T(8,128)(2,1)}, u32[]{:S(2)}, u32[]{:S(2)}) collective-permute-start(bf16[512,4096]{1,0:T(8,128)(2,1)} %convolution_convert_fusion.1), channel_id=1, source_target_pairs={{0,2},{2,0},{4,6},{6,4},{8,10},{10,8},{12,14},{14,12},{16,18},{18,... | collective-permute-start | bytes 12582920 | tf_op jit(solution)/shard_map/ppermute | solution.py:203
  582.9 51.1 %collective-permute-start.2 = (bf16[1536,512]{1,0:T(8,128)(2,1)}, bf16[1536,512]{1,0:T(8,128)(2,1)}, u32[]{:S(2)}, u32[]{:S(2)}) collective-permute-start(bf16[1536,512]{1,0:T(8,128)(2,1)} %convolution_convert_fusion.2), channel_id=1, source_target_pairs={{0,1},{1,0},{2,3},{3,2},{4,5},{5,4},{6,7},{7,6},{8,9},{9,8},{10,11... | collective-permute-start | bytes 4718600 | tf_op jit(solution)/shard_map/ppermute | solution.py:203
  589.1 12.0 %collective-permute-start.26 = (f32[10496]{0:T(1024)S(1)}, f32[10496]{0:T(1024)S(1)}, u32[]{:S(2)}, u32[]{:S(2)}) collective-permute-start(f32[10496]{0:T(1024)S(1)} %add.538), channel_id=1, source_target_pairs={{0,16},{2,18},{4,20},{6,22},{8,24},{10,26},{12,28},{14,30},{16,0},... | collective-permute-start | bytes 125960 | tf_op jit(solution)/shard_map/ppermute | solution.py:203
  601.1 19.7 %collective-permute-start.27 = (f32[10496]{0:T(1024)S(1)}, f32[10496]{0:T(1024)S(1)}, u32[]{:S(2)}, u32[]{:S(2)}) collective-permute-start(f32[10496]{0:T(1024)S(1)} %add.539), channel_id=1, source_target_pairs={{0,1},{1,0},{2,3},{3,2},{4,5},{5,4},{6,7},{7,6},{8,9},{9,8},{10,11... | collective-permute-start | bytes 125960 | tf_op jit(solution)/shard_map/ppermute | solution.py:203
  606.2 19.6 %collective-permute-start.28 = (bf16[512,1024]{1,0:T(8,128)(2,1)}, bf16[512,1024]{1,0:T(8,128)(2,1)S(1)}, u32[]{:S(2)}, u32[]{:S(2)}) collective-permute-start(bf16[512,1024]{1,0:T(8,128)(2,1)} %convolution_convert_fusion.4), channel_id=1, source_target_pairs={{0,2},{2,0},{4,6},{6,4},{8,10},{10,8},{12,14},{14,12},{16,18},{18,... | collective-permute-start | bytes 3145736 | tf_op jit(solution)/shard_map/ppermute | solution.py:203
  633.1 236.1 %collective-permute-start.29 = (bf16[2,2,64,1024]{3,2,0,1:T(8,128)(2,1)}, bf16[2,2,64,1024]{3,2,0,1:T(8,128)(2,1)}, u32[]{:S(2)}, u32[]{:S(2)}) collective-permute-start(bf16[2,2,64,1024]{3,2,0,1:T(8,128)(2,1)} %fusion.77), channel_id=1, source_target_pairs={{0,4},{2,6},{4,0},{6,2},{8,12},{10,14},{12,8},{14,10},{16,20},{18,... | collective-permute-start | bytes 1572872 | tf_op jit(solution)/shard_map/ppermute | solution.py:203
  808.3 43.4 %copy-start.24 = (bf16[3072,128]{1,0:T(8,128)(2,1)S(1)}, bf16[3072,128]{1,0:T(8,128)(2,1)}, u32[]{:S(2)}) copy-start(bf16[3072,128]{1,0:T(8,128)(2,1)} %convert_element_type.430) | copy-start | bytes 2359300
  808.3 43.4 %copy-start.26 = (bf16[128,3072]{0,1:T(8,128)(2,1)S(1)}, bf16[128,3072]{0,1:T(8,128)(2,1)}, u32[]{:S(2)}) copy-start(bf16[128,3072]{0,1:T(8,128)(2,1)} %copy.256) | copy-start | bytes 2359300
  870.6 30.2 %collective-permute-start.30 = (bf16[2,64,1024]{2,1,0:T(8,128)(2,1)S(1)}, bf16[2,64,1024]{2,1,0:T(8,128)(2,1)S(1)}, u32[]{:S(2)}, u32[]{:S(2)}) collective-permute-start(bf16[2,64,1024]{2,1,0:T(8,128)(2,1)S(1)} %fusion.81), channel_id=1, source_target_pairs={{0,8},{2,10},{4,12},{6,14},{8,0},{10,2},{12,4},{14,6},{16,24},{18,... | collective-permute-start | bytes 786440 | tf_op jit(solution)/shard_map/ppermute | solution.py:203
  876.9 1.2 collective-permute-start.43
  878.1 3.7 collective-permute-start.44
  881.9 9.0 collective-permute-start.45
  890.9 4.6 collective-permute-start.46
  895.5 3.7 collective-permute-start.47
  898.8 3.4 collective-permute-start.7
  899.3 5.6 collective-permute-start.11
  900.8 155.7 %collective-permute-start.4 = (bf16[1536,384]{1,0:T(8,128)(2,1)}, bf16[1536,384]{1,0:T(8,128)(2,1)}, u32[]{:S(2)}, u32[]{:S(2)}) collective-permute-start(bf16[1536,384]{1,0:T(8,128)(2,1)} %get-tuple-element.184), channel_id=1, source_target_pairs={{0,1},{1,0},{2,3},{3,2},{4,5},{5,4},{6,7},{7,6},{8,9},{9,8},{10,11... | collective-permute-start | bytes 3538952 | tf_op jit(solution)/shard_map/ppermute | solution.py:203
  902.2 154.4 %collective-permute-start.3 = (bf16[1536,384]{1,0:T(8,128)(2,1)}, bf16[1536,384]{1,0:T(8,128)(2,1)}, u32[]{:S(2)}, u32[]{:S(2)}) collective-permute-start(bf16[1536,384]{1,0:T(8,128)(2,1)} %get-tuple-element.182), channel_id=1, source_target_pairs={{0,1},{1,0},{2,3},{3,2},{4,5},{5,4},{6,7},{7,6},{8,9},{9,8},{10,11... | collective-permute-start | bytes 3538952 | tf_op jit(solution)/shard_map/ppermute | solution.py:203
  904.9 1.9 collective-permute-start.19
  906.8 9.1 collective-permute-start.31
  916.0 1.7 collective-permute-start.15
  916.2 40.8 %copy-start.55 = (f32[64,512]{1,0:T(8,128)S(1)}, f32[64,512]{1,0:T(8,128)}, u32[]{:S(2)}) copy-start(f32[64,512]{1,0:T(8,128)} %param.21) | copy-start | bytes 393220
  916.2 40.8 %copy-start.56 = (f32[2,64,512]{2,1,0:T(8,128)S(1)}, f32[2,64,512]{2,1,0:T(8,128)}, u32[]{:S(2)}) copy-start(f32[2,64,512]{2,1,0:T(8,128)} %param.28) | copy-start | bytes 786436
  917.7 38.3 %collective-permute-start.32 = (bf16[64,512]{1,0:T(8,128)(2,1)S(1)}, bf16[64,512]{1,0:T(8,128)(2,1)S(1)}, u32[]{:S(2)}, u32[]{:S(2)}) collective-permute-start(bf16[64,512]{1,0:T(8,128)(2,1)S(1)} %slice.551), channel_id=1, source_target_pairs={{0,1},{1,0},{2,3},{3,2},{4,5},{5,4},{6,7},{7,6},{8,9},{9,8},{10,11... | collective-permute-start | bytes 196616 | tf_op jit(solution)/shard_map/ppermute | solution.py:203
  956.0 6.4 collective-permute-start.8
  962.3 5.7 collective-permute-start.12
  963.4 58.1 %copy-start.16 = (f32[3,64,512]{2,1,0:T(8,128)S(1)}, f32[3,64,512]{2,1,0:T(8,128)}, u32[]{:S(2)}) copy-start(f32[3,64,512]{2,1,0:T(8,128)} %param.20) | copy-start | bytes 1179652
  963.4 58.1 %copy-start.52 = (f32[2,3,64,512]{3,2,1,0:T(8,128)S(1)}, f32[2,3,64,512]{3,2,1,0:T(8,128)}, u32[]{:S(2)}) copy-start(f32[2,3,64,512]{3,2,1,0:T(8,128)} %param.27) | copy-start | bytes 2359300
  963.5 58.1 %copy-start.78 = (f32[3,512]{1,0:T(4,128)S(1)}, f32[3,512]{1,0:T(4,128)}, u32[]{:S(2)}) copy-start(f32[3,512]{1,0:T(4,128)} %maximum_maximum_fusion) | copy-start | bytes 18436
  968.0 6.7 collective-permute-start.20
  974.7 5.7 collective-permute-start.16
  980.4 4.6 collective-permute-start.9
  985.0 5.4 collective-permute-start.13
  990.4 5.1 collective-permute-start.21
  995.5 4.6 collective-permute-start.17
  1000.1 5.0 collective-permute-start.10
  1005.1 5.0 collective-permute-start.14
  1010.1 5.0 collective-permute-start.22
  1015.1 5.0 collective-permute-start.18
  1020.1 36.6 %collective-permute-start.5 = (bf16[1536,384]{1,0:T(8,128)(2,1)}, bf16[1536,384]{1,0:T(8,128)(2,1)}, u32[]{:S(2)}, u32[]{:S(2)}) collective-permute-start(bf16[1536,384]{1,0:T(8,128)(2,1)} %get-tuple-element.186), channel_id=1, source_target_pairs={{0,1},{1,0},{2,3},{3,2},{4,5},{5,4},{6,7},{7,6},{8,9},{9,8},{10,11... | collective-permute-start | bytes 3538952 | tf_op jit(solution)/shard_map/ppermute | solution.py:203
  1023.6 36.7 %collective-permute-start.6 = (bf16[1536,384]{1,0:T(8,128)(2,1)}, bf16[1536,384]{1,0:T(8,128)(2,1)}, u32[]{:S(2)}, u32[]{:S(2)}) collective-permute-start(bf16[1536,384]{1,0:T(8,128)(2,1)} %get-tuple-element.188), channel_id=1, source_target_pairs={{0,1},{1,0},{2,3},{3,2},{4,5},{5,4},{6,7},{7,6},{8,9},{9,8},{10,11... | collective-permute-start | bytes 3538952 | tf_op jit(solution)/shard_map/ppermute | solution.py:203
  1024.4 35.9 %slice-start.2 = ((s8[6291456]{0:T(1024)(128)(4,1)}), s8[4194304]{0:T(1024)(128)(4,1)S(1)}, s32[]{:S(2)}) async-start(s8[6291456]{0:T(1024)(128)(4,1)} %bitcast.470), calls=%async_computation.5 | async-start | bytes 8388608
  1041.2 48.9 %collective-permute-start.39 = (bf16[2,2,64,4096]{3,2,0,1:T(8,128)(2,1)}, bf16[2,2,64,4096]{3,2,0,1:T(8,128)(2,1)}, u32[]{:S(2)}, u32[]{:S(2)}) collective-permute-start(bf16[2,2,64,4096]{3,2,0,1:T(8,128)(2,1)} %fusion.55), channel_id=1, source_target_pairs={{0,4},{2,6},{4,0},{6,2},{8,12},{10,14},{12,8},{14,10},{16,20},{18,... | collective-permute-start | bytes 6291464 | tf_op jit(solution)/shard_map/ppermute | solution.py:203
  1053.9 36.1 %slice-start.10 = ((s8[8388608]{0:T(1024)(128)(4,1)}), s8[4194304]{0:T(1024)(128)(4,1)S(1)}, s32[]{:S(2)}) async-start(s8[8388608]{0:T(1024)(128)(4,1)} %bitcast.486), calls=%async_computation.13 | async-start | bytes 8388608
  1056.6 63.4 %collective-permute-start.34 = (bf16[2,2,64,4096]{3,2,0,1:T(8,128)(2,1)S(1)}, bf16[2,2,64,4096]{3,2,0,1:T(8,128)(2,1)S(1)}, u32[]{:S(2)}, u32[]{:S(2)}) collective-permute-start(bf16[2,2,64,4096]{3,2,0,1:T(8,128)(2,1)S(1)} %fusion.54), channel_id=1, source_target_pairs={{0,4},{2,6},{4,0},{6,2},{8,12},{10,14},{12,8},{14,10},{16,20},{18,... | collective-permute-start | bytes 6291464 | tf_op jit(solution)/shard_map/ppermute | solution.py:203
  1060.3 29.8 %slice-start.11 = ((s8[8388608]{0:T(1024)(128)(4,1)}), s8[4194304]{0:T(1024)(128)(4,1)S(1)}, s32[]{:S(2)}) async-start(s8[8388608]{0:T(1024)(128)(4,1)} %bitcast.486), calls=%async_computation.14 | async-start | bytes 8388608
  1092.4 30.7 %collective-permute-start.40 = (bf16[2,64,4096]{2,1,0:T(8,128)(2,1)S(1)}, bf16[2,64,4096]{2,1,0:T(8,128)(2,1)S(1)}, u32[]{:S(2)}, u32[]{:S(2)}) collective-permute-start(bf16[2,64,4096]{2,1,0:T(8,128)(2,1)S(1)} %fusion.66), channel_id=1, source_target_pairs={{0,8},{2,10},{4,12},{6,14},{8,0},{10,2},{12,4},{14,6},{16,24},{18,... | collective-permute-start | bytes 3145736 | tf_op jit(solution)/shard_map/ppermute | solution.py:203
  1122.9 24.0 %collective-permute-start.35 = (bf16[2,64,4096]{2,1,0:T(8,128)(2,1)S(1)}, bf16[2,64,4096]{2,1,0:T(8,128)(2,1)S(1)}, u32[]{:S(2)}, u32[]{:S(2)}) collective-permute-start(bf16[2,64,4096]{2,1,0:T(8,128)(2,1)S(1)} %fusion.65), channel_id=1, source_target_pairs={{0,8},{2,10},{4,12},{6,14},{8,0},{10,2},{12,4},{14,6},{16,24},{18,... | collective-permute-start | bytes 3145736 | tf_op jit(solution)/shard_map/ppermute | solution.py:203
  1123.3 24.7 %collective-permute-start.41 = (bf16[64,4096]{1,0:T(8,128)(2,1)S(1)}, bf16[64,4096]{1,0:T(8,128)(2,1)S(1)}, u32[]{:S(2)}, u32[]{:S(2)}) collective-permute-start(bf16[64,4096]{1,0:T(8,128)(2,1)S(1)} %fusion.76), channel_id=1, source_target_pairs={{0,16},{2,18},{4,20},{6,22},{8,24},{10,26},{12,28},{14,30},{16,0},... | collective-permute-start | bytes 1572872 | tf_op jit(solution)/shard_map/ppermute | solution.py:203
  1148.0 17.3 %collective-permute-start.36 = (bf16[64,4096]{1,0:T(8,128)(2,1)}, bf16[64,4096]{1,0:T(8,128)(2,1)}, u32[]{:S(2)}, u32[]{:S(2)}) collective-permute-start(bf16[64,4096]{1,0:T(8,128)(2,1)} %fusion.75), channel_id=1, source_target_pairs={{0,16},{2,18},{4,20},{6,22},{8,24},{10,26},{12,28},{14,30},{16,0},... | collective-permute-start | bytes 1572872 | tf_op jit(solution)/shard_map/ppermute | solution.py:203
  1151.9 17.5 %collective-permute-start.42 = (bf16[64,2048]{1,0:T(8,128)(2,1)S(1)}, bf16[64,2048]{1,0:T(8,128)(2,1)}, u32[]{:S(2)}, u32[]{:S(2)}) collective-permute-start(bf16[64,2048]{1,0:T(8,128)(2,1)S(1)} %bitcast.542), channel_id=1, source_target_pairs={{0,1},{1,0},{2,3},{3,2},{4,5},{5,4},{6,7},{7,6},{8,9},{9,8},{10,11... | collective-permute-start | bytes 786440 | tf_op jit(solution)/shard_map/ppermute | solution.py:203
  1168.1 6.4 collective-permute-start.37
  (90 other events, 708.6 us)
Sparse Core Ops, SparseCore 0:
  10.8 47.9 all-gather.3
  62.2 85.6 all-gather.5
  151.3 103.8 all-gather.7

commit v2 on v0

v2 whole, which is shorter than its diff:
```python
import functools

import jax
import jax.numpy as jnp
from jax import lax
from jax.experimental import pallas as pl
from jax.experimental.pallas import tpu as pltpu
from jax.sharding import PartitionSpec as P

HEAD_DIM = 64
ADAM_STEP = 5
PAIR = 2 * HEAD_DIM
LOG2E = 1.4426950408889634

low = jnp.bfloat16
f32 = jnp.float32
very_low = -1e30
clip_tau = 5.0
learn_rate = 0.25
weight_decay = 0.1
moment_beta = 0.5
adam_epsilon = 1e-08


def norm_rows(values, gain_row, shift_row):
    center = values - jnp.mean(values, axis=-1, keepdims=True)
    spread = jnp.mean(center * center, axis=-1, keepdims=True)
    return center * lax.rsqrt(spread + 1e-05) * gain_row + shift_row


def times_transposed(left_side, right_side):
    return lax.dot_general(
        left_side, right_side, (((1,), (1,)), ((), ())), preferred_element_type=jnp.float32
    )


def adam_update(param, moments, grad, step_value):
    first_moment = moment_beta * moments[0] + (1.0 - moment_beta) * grad
    second_moment = moment_beta * moments[1] + (1.0 - moment_beta) * grad * grad
    correct = 1.0 - jnp.power(moment_beta, step_value)
    update = first_moment / correct / (jnp.sqrt(second_moment / correct) + adam_epsilon)
    return (
        param - learn_rate * (update + weight_decay * param),
        jnp.stack([first_moment, second_moment]),
    )


def dot(left, right):
    return lax.dot_general(left, right, (((1,), (0,)), ((), ())), preferred_element_type=f32)


def dot_nt(left, right):
    return lax.dot_general(left, right, (((1,), (1,)), ((), ())), preferred_element_type=f32)


def kernel_params(axes=1):
    return pltpu.CompilerParams(
        vmem_limit_bytes=58 * 2**20, dimension_semantics=("arbitrary",) * axes
    )


def brief(flops):
    return pl.CostEstimate(flops=flops // 16, bytes_accessed=2**20, transcendentals=0)


def project_kernel(pairs, x, weights, biases, marks, q_ref, qt_ref, k_ref, kt_ref, v_ref, vt_ref):
    for pair in range(pairs):
        span = slice(pair * PAIR, (pair + 1) * PAIR)
        every = dot(x[...], weights[:, 3 * pair * PAIR : 3 * (pair + 1) * PAIR])
        q = every[:, :PAIR] + biases[0:1, span]
        k = every[:, PAIR : 2 * PAIR]
        v = every[:, 2 * PAIR :] + biases[1:2, span]
        q_ref[:, span] = q.astype(low)
        qt_ref[span, :] = q.T.astype(low)
        k_ref[pair, :, :PAIR] = k.astype(low)
        k_ref[pair, :, PAIR:] = marks[...]
        kt_ref[span, :] = k.T.astype(low)
        v_ref[:, span] = v.astype(low)
        vt_ref[span, :] = v.T.astype(low)


def project(x, weights, biases, marks):
    tokens, dim = x.shape
    width = weights.shape[1] // 3
    pairs = width // PAIR
    block = min(512, tokens)
    rows = lambda n: pl.BlockSpec((block, n), lambda i: (i, 0))
    columns = pl.BlockSpec((width, block), lambda i: (0, i))
    natural = jax.ShapeDtypeStruct((tokens, width), low)
    turned = jax.ShapeDtypeStruct((width, tokens), low)
    return pl.pallas_call(
        functools.partial(project_kernel, pairs),
        grid=(tokens // block,),
        in_specs=[
            rows(dim),
            pl.BlockSpec((dim, 3 * width), lambda i: (0, 0)),
            pl.BlockSpec((2, width), lambda i: (0, 0)),
            rows(PAIR),
        ],
        out_specs=[
            rows(width),
            columns,
            pl.BlockSpec((pairs, block, 2 * PAIR), lambda i: (0, i, 0)),
            columns,
            rows(width),
            columns,
        ],
        out_shape=[
            natural,
            turned,
            jax.ShapeDtypeStruct((pairs, tokens, 2 * PAIR), low),
            turned,
            natural,
            turned,
        ],
        compiler_params=kernel_params(),
        cost_estimate=brief(6 * tokens * dim * width),
        name="project",
    )(x, weights, biases, marks)


def forward_kernel(
    bq, ch, tokens, k_cur, k_nxt, q_cur, q_nxt, s_cur, s_nxt, vt,
    p_ref, ot_ref, o_ref, l_ref, m_ref, score_a, score_b, max_a, max_b,
):
    zeros = jnp.zeros((HEAD_DIM, bq), low)
    factor = f32(LOG2E * HEAD_DIM**-0.5)
    steps = tokens // ch
    nq = tokens // bq

    def query_rows(q_ref, marks, head):
        q = q_ref[head * HEAD_DIM : (head + 1) * HEAD_DIM, :]
        parts = [q, zeros] if head == 0 else [zeros, q]
        return jnp.concatenate(parts + [marks[...]], axis=0)

    def scores(keys, q, out, step, top):
        part = dot(keys[step * ch : (step + 1) * ch, :], q)
        out[step * ch : (step + 1) * ch, :] = part
        return jnp.maximum(top, jnp.max(part.reshape(ch // 8, 8, bq), axis=0))

    def finish(top, out):
        out[...] = jnp.broadcast_to(jnp.max(top, axis=0, keepdims=True), (8, bq))

    lowest = jnp.full((8, bq), -3e38, f32)

    @pl.when(pl.program_id(0) == 0)
    def _():
        q = query_rows(q_cur, s_cur, 0)
        top = lowest
        for step in range(steps):
            top = scores(k_cur, q, score_a, step, top)
        finish(top, max_a)

    def phase(head, s_in, m_in, keys, q, s_out, m_out):
        top_row = m_in[0:1, :]
        top = lowest
        sums = jnp.zeros((8, bq), f32)
        total = jnp.zeros((HEAD_DIM, bq), f32)
        for step in range(steps):
            span = slice(step * ch, (step + 1) * ch)
            top = scores(keys, q, s_out, step, top)
            p = jnp.exp2((s_in[span, :] - top_row) * factor)
            sums = sums + jnp.sum(p.reshape(ch // 8, 8, bq), axis=0)
            p_low = p.astype(low)
            p_ref[0, head, 0, span, :] = p_low
            total = total + dot(vt[head * HEAD_DIM : (head + 1) * HEAD_DIM, span], p_low)
        finish(top, m_out)
        row_sum = jnp.sum(sums, axis=0, keepdims=True)
        l_ref[0, head : head + 1, :] = row_sum
        best = top_row[:, :PAIR]
        for first in range(PAIR, bq, PAIR):
            best = jnp.maximum(best, top_row[:, first : first + PAIR])
        here = jnp.where(pl.program_id(0) % nq == 0, lowest[0:1, :PAIR], m_ref[0, head : head + 1, :])
        m_ref[0, head : head + 1, :] = jnp.maximum(here, best)
        return total / row_sum

    first = phase(0, score_a, max_a, k_cur, query_rows(q_cur, s_cur, 1), score_b, max_b)
    second = phase(1, score_b, max_b, k_nxt, query_rows(q_nxt, s_nxt, 0), score_a, max_a)
    both = jnp.concatenate([first, second], axis=0)
    ot_ref[...] = both
    o_ref[...] = both.T.astype(low)


def attention_forward(keys, q_t, marks_t, v_t, first, pairs, bq, ch=512):
    _, tokens, _ = keys.shape
    nq = tokens // bq
    ch = min(ch, tokens)
    count = pairs * nq
    now = lambda i: i
    later = lambda i: jnp.minimum(i + 1, count - 1)
    key_spec = lambda at: pl.BlockSpec(
        (None, tokens, 2 * PAIR), lambda i: (first + at(i) // nq, 0, 0)
    )
    query_spec = lambda at: pl.BlockSpec((PAIR, bq), lambda i: (first + at(i) // nq, at(i) % nq))
    mark_spec = lambda at: pl.BlockSpec((PAIR, bq), lambda i: (0, at(i) % nq))
    row_spec = pl.BlockSpec((1, 2, bq), lambda i: (i // nq, 0, i % nq))
    size = 2 * pairs * tokens * tokens
    return pl.pallas_call(
        functools.partial(forward_kernel, bq, ch, tokens),
        grid=(count,),
        in_specs=[
            key_spec(now), key_spec(later), query_spec(now), query_spec(later),
            mark_spec(now), mark_spec(later),
            pl.BlockSpec((PAIR, tokens), lambda i: (first + i // nq, 0)),
        ],
        out_specs=[
            pl.BlockSpec((1, 2, 1, tokens, bq), lambda i: (i // nq, 0, i % nq, 0, 0)),
            pl.BlockSpec((PAIR, bq), lambda i: (i // nq, i % nq)),
            pl.BlockSpec((bq, PAIR), lambda i: (i % nq, i // nq)),
            row_spec,
            pl.BlockSpec((1, 2, PAIR), lambda i: (i // nq, 0, 0)),
        ],
        out_shape=[
            jax.ShapeDtypeStruct((pairs, 2, nq, tokens, bq), low),
            jax.ShapeDtypeStruct((pairs * PAIR, tokens), f32),
            jax.ShapeDtypeStruct((tokens, pairs * PAIR), low),
            jax.ShapeDtypeStruct((pairs, 2, tokens), f32),
            jax.ShapeDtypeStruct((pairs, 2, PAIR), f32),
        ],
        scratch_shapes=[
            pltpu.VMEM((tokens, bq), f32),
            pltpu.VMEM((tokens, bq), f32),
            pltpu.VMEM((8, bq), f32),
            pltpu.VMEM((8, bq), f32),
        ],
        compiler_params=kernel_params(),
        cost_estimate=brief(16 * HEAD_DIM * size),
        name="attend",
    )(keys, keys, q_t, q_t, marks_t, marks_t, v_t)


def backward_kernel(
    bq, ch, tokens, p_ref, grad, out_t, totals, q, v, kt, g_ref, b_ref, key_acc, value_acc, sums
):
    step_q = pl.program_id(0)

    @pl.when(step_q == 0)
    def _():
        key_acc[...] = jnp.zeros_like(key_acc)
        value_acc[...] = jnp.zeros_like(value_acc)
        sums[...] = jnp.zeros_like(sums)

    zeros = jnp.zeros((HEAD_DIM, bq), low)
    scale = f32(HEAD_DIM**-0.5)
    lane = lax.broadcasted_iota(jnp.int32, (bq, PAIR), 1)

    def diagonal(x):
        zero = jnp.zeros_like(x)
        return jnp.concatenate(
            [jnp.where(lane < HEAD_DIM, x, zero), jnp.where(lane >= HEAD_DIM, x, zero)], axis=0
        )

    grad_t = grad[...].astype(f32).T
    scaled_t, deltas = [], []
    for head in range(2):
        inverse = 1.0 / totals[0, head : head + 1, :]
        span = slice(head * HEAD_DIM, (head + 1) * HEAD_DIM)
        part = grad_t[span] * inverse
        deltas.append(jnp.sum(part * out_t[span, :], axis=0, keepdims=True))
        scaled_t.append(part)
    scaled = jnp.concatenate(scaled_t, axis=0).T.astype(low)
    grad_rows = diagonal(scaled)
    query_rows = diagonal(q[...])
    grad_columns = [
        jnp.concatenate([scaled_t[0].astype(low), zeros], axis=0),
        jnp.concatenate([zeros, scaled_t[1].astype(low)], axis=0),
    ]
    query_grads = [jnp.zeros((HEAD_DIM, bq), f32) for _ in range(2)]
    for step in range(tokens // ch):
        span = slice(step * ch, (step + 1) * ch)
        values = v[span, :]
        probs, score_grads = [], []
        for head in range(2):
            prob_grad = dot(values, grad_columns[head])
            p = p_ref[0, head, 0, span, :]
            score_grad = (p.astype(f32) * (prob_grad - deltas[head])).astype(low)
            probs.append(p)
            score_grads.append(score_grad)
            query_grads[head] = query_grads[head] + dot(
                kt[head * HEAD_DIM : (head + 1) * HEAD_DIM, span], score_grad
            )
        value_acc[span, :] += dot(jnp.concatenate(probs, axis=1), grad_rows)
        key_acc[span, :] += dot(jnp.concatenate(score_grads, axis=1), query_rows)
    query_grad = jnp.concatenate(query_grads, axis=0).T * scale
    g_ref[pl.ds(pl.multiple_of(step_q * bq, bq), bq), 0:PAIR] = query_grad.astype(low)
    sums[...] += jnp.sum(query_grad.reshape(bq // 8, 8, PAIR), axis=0)

    @pl.when(step_q == pl.num_programs(0) - 1)
    def _():
        g_ref[:, PAIR : 2 * PAIR] = (key_acc[...] * scale).astype(low)
        value_grad = value_acc[...]
        g_ref[:, 2 * PAIR :] = value_grad.astype(low)
        b_ref[0:1, :] = jnp.sum(sums[...], axis=0, keepdims=True)
        b_ref[1:2, :] = jnp.sum(value_grad, axis=0, keepdims=True)


def attention_backward(probs, grad, out_t, totals, q, v, k_t, pair, at, ch=1536):
    _, _, nq, tokens, bq = probs.shape
    ch = min(ch, tokens)
    size = 2 * tokens * tokens
    return pl.pallas_call(
        functools.partial(backward_kernel, bq, ch, tokens),
        grid=(nq,),
        in_specs=[
            pl.BlockSpec((1, 2, 1, tokens, bq), lambda i: (at, 0, i, 0, 0)),
            pl.BlockSpec((bq, PAIR), lambda i: (i, 0)),
            pl.BlockSpec((PAIR, bq), lambda i: (at, i)),
            pl.BlockSpec((1, 2, bq), lambda i: (at, 0, i)),
            pl.BlockSpec((bq, PAIR), lambda i: (i, pair)),
            pl.BlockSpec((tokens, PAIR), lambda i: (0, pair)),
            pl.BlockSpec((PAIR, tokens), lambda i: (pair, 0)),
        ],
        out_specs=[
            pl.BlockSpec((tokens, 3 * PAIR), lambda i: (0, 0)),
            pl.BlockSpec((2, PAIR), lambda i: (0, 0)),
        ],
        out_shape=[
            jax.ShapeDtypeStruct((tokens, 3 * PAIR), low),
            jax.ShapeDtypeStruct((2, PAIR), f32),
        ],
        scratch_shapes=[
            pltpu.VMEM((tokens, PAIR), f32),
            pltpu.VMEM((tokens, PAIR), f32),
            pltpu.VMEM((8, PAIR), f32),
        ],
        compiler_params=kernel_params(),
        cost_estimate=brief(32 * HEAD_DIM * size),
        name="attend_back",
    )(probs, grad, out_t, totals, q, v, k_t)


def gelu_and_slope(x):
    size = jnp.abs(x) * f32(0.7071067811865476)
    t = 1.0 / (1.0 + f32(0.3275911) * size)
    bell = jnp.exp2(x * x * f32(-0.5 * LOG2E))
    poly = f32(1.061405429 / 2)
    for coefficient in (-1.453152027, 1.421413741, -0.284496736, 0.254829592):
        poly = poly * t + f32(coefficient / 2)
    tail = poly * t * bell
    phi = jnp.where(x >= 0, 1.0 - tail, tail)
    return x * phi, phi + x * bell * f32(0.3989422804014327)


def feed_kernel(rows, ch, x, up, down, bias, hidden_ref, slope_ref, out_ref):
    @pl.when(pl.program_id(0) == 0)
    def _():
        out_ref[...] = jnp.zeros_like(out_ref)

    def finish(span, pre):
        hidden, slope = gelu_and_slope(pre + bias[...])
        hidden = hidden.astype(low)
        hidden_ref[span, :] = hidden
        slope_ref[span, :] = slope.astype(low)
        out_ref[span, :] += dot_nt(hidden, down[...])

    before = None
    for first in range(0, rows, ch):
        span = slice(first, first + ch)
        pre = dot(x[span, :], up[...])
        if before is not None:
            finish(*before)
        before = (span, pre)
    finish(*before)


def feed_forward(x, weights, bias, units, block=1024, ch=512):
    rows, dim = x.shape
    groups = weights.shape[0]
    block = min(block, units)
    per = units // block
    ch = ch if rows % ch == 0 else rows
    every = groups * units
    weight = lambda skip: pl.BlockSpec(
        (None, dim, block), lambda i: (i // per, 0, skip * per + i % per)
    )
    part = pl.BlockSpec((rows, block), lambda i: (0, i))
    whole = pl.BlockSpec((rows, dim), lambda i: (0, 0))
    return pl.pallas_call(
        functools.partial(feed_kernel, rows, ch),
        grid=(groups * per,),
        in_specs=[whole, weight(0), weight(1), pl.BlockSpec((1, block), lambda i: (0, i))],
        out_specs=[part, part, whole],
        out_shape=[
            jax.ShapeDtypeStruct((rows, every), low),
            jax.ShapeDtypeStruct((rows, every), low),
            jax.ShapeDtypeStruct((rows, dim), f32),
        ],
        compiler_params=kernel_params(),
        cost_estimate=brief(4 * rows * dim * every),
        name="feed",
    )(x, weights, weights, bias)


def feed_back_kernel(
    rows, ch, blocks, core, x, normed, up, down, slope, hidden,
    sum_ref, out_ref, sent_ref, own_ref, x_t, normed_t, pre_all,
):
    half = x_t.shape[0] // 2
    size = 2 * half // blocks

    @pl.when(pl.program_id(0) == 0)
    def _():
        out_ref[...] = jnp.zeros_like(out_ref)
        for source, turned in ((x, x_t), (normed, normed_t)):
            for first in range(0, blocks, 2):
                pair = source[:, first * size : (first + 2) * size].T
                for odd in range(2):
                    own = jnp.where(core[0] == odd, half, 0)
                    at = pl.multiple_of(own + first // 2 * size, size)
                    turned[pl.ds(at, size), :] = pair[odd * size : (odd + 1) * size]

    block = slope.shape[1]
    sums = jnp.zeros((8, block), f32)

    def finish(span, hidden_grad, sums):
        pre = hidden_grad * slope[span, :].astype(f32)
        sums = sums + jnp.sum(pre.reshape(ch // 8, 8, block), axis=0)
        pre = pre.astype(low)
        pre_all[span, :] = pre
        out_ref[span, :] += dot_nt(pre, up[...])
        return sums

    before = None
    for first in range(0, rows, ch):
        span = slice(first, first + ch)
        hidden_grad = dot(x[span, :], down[...])
        if before is not None:
            sums = finish(*before, sums)
        before = (span, hidden_grad)
    owners = (blocks // 2, size, block)
    sent_ref[:, 1] = dot(x_t[:half, :], hidden[...]).astype(low).reshape(owners)
    sums = finish(*before, sums)
    sum_ref[...] = jnp.sum(sums, axis=0, keepdims=True)
    own_ref[:, 1] = dot(x_t[half:, :], hidden[...]).reshape(owners)
    sent_ref[:, 0] = dot(normed_t[:half, :], pre_all[...]).astype(low).reshape(owners)
    own_ref[:, 0] = dot(normed_t[half:, :], pre_all[...]).reshape(owners)


def feed_back(core, blocks, x, normed, weights, slope, hidden, units, block=512, ch=512):
    rows, dim = x.shape
    groups = weights.shape[0]
    block = min(block, units)
    per = units // block
    ch = ch if rows % ch == 0 else rows
    every = groups * units
    weight = lambda skip: pl.BlockSpec(
        (None, dim, block), lambda i: (i // per, 0, skip * per + i % per)
    )
    part = pl.BlockSpec((rows, block), lambda i: (0, i))
    owners = (blocks // 2, 2, dim // blocks)
    half = pl.BlockSpec(owners + (block,), lambda i: (0, 0, 0, i))
    once = pl.BlockSpec((rows, dim), lambda i: (0, 0), pipeline_mode=pl.Buffered(1))
    return pl.pallas_call(
        functools.partial(feed_back_kernel, rows, ch, blocks),
        grid=(groups * per,),
        in_specs=[
            pl.BlockSpec(memory_space=pltpu.SMEM), once, once, weight(0), weight(1), part, part
        ],
        out_specs=[
            pl.BlockSpec((1, block), lambda i: (0, i)),
            pl.BlockSpec((rows, dim), lambda i: (0, 0)),
            half,
            half,
        ],
        out_shape=[
            jax.ShapeDtypeStruct((1, every), f32),
            jax.ShapeDtypeStruct((rows, dim), f32),
            jax.ShapeDtypeStruct(owners + (every,), low),
            jax.ShapeDtypeStruct(owners + (every,), f32),
        ],
        scratch_shapes=[
            pltpu.VMEM((dim, rows), low),
            pltpu.VMEM((dim, rows), low),
            pltpu.VMEM((rows, block), low),
        ],
        compiler_params=kernel_params(),
        cost_estimate=brief(8 * rows * dim * every),
        name="feed_back",
    )(core, x, normed, weights, weights, slope, hidden)


def bits_of(size):
    return size.bit_length() - 1


def swap(value, axis_name, mask):
    size = lax.axis_size(axis_name)
    return lax.ppermute(value, axis_name, [(i, i ^ mask) for i in range(size)])


def pick(value, index, axis):
    return lax.dynamic_index_in_dim(value, index, axis, keepdims=False)


def after(value, *others):
    return lax.optimization_barrier((value,) + others)[0]


def halve_parts(value, axis_name, bit, axis):
    mine = (lax.axis_index(axis_name) >> bit) & 1
    return pick(value, 1 - mine, axis).astype(jnp.bfloat16), pick(value, mine, axis)


def halve(value, axis_name, bit, axis):
    sent, kept = halve_parts(value, axis_name, bit, axis)
    return kept + swap(sent, axis_name, 1 << bit).astype(jnp.float32)


def chip_steps():
    return bits_of(lax.axis_size("dp")) - 1


def by_bits(value):
    return value.reshape((2,) * chip_steps() + (-1, value.shape[-1]))


def core_halves(rows_t):
    core = lax.axis_index("dp") & 1
    tokens = rows_t.shape[1]
    split = rows_t.reshape(lax.axis_size("dp") // 2, 2, -1, tokens)
    return pick(split, 1 - core, 1).reshape(-1, tokens), pick(split, core, 1).reshape(-1, tokens)


def core_first(halves, right):
    other, own = halves
    sent = jnp.dot(other, right, preferred_element_type=jnp.float32).astype(jnp.bfloat16)
    got = swap(sent, "dp", 1)
    return jnp.dot(own, right, preferred_element_type=jnp.float32) + got.astype(jnp.float32)


def over_chips(value):
    dp = lax.axis_size("dp")
    groups = [[i for i in range(dp) if i % 2 == core] for core in range(2)]
    return lax.psum_scatter(
        value, "dp", scatter_dimension=0, axis_index_groups=groups, tiled=True
    )


def over_mp(value):
    steps = bits_of(lax.axis_size("mp"))
    rows, _, width = value.shape
    value = value.reshape((rows,) + (2,) * steps + (width,))
    for step in range(steps):
        value = halve(value, "mp", step, steps - step)
    return value


def over_mp_relative(blocks):
    blocks = list(blocks)
    for step in reversed(range(bits_of(len(blocks)))):
        size = 1 << step
        blocks = [
            blocks[j] + swap(blocks[j + size].astype(jnp.bfloat16), "mp", size).astype(jnp.float32)
            for j in range(size)
        ]
    return blocks[0]


def sum_steps():
    return [
        (name, 1 << step) for name in ("mp", "dp") for step in range(bits_of(lax.axis_size(name)))
    ]


def body(
    layer_input,
    out_cotangent,
    segment_ids,
    qkv_weight,
    out_weight,
    up_weight,
    down_weight,
    norm_gains,
    bias_rows,
    up_bias,
    qkv_moments,
    out_moments,
    up_moments,
    down_moments,
    gain_moments,
    bias_moments,
    up_bias_moments,
):
    mp = lax.axis_size("mp")
    me = lax.axis_index("mp")
    dp = lax.axis_size("dp")
    dp_me = lax.axis_index("dp")
    width = qkv_weight.shape[2]
    units = up_weight.shape[1]
    tokens, dim = layer_input.shape
    rows = tokens // mp
    pairs = width // PAIR
    heads_local = width // HEAD_DIM
    low = jnp.bfloat16
    block = min(512, tokens)
    column_start = me * width

    def relative(value, axis):
        shape = value.shape
        value = value.reshape(shape[:axis] + (mp, rows) + shape[axis + 1 :])
        parts = [pick(value, me ^ j, axis) for j in range(mp)]
        return jnp.concatenate(parts, axis=axis)

    qkv_low = qkv_weight.astype(low)
    by_pair = qkv_low.reshape(3, -1, pairs, PAIR).transpose(1, 2, 0, 3).reshape(-1, 3 * width)
    qkv_full = lax.all_gather(by_pair, "dp", axis=0, tiled=True)
    weight_set = jnp.concatenate(
        [up_weight.astype(low), down_weight.astype(low), out_weight.astype(low)], axis=1
    )
    inputs = relative(layer_input, 0)
    input_halves = core_halves(inputs.T)
    ids = relative(segment_ids.reshape(-1), 0)
    document = jnp.arange(PAIR, dtype=jnp.int32)
    same = ids[:, None] == document[None, :]
    key_marks = jnp.where(same | (document[None, :] > 2), 0.0, very_low).astype(low)
    query_marks = same.T.astype(low)
    head_bias = lax.dynamic_slice_in_dim(bias_rows[:2], column_start, width, 1)

    queries, queries_t, key_rows, keys_t, values_all, values_t = project(
        inputs, qkv_full, head_bias, key_marks
    )
    weight_set = after(weight_set, qkv_full, key_marks, query_marks, *input_halves)
    weights_all = lax.all_gather(weight_set, ("mp", "dp"), axis=0, tiled=True)
    weights_all = weights_all.reshape(mp, dim, -1)
    qkv_all = lax.all_gather(after(qkv_full, weights_all), "mp", axis=0, tiled=False)
    own_core = (dp_me & 1).astype(jnp.int32).reshape(1)

    calls = [(0, pairs - 1), (pairs - 1, 1)] if pairs > 1 else [(0, 1)]
    place = [(call, at) for call, (_, count) in enumerate(calls) for at in range(count)]
    saved, attended_rel, tops = [], [[] for _ in range(mp)], []
    for first, count in calls:
        probs, attended_t, attended, totals, maxima = attention_forward(
            key_rows, queries_t, query_marks, values_t, first, count, block
        )
        saved.append((probs, attended_t, totals))
        tops.append(maxima)
        for j in range(mp):
            piece = attended[j * rows : (j + 1) * rows]
            attended_rel[j].append(piece if j == 0 else swap(piece, "mp", j))
    head_max = jnp.max(jnp.concatenate(tops).reshape(heads_local, PAIR), axis=1)
    head_max = head_max * HEAD_DIM ** (-0.5)
    attended_all = jnp.concatenate([piece for parts in attended_rel for piece in parts], axis=1)

    out_rel = [pick(weights_all[:, :, 2 * units :], me ^ j, 0) for j in range(mp)]
    branch = times_transposed(attended_all, jnp.concatenate(out_rel, axis=1))
    summed = inputs[:rows].astype(jnp.float32) + branch + bias_rows[2]
    normed, first_norm_pull = jax.vjp(norm_rows, summed, norm_gains[0], bias_rows[4])
    normed_low = normed.astype(low)
    hidden_low, slope, ffn_out = feed_forward(
        normed_low, weights_all, up_bias[None], units
    )
    total = normed + ffn_out + bias_rows[3]
    result, second_norm_pull = jax.vjp(norm_rows, total, norm_gains[1], bias_rows[5])
    total_grad, second_gain_grad, second_shift_grad = second_norm_pull(
        out_cotangent.astype(jnp.float32)
    )
    total_low = total_grad.astype(low)
    total_low = after(total_low, qkv_all)
    up_bias_grad, feed_grad, sent, own = feed_back(
        own_core, dp, total_low, normed_low, weights_all, slope, hidden_low, units
    )
    feed_low = (own + swap(sent, "dp", 1).astype(jnp.float32)).astype(low)
    summed_grad, first_gain_grad, first_shift_grad = first_norm_pull(feed_grad + total_grad)
    summed_low = summed_grad.astype(low)
    grad_rel = [[None] * mp for _ in range(pairs)]
    for j in reversed(range(mp)):
        piece = jnp.dot(summed_low, out_rel[j], preferred_element_type=jnp.float32).astype(low)
        for pair in range(pairs):
            part = piece[:, pair * PAIR : (pair + 1) * PAIR]
            if j and pair:
                part = after(part, grad_rel[0][j])
            grad_rel[pair][j] = part if j == 0 else swap(part, "mp", j)
        summed_late = after(summed_low, piece) if j == mp - 1 else summed_late
    feed_part = over_chips(feed_low.reshape(-1, mp * units))
    out_part = core_first(core_halves(summed_late.T), attended_all)

    slot = lax.broadcasted_iota(jnp.int32, (dp * mp, heads_local), 0)
    slots = jnp.where(slot == dp_me * mp + me, head_max[None], 0.0)
    early = jnp.concatenate(
        [
            first_gain_grad,
            second_gain_grad,
            jnp.sum(summed_grad, axis=0),
            jnp.sum(total_grad, axis=0),
            first_shift_grad,
            second_shift_grad,
            up_bias_grad.reshape(-1),
            slots.reshape(-1),
        ]
    )
    waiting = sum_steps()

    def add_step(value, *others):
        name, mask = waiting.pop(0)
        value = after(value, *others)
        return value + swap(value, name, mask)

    early = add_step(early)
    halves_other, halves_own = input_halves
    own_rows, got_rows = [], [[] for _ in range(mp - 1)]
    sent_pieces, qkv_pieces, bias_pieces = [], [], []
    chains, chained = [], 0

    def own_piece(pair, *others):
        grads, got = sent_pieces[pair]
        own_part = jnp.dot(after(halves_own, *others), grads, preferred_element_type=jnp.float32)
        return own_part + got.astype(jnp.float32)

    grads_low = None
    for pair, (call, at) in enumerate(place):
        probs, attended_t, totals = saved[call]
        ready = [feed_low, out_part, early] if pair == 0 else [early, grads_low, *sending]
        if pair > 1:
            ready += [rows_of[pair - 2] for rows_of in got_rows] + [qkv_pieces[pair - 2]]
        if len(qkv_pieces) > chained:
            fresh = qkv_pieces[chained:]
            fresh = [out_part, *fresh] if chained == 0 else fresh
            chains.append((0, by_bits(jnp.concatenate(fresh, axis=1))))
            chained = len(qkv_pieces)
        moving = []
        for step, value in chains:
            if step == chip_steps():
                moving.append((step, value, None))
                continue
            sent, kept = halve_parts(value, "dp", step + 1, chip_steps() - 1 - step)
            sent = after(sent, grads_low)
            ready.append(sent)
            moving.append((step + 1, kept, swap(sent, "dp", 2 << step)))
        grad_parts = list(grad_rel[pair])
        if pair > 0:
            grad_parts[0] = after(grad_parts[0], grads_low)
        grad_now = after(jnp.concatenate(grad_parts, axis=0), *ready)
        if waiting:
            early = add_step(early, *([] if grads_low is None else [grads_low]))
        grads_low, head_sums = attention_backward(
            probs, grad_now, attended_t, totals, queries, values_all, keys_t, pair, at
        )
        bias_pieces.append(head_sums)
        if pair > 0:
            qkv_pieces.append(own_piece(pair - 1, grads_low))
        chains = [
            (step, kept if got is None else after(kept, grads_low) + got.astype(jnp.float32))
            for step, kept, got in moving
        ]
        own_rows.append(grads_low[:rows])
        sending = [grads_low[j * rows : (j + 1) * rows] for j in range(1, mp)]
        for j in range(1, mp):
            got_rows[j - 1].append(swap(sending[j - 1], "mp", j))
        sent = jnp.dot(halves_other, grads_low, preferred_element_type=jnp.float32).astype(low)
        sent_pieces.append((grads_low, swap(sent, "dp", 1)))
        sending.append(sent)
    qkv_pieces.append(own_piece(pairs - 1))
    while waiting:
        early = add_step(early)
    parts = feed_part.astype(jnp.float32).reshape(2, -1, mp, units)
    up_sum, down_sum = over_mp(parts[0]), over_mp(parts[1])
    gain_sum = early[: 2 * dim].reshape(2, dim)
    late_biases = early[2 * dim : 6 * dim].reshape(4, dim)
    unit_sum = early[6 * dim : 6 * dim + units * mp]
    group_max = jnp.max(early[6 * dim + units * mp :].reshape(dp, mp, heads_local), axis=0)
    local_max = pick(group_max, me, 0)

    input_grad = summed_grad + times_transposed(
        jnp.concatenate(own_rows, axis=1), qkv_full
    )
    last_parts = []
    for j in range(1, mp):
        others = pick(qkv_all, me ^ j, 0)
        parts = got_rows[j - 1]
        if pairs > 1:
            input_grad = input_grad + times_transposed(
                jnp.concatenate(parts[:-1], axis=1), others[:, : -3 * PAIR]
            )
        last_parts.append((parts[-1], others[:, -3 * PAIR :]))
    most_grad = input_grad
    for got, others in last_parts:
        input_grad = input_grad + times_transposed(got, others)
    fresh = qkv_pieces[chained:]
    fresh = [out_part, *fresh] if chained == 0 else fresh
    summing = by_bits(jnp.concatenate(fresh, axis=1))
    for step in range(chip_steps()):
        while chains and chains[-1][0] == step:
            summing = jnp.concatenate([chains.pop()[1], summing], axis=-1)
        summing = halve(summing, "dp", step + 1, chip_steps() - 1 - step)
        if step == 0:
            summing = after(summing, most_grad)
    summing = jnp.concatenate([value for _, value in chains] + [summing], axis=-1)
    out_sum = summing[:, : mp * width]
    qkv_sum = summing[:, mp * width :].reshape(-1, pairs, 3, PAIR)
    out_sum = over_mp_relative([out_sum[:, j * width : (j + 1) * width] for j in range(mp)])
    qkv_sum = qkv_sum.transpose(2, 0, 1, 3).reshape(3, -1, width)

    head_biases = lax.dynamic_update_slice_in_dim(
        jnp.zeros((2, width * mp), jnp.float32),
        jnp.concatenate(bias_pieces, axis=1),
        column_start,
        1,
    )
    for name, mask in sum_steps():
        head_biases = head_biases + swap(head_biases, name, mask)
    bias_sum = jnp.concatenate([head_biases, late_biases], axis=0)

    grad_scale = lax.rsqrt(jnp.float32(tokens * dp))
    step_value = jnp.float32(ADAM_STEP)
    new_qkv, next_qkv = adam_update(qkv_weight, qkv_moments, qkv_sum * grad_scale, step_value)
    new_out, next_out = adam_update(out_weight, out_moments, out_sum * grad_scale, step_value)
    new_up, next_up = adam_update(up_weight, up_moments, up_sum * grad_scale, step_value)
    new_down, next_down = adam_update(down_weight, down_moments, down_sum * grad_scale, step_value)
    new_gains, next_gains = adam_update(norm_gains, gain_moments, gain_sum * grad_scale, step_value)
    new_biases, next_biases = adam_update(
        bias_rows, bias_moments, bias_sum * grad_scale, step_value
    )
    new_up_bias, next_up_bias = adam_update(
        up_bias, up_bias_moments, unit_sum * grad_scale, step_value
    )
    factor = jnp.sqrt(clip_tau / jnp.maximum(local_max, clip_tau))
    column = jnp.repeat(factor, HEAD_DIM)
    scales = jnp.stack([column, column, jnp.ones_like(column)])[:, None, :]
    new_qkv = new_qkv * scales
    return (
        result.astype(jnp.bfloat16),
        input_grad,
        new_qkv,
        new_out,
        new_up,
        new_down,
        new_gains,
        new_biases,
        new_up_bias,
        next_qkv,
        next_out,
        next_up,
        next_down,
        next_gains,
        next_biases,
        next_up_bias,
    )


def solution(mesh):
    placed = (
        P("dp", None),
        P(("dp", "mp"), None),
        P("dp", None),
        P(None, "dp", "mp"),
        P("dp", "mp"),
        P("dp", "mp"),
        P("dp", "mp"),
        P(),
        P(),
        P(),
        P(None, None, "dp", "mp"),
        P(None, "dp", "mp"),
        P(None, "dp", "mp"),
        P(None, "dp", "mp"),
        P(),
        P(),
        P(),
    )
    return jax.shard_map(
        body,
        mesh=mesh,
        in_specs=placed,
        out_specs=(
            P(("dp", "mp"), None),
            P(("dp", "mp"), None),
            P(None, "dp", "mp"),
            P("dp", "mp"),
            P("dp", "mp"),
            P("dp", "mp"),
            P(),
            P(),
            P(),
            P(None, None, "dp", "mp"),
            P(None, "dp", "mp"),
            P(None, "dp", "mp"),
            P(None, "dp", "mp"),
            P(),
            P(),
            P(),
        ),
        check_vma=False,
    )
```

time: 2890 us -> 779 us (0.27)
  matrix products: 1200 us -> 65.3 us
  waiting for transfers between devices: 975 us -> 50.7 us
  Pallas kernels: 0 us -> 439 us
  other arithmetic: 494 us -> 89 us
  blocking collectives: 73.2 us -> 0 us
  starting transfers between devices: 0.63 us -> 30.4 us
    dot_general x51 -> x12, matrix products: 1150 us -> 37.9 us  [the longest x4 13.8 us: body(): jnp.dot(halves_other, grads_low, preferred_element_type=jnp.float32)]
    reduce_scatter x7 -> x1, waiting for transfers between devices: 635 us -> 0.01 us  [over_chips(): lax.psum_scatter(value, 'dp', scatter_dimension=0, axis_index_groups=grou...]
    pallas_call x0 -> x9, Pallas kernels: none -> 439 us  [the longest x4 184 us: attention_backward(): pl.pallas_call(functools.partial(backward_kernel, bq, ch, tokens), grid=(...]
    all_gather x7 -> x3, waiting for transfers between devices: 281 us -> 10.5 us  [the longest x1 10.5 us: body(): qkv_full = lax.all_gather(by_pair, 'dp', axis=0, tiled=True)]
    convert_element_type x14 -> x10, other arithmetic: 265 us -> 17.6 us  [the longest x1 8.01 us: body(): feed_low = (own + swap(sent, 'dp', 1).astype(jnp.float32)).astype(low)]
    reduce_max x7 -> x2, other arithmetic: 140 us -> 0.12 us  [the longest x1 0.09 us: body(): head_max = jnp.max(jnp.concatenate(tops).reshape(heads_local, PAIR), axis=1)]
    unnamed x16 -> x4, waiting for transfers between devices: 58.8 us -> 0.07 us
    ppermute x0 -> x35, waiting for transfers between devices: none -> 40.2 us  [swap(): return lax.ppermute(value, axis_name, [(i, i ^ mask) for i in range(size)])]
  transfers between devices with their start and end apart: 15 -> 39, of which waited for: 11 -> 11; matrix products, arithmetic and copies ran while one was open for 57% -> 29% of each run, Pallas kernels for 0% -> 49%
where the time goes in v2:
time: 779 us; the launch traced here: 773 us
  Pallas kernels  439 us (56%)
  other arithmetic  89 us (11%)
  local copies, waits for them, and re-layouts  83.9 us (11%)
  matrix products  65.3 us (8%)
  waiting for transfers between devices  50.7 us (7%)
  starting transfers between devices  30.4 us (4%)
  between operations  15.4 us (2%)
    pallas_call x4, Pallas kernels, attention_backward(): pl.pallas_call(functools.partial(backward_kernel, bq, ch, tokens), grid=(...  184 us
    pallas_call x2, Pallas kernels, attention_forward(): pl.pallas_call(functools.partial(forward_kernel, bq, ch, tokens), grid=(c...  126 us
    pallas_call x1, Pallas kernels, feed_back(): pl.pallas_call(functools.partial(feed_back_kernel, rows, ch, blocks), gri...  62.1 us
    pallas_call x1, Pallas kernels, feed_forward(): pl.pallas_call(functools.partial(feed_kernel, rows, ch), grid=(groups * p...  47.5 us
    ppermute x35, waiting for transfers between devices, swap(): return lax.ppermute(value, axis_name, [(i, i ^ mask) for i in range(size)])  40.2 us
    ppermute x35, starting transfers between devices, swap(): return lax.ppermute(value, axis_name, [(i, i ^ mask) for i in range(size)])  29.9 us
    dot_general x4, matrix products, times_transposed(): lax.dot_general(left_side, right_side, (((1,), (1,)), ((), ())), preferre...  27.3 us
    pallas_call x1, Pallas kernels, project(): pl.pallas_call(functools.partial(project_kernel, pairs), grid=(tokens //...  19.4 us
  transfers between devices with their start and end apart: 39, of which 11 were waited for; matrix products, arithmetic and copies ran while one was open for 29% of the time, Pallas kernels for 49%

profile of v2, /device:TPU:0, one launch (start us, length us, event | category | flops | bytes accessed | tf_op | source)
XLA Modules:
  0.0 773.2 jit_solution(8294855795579124893)
XLA Ops:
  14.1 5.2 dynamic-slice_bitcast_fusion.1
  19.4 9.7 %pad_maximum_fusion = (bf16[3072,1024]{1,0:T(8,128)(2,1)}, bf16[1024,3072]{0,1:T(8,128)(2,1)}) fusion(bf16[1536,1024]{1,0:T(8,128)(2,1)} %get-tuple-element.191, bf16[1536,1024]{1,0:T(8,128)(2,1)S(1)} %get-tuple-element.192), kind=kLoop, calls=%fused_computation.10 | loop fusion | flops 12582912 | bytes 18874368 | tf_op jit(solution)/shard_map/concatenate | solution.py:602
  29.1 8.6 %copy.70 = bf16[1024,3072]{1,0:T(8,128)(2,1)} copy(bf16[1024,3072]{0,1:T(8,128)(2,1)} %get-tuple-element.188) | data formatting | bytes 12582912 | tf_op jit(solution)/shard_map/transpose | solution.py:611
  37.8 6.5 constant_dynamic-slice_fusion.13
  46.2 2.1 select_convert_fusion.marks
  48.3 10.5 %all-gather.5.cloned.1.call-done.weights = bf16[1024,1536]{1,0:T(8,128)(2,1)} async-done(((bf16[64,1536]{1,0:T(8,128)(2,1)}), bf16[1024,1536]{1,0:T(8,128)(2,1)}) %all-gather.5.cloned.1.call-update) | async-done | bytes 3145744 | tf_op jit(solution)/shard_map/all_gather | solution.py:606
  60.4 19.4 %project.1 = (bf16[3072,512]{1,0:T(8,128)(2,1)}, bf16[512,3072]{1,0:T(8,128)(2,1)}, bf16[4,3072,256]{2,1,0:T(8,128)(2,1)}, bf16[512,3072]{1,0:T(8,128)(2,1)}, bf...) custom-call(bf16[3072,1024]{1,0:T(8,128)(2,1)} %get-tuple-element.187.x, ...), custom_call_target="tpu_custom_call" | custom-call | flops 603979776 | bytes 1048576 | tf_op jit(solution)/shard_map/project/pallas_call | solution.py:91
  79.8 90.7 %attend.2 = (bf16[3,2,6,3072,512]{4,3,2,1,0:T(8,128)(2,1)}, f32[384,3072]{1,0:T(8,128)}, bf16[3072,384]{1,0:T(8,128)(2,1)}, f32[3,2,3072]{2,1,0:T(2,128)}, f32[3,2,128]{2,1,0:T(2,128)}) custom-call(bf16[4,3072,256]{2,1,0:T(8,128)(2,1)} %get-tuple-element.74.k_cur.k_nxt, bf16[4,3072,256]{2,1,0:T(8,128)(2,1)} %get-tuple-element.74.k_cur.k_nxt, ...), custom_call_target="tpu_custom_call" | custom-call | flops 3623878656 | bytes 1048576 | tf_op jit(solution)/shard_map/attend/pallas_call | solution.py:198
  170.6 3.2 fusion.97
  175.3 35.1 %attend.3 = (bf16[1,2,6,3072,512]{4,3,2,1,0:T(8,128)(2,1)}, f32[128,3072]{1,0:T(8,128)}, bf16[3072,128]{1,0:T(8,128)(2,1)}, f32[1,2,3072]{2,1,0:T(2,128)}, f32[1,2,128]{2,1,0:T(2,128)}) custom-call(bf16[4,3072,256]{2,1,0:T(8,128)(2,1)} %get-tuple-element.74.k_cur.k_nxt, bf16[4,3072,256]{2,1,0:T(8,128)(2,1)} %get-tuple-element.74.k_cur.k_nxt, ...), custom_call_target="tpu_custom_call" | custom-call | flops 1207959552 | bytes 1048576 | tf_op jit(solution)/shard_map/attend/pallas_call | solution.py:198
  210.4 1.9 fusion.101
  215.5 3.0 slice.230
  220.5 3.0 collective-permute-done.1
  223.5 5.7 fusion.105
  230.1 1.9 copy-done
  232.0 2.6 fusion.4.x.normed
  234.5 47.5 %feed.1 = (bf16[1536,4096]{1,0:T(8,128)(2,1)}, bf16[1536,4096]{1,0:T(8,128)(2,1)}, f32[1536,1024]{1,0:T(8,128)}) custom-call(bf16[1536,1024]{1,0:T(8,128)(2,1)} %fusion.4.x.normed, bf16[2,1024,4608]{2,1,0:T(8,128)(2,1)} %bitcast.255, bf16[2,1024,4608]{2,1,0:T(8,128)(2,1)} %bitcast.256, f32[1,4096]{1,0:T(1,128)} %bitcast.299), custom_call_target="tpu_custom_call" | custom-call | flops 1610612736 | bytes 1048576 | tf_op jit(solution)/shard_map/feed/pallas_call | solution.py:378
  282.1 5.9 fusion.92
  289.9 3.3 fusion.3
  293.1 4.3 fusion.91
  297.4 2.6 copy-done.1
  300.0 2.2 add_reduce_fusion.1
  302.3 62.1 %feed_back.1 = (f32[1,4096]{1,0:T(1,128)}, f32[1536,1024]{1,0:T(8,128)}, bf16[8,2,64,4096]{3,2,1,0:T(8,128)(2,1)}, f32[8,2,64,4096]{3,2,1,0:T(8,128)}) custom-call(s32[1]{0:T(128)} %bitcast.18.core, bf16[1536,1024]{1,0:T(8,128)(2,1)} %get-tuple-element.82.x, bf16[1536,1024]{1,0:T(8,128)(2,1)} %fusion.4.x.normed, bf16[2,1024,4608]{2,1,0:T(8,128)(2,1)} %bitcast.257, ...), custom_call_target="tpu_custom_call" | custom-call | flops 3221225472 | bytes 1048576 | tf_op jit(solution)/shard_map/feed_back/pallas_call | solution.py:453
  365.5 8.1 %multiply_reduce_fusion = (f32[1024]{0:T(1024)S(1)}, f32[1536]{0:T(1024)S(1)}, f32[1024]{0:T(1024)S(1)}, f32[1536,1024]{1,0:T(8,128)S(1)}) fusion(f32[1536,1024]{1,0:T(8,128)} %copy-done, f32[1536]{0:T(1024)S(1)} %fusion.71, f32[1536]{0:T(1024)S(1)} %broadcast_multiply_fusion.1, f32[1024]{0:T(1024)S(1)} %bitcast.296, f32[1536,1024]{1,0:T(8,128)} %get-tuple-element.85, ...), kind=kLoop, calls=%fused_computation.12 | loop fusion | flops 15725056 | bytes 25202688 | tf_op jit(solution)/shard_map/transpose(jvp())/reduce_sum | solution.py:28
  374.8 3.0 fusion.90
  378.5 2.0 copy-done.2
  389.0 2.9 copy.72
  392.0 2.2 constant_dynamic-slice_fusion.12
  394.2 3.8 convolution_convert_fusion.2
  402.4 1.9 dynamic-slice_bitcast_fusion
  407.5 1.9 pad_maximum_fusion.6.grad
  409.5 4.7 convert_add_fusion
  414.2 8.0 %add_convert_fusion = bf16[8,2,64,4096]{3,2,1,0:T(8,128)(2,1)} fusion(f32[8,2,64,4096]{3,2,1,0:T(8,128)S(1)} %bitcast.266, bf16[8,2,64,4096]{3,2,1,0:T(8,128)(2,1)} %collective-permute-done.3), kind=kLoop, calls=%fused_computation | loop fusion | flops 12582912 | bytes 33554432 | tf_op jit(solution)/shard_map/convert_element_type | solution.py:662
  422.2 45.9 %attend_back.4 = (bf16[3072,384]{1,0:T(8,128)(2,1)}, f32[2,128]{1,0:T(2,128)}) custom-call(bf16[3,2,6,3072,512]{4,3,2,1,0:T(8,128)(2,1)} %get-tuple-element.86.p_ref, bf16[3072,128]{1,0:T(8,128)(2,1)} %pad_maximum_fusion.6.grad, f32[384,3072]{1,0:T(8,128)} %get-tuple-element.94.out_t, f32[3,2,3072]{2,1,0:T(2,128)} %get-tuple-element.95.totals, ...), custom_call_target="tpu_custom_call" | custom-call | flops 2415919104 | bytes 1048576 | tf_op jit(solution)/shard_map/attend_back/pallas_call | solution.py:301
  468.1 4.3 convolution_convert_fusion.6
  476.8 45.8 %attend_back.5 = (bf16[3072,384]{1,0:T(8,128)(2,1)}, f32[2,128]{1,0:T(2,128)}) custom-call(bf16[3,2,6,3072,512]{4,3,2,1,0:T(8,128)(2,1)} %get-tuple-element.86.p_ref, bf16[3072,128]{1,0:T(8,128)(2,1)} %pad_maximum_fusion.7.grad, f32[384,3072]{1,0:T(8,128)} %get-tuple-element.94.out_t, f32[3,2,3072]{2,1,0:T(2,128)} %get-tuple-element.95.totals, ...), custom_call_target="tpu_custom_call" | custom-call | flops 2415919104 | bytes 1048576 | tf_op jit(solution)/shard_map/attend_back/pallas_call | solution.py:301
  522.6 3.6 fusion.95
  526.1 4.4 convolution_convert_fusion.5
  530.7 1.9 pad_maximum_fusion.8.grad
  533.4 1.9 collective-permute-start.13
  535.3 5.8 collective-permute-done.13
  542.2 1.9 convert_add_fusion.5
  546.7 46.3 %attend_back.6 = (bf16[3072,384]{1,0:T(8,128)(2,1)}, f32[2,128]{1,0:T(2,128)}) custom-call(bf16[3,2,6,3072,512]{4,3,2,1,0:T(8,128)(2,1)} %get-tuple-element.86.p_ref, bf16[3072,128]{1,0:T(8,128)(2,1)} %pad_maximum_fusion.8.grad, f32[384,3072]{1,0:T(8,128)} %get-tuple-element.94.out_t, f32[3,2,3072]{2,1,0:T(2,128)} %get-tuple-element.95.totals, ...), custom_call_target="tpu_custom_call" | custom-call | flops 2415919104 | bytes 1048576 | tf_op jit(solution)/shard_map/attend_back/pallas_call | solution.py:301
  593.1 3.5 convert_add_fusion.4
  597.9 2.0 convert_add_fusion.1
  600.7 1.9 pad_maximum_fusion.9.grad
  602.7 2.6 convolution_convert_fusion.4
  606.5 45.7 %attend_back.7 = (bf16[3072,384]{1,0:T(8,128)(2,1)}, f32[2,128]{1,0:T(2,128)}) custom-call(bf16[1,2,6,3072,512]{4,3,2,1,0:T(8,128)(2,1)} %get-tuple-element.111.p_ref, bf16[3072,128]{1,0:T(8,128)(2,1)} %pad_maximum_fusion.9.grad, f32[128,3072]{1,0:T(8,128)} %get-tuple-element.120.out_t, f32[1,2,3072]{2,1,0:T(2,128)} %get-tuple-element.121.totals, ...), custom_call_target="tpu_custom_call" | custom-call | flops 2415919104 | bytes 1048576 | tf_op jit(solution)/shard_map/attend_back/pallas_call | solution.py:301
  656.8 2.9 fusion.93
  660.5 2.5 convolution_convert_fusion.3
  663.0 3.8 collective-permute-start.26
  667.0 7.1 fusion.5
  676.3 2.5 collective-permute-done.34
  684.8 3.7 convert_add_fusion.3
  688.6 3.0 convert_add_fusion.2
  695.2 7.8 %collective-permute-done.23 = bf16[2,2,64,768]{3,2,0,1:T(8,128)(2,1)S(1)} collective-permute-done((bf16[2,2,64,768]{3,2,0,1:T(8,128)(2,1)S(1)}, bf16[2,2,64,768]{3,2,0,1:T(8,128)(2,1)S(1)}, u32[]{:S(2)}, u32[]{:S(2)}) %collective-permute-start.23) | collective-permute-done | bytes 393248 | tf_op jit(solution)/shard_map/ppermute | solution.py:488
  703.1 4.9 collective-permute-done.17
  708.1 8.6 %add_add_fusion.2 = f32[1536,1024]{1,0:T(8,128)S(1)} fusion(f32[1536,1024]{1,0:T(8,128)} %fusion.5, f32[1536,1024]{1,0:T(8,128)S(1)} %bitcast.264, bf16[1536,384]{1,0:T(8,128)(2,1)} %collective-permute-done.17, bf16[1536,384]{1,0:T(8,128)(2,1)} %collective-permute-done.14, bf16[1536,384]{1,0:T(8,128)(2,1)} %collective-permute-done.10, ...), kind=kOutput, calls=%fused_computation.11 | convolution fusion | flops 3639214080 | bytes 24780800 | tf_op jit(solution)/shard_map/dot_general | solution.py:32
  716.7 2.1 collective-permute-start.24
  719.8 6.0 collective-permute-done.24
  726.1 5.0 collective-permute-done.18
  731.1 5.9 convolution_add_fusion
  757.0 3.6 collective-permute-done.29
  760.6 2.3 fusion.85
  (359 shorter events, 92.9 us)
Async XLA Ops:
  7.2 51.6 %all-gather.5.cloned.1.call-start = ((), (), s32[]{:S(2)}) async-start(), calls=%async_computation.1 | async-start | bytes 3342336 | tf_op jit(solution)/shard_map/all_gather | solution.py:606
  9.4 206.1 %all-gather.7.cloned.1.call-start = ((), (), s32[]{:S(2)}) async-start(), calls=%async_computation.2 | async-start | bytes 19464192 | tf_op jit(solution)/shard_map/all_gather | solution.py:623
  44.3 14.9 %slice-start.10 = ((f32[6,1024]{1,0:T(8,128)}), f32[2,1024]{1,0:T(2,128)S(1)}, s32[]{:S(2)}) async-start(f32[6,1024]{1,0:T(8,128)} %param.25), calls=%async_computation.15 | async-start | bytes 16384 | tf_op jit(solution)/shard_map/slice | solution.py:617
  44.3 15.5 %copy-start.53 = (f32[2,4096]{1,0:T(2,128)S(1)}, f32[2,4096]{1,0:T(2,128)}, u32[]{:S(2)}) copy-start(f32[2,4096]{1,0:T(2,128)} %param.33) | copy-start | bytes 98308
  58.8 243.4 %all-gather.9.cloned.1.call-start = ((), (), s32[]{:S(2)}) async-start(), calls=%async_computation.4 | async-start | bytes 9437184 | tf_op jit(solution)/shard_map/all_gather | solution.py:625
  173.8 49.6 %collective-permute-start = (bf16[1536,384]{1,0:T(8,128)(2,1)}, bf16[1536,384]{1,0:T(8,128)(2,1)}, u32[]{:S(2)}, u32[]{:S(2)}) collective-permute-start(bf16[1536,384]{1,0:T(8,128)(2,1)} %get-tuple-element.204), channel_id=1, source_target_pairs={{0,1},{1,0},{2,3},{3,2},{4,5},{5,4},{6,7},{7,6},{8,9},{9,8},{10,11... | collective-permute-start | bytes 3538952 | tf_op jit(solution)/shard_map/ppermute | solution.py:488
  212.3 11.2 %collective-permute-start.1 = (bf16[1536,128]{1,0:T(8,128)(2,1)}, bf16[1536,128]{1,0:T(8,128)(2,1)}, u32[]{:S(2)}, u32[]{:S(2)}) collective-permute-start(bf16[1536,128]{1,0:T(8,128)(2,1)} %get-tuple-element.229), channel_id=1, source_target_pairs={{0,1},{1,0},{2,3},{3,2},{4,5},{5,4},{6,7},{7,6},{8,9},{9,8},{10,11... | collective-permute-start | bytes 1179656 | tf_op jit(solution)/shard_map/ppermute | solution.py:488
  218.6 529.8 %reduce-scatter.2.cloned.1.call-start = ((), (), s32[]{:S(2)}) async-start(), calls=%async_computation.3 | async-start | bytes 9437184 | tf_op jit(solution)/shard_map/reduce_scatter | solution.py:534
  234.5 47.5 %copy-start.56 = (f32[1,1024]{1,0:T(1,128)S(1)}, f32[1,1024]{1,0:T(1,128)}, u32[]{:S(2)}) copy-start(f32[1,1024]{1,0:T(1,128)} %get-tuple-element.240) | copy-start | bytes 12292
  302.3 62.2 %copy-start.50 = (f32[2,6,1024]{2,0,1:T(2,128)S(1)}, f32[2,6,1024]{2,0,1:T(2,128)}, u32[]{:S(2)}) copy-start(f32[2,6,1024]{2,0,1:T(2,128)} %param.32) | copy-start | bytes 147460
  302.3 62.8 %copy-start.58 = (f32[3,2,128]{2,1,0:T(2,128)S(1)}, f32[3,2,128]{2,1,0:T(2,128)}, u32[]{:S(2)}) copy-start(f32[3,2,128]{2,1,0:T(2,128)} %get-tuple-element.91) | copy-start | bytes 9220
  302.3 62.8 %copy-start.62 = (f32[1,2,128]{2,1,0:T(2,128)S(1)}, f32[1,2,128]{2,1,0:T(2,128)}, u32[]{:S(2)}) copy-start(f32[1,2,128]{2,1,0:T(2,128)} %get-tuple-element.92) | copy-start | bytes 3076
  302.3 63.0 %copy-start.63 = (pred[32]{0:T(512)(128)(4,1)S(1)}, pred[32]{0:T(512)(128)(4,1)}, u32[]{:S(2)}) copy-start(pred[32]{0:T(512)(128)(4,1)} %iota_compare_fusion.2) | copy-start | bytes 100
  364.4 49.7 %collective-permute-start.3 = (bf16[8,2,64,4096]{3,2,1,0:T(8,128)(2,1)}, bf16[8,2,64,4096]{3,2,1,0:T(8,128)(2,1)}, u32[]{:S(2)}, u32[]{:S(2)}) collective-permute-start(bf16[8,2,64,4096]{3,2,1,0:T(8,128)(2,1)} %get-tuple-element.88), channel_id=1, source_target_pairs={{0,2},{2,0},{4,6},{6,4},{8,10},{10,8},{12,14},{14,12},{16,18},{18,... | collective-permute-start | bytes 25165832 | tf_op jit(solution)/shard_map/ppermute | solution.py:488
  384.0 17.0 %collective-permute-start.5 = (f32[10496]{0:T(1024)}, f32[10496]{0:T(1024)}, u32[]{:S(2)}, u32[]{:S(2)}) collective-permute-start(f32[10496]{0:T(1024)} %constant_dynamic-update-slice_fusion.7), channel_id=1, source_target_pairs={{0,1},{1,0},{2,3},{3,2},{4,5},{5,4},{6,7},{7,6},{8,9},{9,8},{10,11... | collective-permute-start | bytes 125960 | tf_op jit(solution)/shard_map/ppermute | solution.py:488
  387.5 17.5 %collective-permute-start.2 = (bf16[1536,128]{1,0:T(8,128)(2,1)}, bf16[1536,128]{1,0:T(8,128)(2,1)}, u32[]{:S(2)}, u32[]{:S(2)}) collective-permute-start(bf16[1536,128]{1,0:T(8,128)(2,1)} %get-tuple-element.220), channel_id=1, source_target_pairs={{0,1},{1,0},{2,3},{3,2},{4,5},{5,4},{6,7},{7,6},{8,9},{9,8},{10,11... | collective-permute-start | bytes 1179656 | tf_op jit(solution)/shard_map/ppermute | solution.py:488
  398.0 11.4 %collective-permute-start.4 = (bf16[512,1024]{1,0:T(8,128)(2,1)S(1)}, bf16[512,1024]{1,0:T(8,128)(2,1)S(1)}, u32[]{:S(2)}, u32[]{:S(2)}) collective-permute-start(bf16[512,1024]{1,0:T(8,128)(2,1)S(1)} %convolution_convert_fusion.2), channel_id=1, source_target_pairs={{0,2},{2,0},{4,6},{6,4},{8,10},{10,8},{12,14},{14,12},{16,18},{18,... | collective-permute-start | bytes 3145736 | tf_op jit(solution)/shard_map/ppermute | solution.py:488
  398.1 16.1 %slice-start.4 = ((s8[16777216]{0:T(1024)(128)(4,1)}), s8[4194304]{0:T(1024)(128)(4,1)S(1)}, s32[]{:S(2)}) async-start(s8[16777216]{0:T(1024)(128)(4,1)} %bitcast.265), calls=%async_computation.9 | async-start | bytes 8388608
  398.1 16.1 %slice-start.5 = ((s8[16777216]{0:T(1024)(128)(4,1)}), s8[4194304]{0:T(1024)(128)(4,1)S(1)}, s32[]{:S(2)}) async-start(s8[16777216]{0:T(1024)(128)(4,1)} %bitcast.265), calls=%async_computation.10 | async-start | bytes 8388608
  401.9 2.4 collective-permute-start.7
  405.0 69.8 %collective-permute-start.6 = (bf16[1536,128]{1,0:T(8,128)(2,1)S(1)}, bf16[1536,128]{1,0:T(8,128)(2,1)S(1)}, u32[]{:S(2)}, u32[]{:S(2)}) collective-permute-start(bf16[1536,128]{1,0:T(8,128)(2,1)S(1)} %get-tuple-element.101), channel_id=1, source_target_pairs={{0,1},{1,0},{2,3},{3,2},{4,5},{5,4},{6,7},{7,6},{8,9},{9,8},{10,11... | collective-permute-start | bytes 1179656 | tf_op jit(solution)/shard_map/ppermute | solution.py:488
  405.5 125.0 %collective-permute-start.8 = (bf16[1536,128]{1,0:T(8,128)(2,1)}, bf16[1536,128]{1,0:T(8,128)(2,1)}, u32[]{:S(2)}, u32[]{:S(2)}) collective-permute-start(bf16[1536,128]{1,0:T(8,128)(2,1)} %get-tuple-element.105), channel_id=1, source_target_pairs={{0,1},{1,0},{2,3},{3,2},{4,5},{5,4},{6,7},{7,6},{8,9},{9,8},{10,11... | collective-permute-start | bytes 1179656 | tf_op jit(solution)/shard_map/ppermute | solution.py:488
  407.0 193.7 %collective-permute-start.12 = (bf16[1536,128]{1,0:T(8,128)(2,1)}, bf16[1536,128]{1,0:T(8,128)(2,1)}, u32[]{:S(2)}, u32[]{:S(2)}) collective-permute-start(bf16[1536,128]{1,0:T(8,128)(2,1)} %get-tuple-element.113), channel_id=1, source_target_pairs={{0,1},{1,0},{2,3},{3,2},{4,5},{5,4},{6,7},{7,6},{8,9},{9,8},{10,11... | collective-permute-start | bytes 1179656 | tf_op jit(solution)/shard_map/ppermute | solution.py:488
  422.2 45.9 %copy-start.7 = (bf16[8,1,64,3072]{3,2,1,0:T(8,128)(2,1)S(1)}, bf16[8,1,64,3072]{3,2,1,0:T(8,128)(2,1)}, u32[]{:S(2)}) copy-start(bf16[8,1,64,3072]{3,2,1,0:T(8,128)(2,1)} %get-tuple-element.190) | copy-start | bytes 9437188
  472.5 60.1 %collective-permute-start.9 = (f32[10496]{0:T(1024)}, f32[10496]{0:T(1024)S(1)}, u32[]{:S(2)}, u32[]{:S(2)}) collective-permute-start(f32[10496]{0:T(1024)} %add.377), channel_id=1, source_target_pairs={{0,4},{2,6},{4,0},{6,2},{8,12},{10,14},{12,8},{14,10},{16,20},{18,... | collective-permute-start | bytes 125960 | tf_op jit(solution)/shard_map/ppermute | solution.py:488
  473.5 68.7 %collective-permute-start.11 = (bf16[512,384]{1,0:T(8,128)(2,1)}, bf16[512,384]{1,0:T(8,128)(2,1)S(1)}, u32[]{:S(2)}, u32[]{:S(2)}) collective-permute-start(bf16[512,384]{1,0:T(8,128)(2,1)} %convolution_convert_fusion.6), channel_id=1, source_target_pairs={{0,2},{2,0},{4,6},{6,4},{8,10},{10,8},{12,14},{14,12},{16,18},{18,... | collective-permute-start | bytes 1179656 | tf_op jit(solution)/shard_map/ppermute | solution.py:488
  474.7 72.0 %collective-permute-start.10 = (bf16[1536,384]{1,0:T(8,128)(2,1)S(1)}, bf16[1536,384]{1,0:T(8,128)(2,1)}, u32[]{:S(2)}, u32[]{:S(2)}) collective-permute-start(bf16[1536,384]{1,0:T(8,128)(2,1)S(1)} %get-tuple-element.198), channel_id=1, source_target_pairs={{0,1},{1,0},{2,3},{3,2},{4,5},{5,4},{6,7},{7,6},{8,9},{9,8},{10,11... | collective-permute-start | bytes 3538952 | tf_op jit(solution)/shard_map/ppermute | solution.py:488
  526.1 16.0 %copy-start.6 = (bf16[8,1,64,3072]{3,2,1,0:T(8,128)(2,1)S(1)}, bf16[8,1,64,3072]{3,2,1,0:T(8,128)(2,1)}, u32[]{:S(2)}) copy-start(bf16[8,1,64,3072]{3,2,1,0:T(8,128)(2,1)} %get-tuple-element.189) | copy-start | bytes 9437188
  526.1 16.0 %copy-start.17 = (bf16[3072,384]{1,0:T(8,128)(2,1)S(1)}, bf16[3072,384]{1,0:T(8,128)(2,1)}, u32[]{:S(2)}) copy-start(bf16[3072,384]{1,0:T(8,128)(2,1)} %get-tuple-element.99) | copy-start | bytes 7077892
  530.5 62.5 %collective-permute-start.15 = (bf16[512,384]{1,0:T(8,128)(2,1)}, bf16[512,384]{1,0:T(8,128)(2,1)}, u32[]{:S(2)}, u32[]{:S(2)}) collective-permute-start(bf16[512,384]{1,0:T(8,128)(2,1)} %convolution_convert_fusion.5), channel_id=1, source_target_pairs={{0,2},{2,0},{4,6},{6,4},{8,10},{10,8},{12,14},{14,12},{16,18},{18,... | collective-permute-start | bytes 1179656 | tf_op jit(solution)/shard_map/ppermute | solution.py:488
  533.4 7.7 collective-permute-start.13
  541.2 65.3 %collective-permute-start.14 = (bf16[1536,384]{1,0:T(8,128)(2,1)}, bf16[1536,384]{1,0:T(8,128)(2,1)}, u32[]{:S(2)}, u32[]{:S(2)}) collective-permute-start(bf16[1536,384]{1,0:T(8,128)(2,1)} %get-tuple-element.200), channel_id=1, source_target_pairs={{0,1},{1,0},{2,3},{3,2},{4,5},{5,4},{6,7},{7,6},{8,9},{9,8},{10,11... | collective-permute-start | bytes 3538952 | tf_op jit(solution)/shard_map/ppermute | solution.py:488
  545.2 52.7 %collective-permute-start.16 = (bf16[2,2,64,1408]{3,2,0,1:T(8,128)(2,1)}, bf16[2,2,64,1408]{3,2,0,1:T(8,128)(2,1)}, u32[]{:S(2)}, u32[]{:S(2)}) collective-permute-start(bf16[2,2,64,1408]{3,2,0,1:T(8,128)(2,1)} %fusion.25), channel_id=1, source_target_pairs={{0,4},{2,6},{4,0},{6,2},{8,12},{10,14},{12,8},{14,10},{16,20},{18,... | collective-permute-start | bytes 2162696 | tf_op jit(solution)/shard_map/ppermute | solution.py:488
  597.3 96.9 %collective-permute-start.20 = (bf16[2,2,64,384]{3,2,0,1:T(8,128)(2,1)}, bf16[2,2,64,384]{3,2,0,1:T(8,128)(2,1)}, u32[]{:S(2)}, u32[]{:S(2)}) collective-permute-start(bf16[2,2,64,384]{3,2,0,1:T(8,128)(2,1)} %fusion.51), channel_id=1, source_target_pairs={{0,4},{2,6},{4,0},{6,2},{8,12},{10,14},{12,8},{14,10},{16,20},{18,... | collective-permute-start | bytes 589832 | tf_op jit(solution)/shard_map/ppermute | solution.py:488
  600.7 118.0 %collective-permute-start.19 = (bf16[2,64,1408]{2,1,0:T(8,128)(2,1)}, bf16[2,64,1408]{2,1,0:T(8,128)(2,1)}, u32[]{:S(2)}, u32[]{:S(2)}) collective-permute-start(bf16[2,64,1408]{2,1,0:T(8,128)(2,1)} %fusion.46), channel_id=1, source_target_pairs={{0,8},{2,10},{4,12},{6,14},{8,0},{10,2},{12,4},{14,6},{16,24},{18,... | collective-permute-start | bytes 1081352 | tf_op jit(solution)/shard_map/ppermute | solution.py:488
  653.1 3.7 collective-permute-start.30
  656.0 27.6 %collective-permute-start.21 = (bf16[512,384]{1,0:T(8,128)(2,1)}, bf16[512,384]{1,0:T(8,128)(2,1)}, u32[]{:S(2)}, u32[]{:S(2)}) collective-permute-start(bf16[512,384]{1,0:T(8,128)(2,1)} %convolution_convert_fusion.4), channel_id=1, source_target_pairs={{0,2},{2,0},{4,6},{6,4},{8,10},{10,8},{12,14},{14,12},{16,18},{18,... | collective-permute-start | bytes 1179656 | tf_op jit(solution)/shard_map/ppermute | solution.py:488
  656.8 2.9 collective-permute-start.31
  659.7 7.1 collective-permute-start.32
  663.0 16.6 %collective-permute-start.26 = (f32[10496]{0:T(1024)S(1)}, f32[10496]{0:T(1024)S(1)}, u32[]{:S(2)}, u32[]{:S(2)}) collective-permute-start(f32[10496]{0:T(1024)S(1)} %add.381), channel_id=1, source_target_pairs={{0,16},{2,18},{4,20},{6,22},{8,24},{10,26},{12,28},{14,30},{16,0},... | collective-permute-start | bytes 125960 | tf_op jit(solution)/shard_map/ppermute | solution.py:488
  666.8 7.3 collective-permute-start.33
  666.9 12.8 %copy-start.46 = (f32[4096]{0:T(1024)S(1)}, f32[4096]{0:T(1024)}, u32[]{:S(2)}) copy-start(f32[4096]{0:T(1024)} %param.26) | copy-start | bytes 49156
  666.9 12.8 %copy-start.48 = (f32[1,4096]{1,0:T(1,128)S(1)}, f32[1,4096]{1,0:T(1,128)}, u32[]{:S(2)}) copy-start(f32[1,4096]{1,0:T(1,128)} %get-tuple-element.237) | copy-start | bytes 49156
  667.0 12.8 %copy-start.49 = (f32[1,4096]{1,0:T(1,128)S(1)}, f32[1,4096]{1,0:T(1,128)}, u32[]{:S(2)}) copy-start(f32[1,4096]{1,0:T(1,128)} %get-tuple-element.238) | copy-start | bytes 49156
  667.0 13.8 %copy-start.64 = (f32[3]{0:T(128)S(1)}, f32[3]{0:T(128)}, u32[]{:S(2)}) copy-start(f32[3]{0:T(128)} %pad.20.clone) | copy-start | bytes 40
  667.0 13.9 %copy-start.47 = (f32[2,2,1024]{2,1,0:T(2,128)S(1)}, f32[2,2,1024]{2,1,0:T(2,128)}, u32[]{:S(2)}) copy-start(f32[2,2,1024]{2,1,0:T(2,128)} %param.31) | copy-start | bytes 49156
  667.0 15.2 %copy-start.43 = (f32[1,6,1024]{2,0,1:T(1,128)S(1)}, f32[1,6,1024]{2,0,1:T(1,128)}, u32[]{:S(2)}) copy-start(f32[1,6,1024]{2,0,1:T(1,128)} %get-tuple-element.232) | copy-start | bytes 73732
  667.0 15.2 %copy-start.44 = (f32[1,6,1024]{2,0,1:T(1,128)S(1)}, f32[1,6,1024]{2,0,1:T(1,128)}, u32[]{:S(2)}) copy-start(f32[1,6,1024]{2,0,1:T(1,128)} %get-tuple-element.233) | copy-start | bytes 73732
  667.0 15.2 %copy-start.45 = (f32[6,1024]{1,0:T(8,128)S(1)}, f32[6,1024]{1,0:T(8,128)}, u32[]{:S(2)}) copy-start(f32[6,1024]{1,0:T(8,128)} %param.25) | copy-start | bytes 73732
  674.2 4.6 collective-permute-start.34
  678.8 29.2 %collective-permute-start.17 = (bf16[1536,384]{1,0:T(8,128)(2,1)}, bf16[1536,384]{1,0:T(8,128)(2,1)}, u32[]{:S(2)}, u32[]{:S(2)}) collective-permute-start(bf16[1536,384]{1,0:T(8,128)(2,1)} %get-tuple-element.202), channel_id=1, source_target_pairs={{0,1},{1,0},{2,3},{3,2},{4,5},{5,4},{6,7},{7,6},{8,9},{9,8},{10,11... | collective-permute-start | bytes 3538952 | tf_op jit(solution)/shard_map/ppermute | solution.py:488
  679.6 8.9 %collective-permute-start.22 = (bf16[512,384]{1,0:T(8,128)(2,1)}, bf16[512,384]{1,0:T(8,128)(2,1)}, u32[]{:S(2)}, u32[]{:S(2)}) collective-permute-start(bf16[512,384]{1,0:T(8,128)(2,1)} %convolution_convert_fusion.3), channel_id=1, source_target_pairs={{0,2},{2,0},{4,6},{6,4},{8,10},{10,8},{12,14},{14,12},{16,18},{18,... | collective-permute-start | bytes 1179656 | tf_op jit(solution)/shard_map/ppermute | solution.py:488
  683.6 47.5 %collective-permute-start.18 = (bf16[1536,384]{1,0:T(8,128)(2,1)}, bf16[1536,384]{1,0:T(8,128)(2,1)}, u32[]{:S(2)}, u32[]{:S(2)}) collective-permute-start(bf16[1536,384]{1,0:T(8,128)(2,1)} %get-tuple-element.195), channel_id=1, source_target_pairs={{0,1},{1,0},{2,3},{3,2},{4,5},{5,4},{6,7},{7,6},{8,9},{9,8},{10,11... | collective-permute-start | bytes 3538952 | tf_op jit(solution)/shard_map/ppermute | solution.py:488
  684.8 23.2 %slice-start.2 = ((s8[6291456]{0:T(1024)(128)(4,1)}), s8[4194304]{0:T(1024)(128)(4,1)S(1)}, s32[]{:S(2)}) async-start(s8[6291456]{0:T(1024)(128)(4,1)} %bitcast.263), calls=%async_computation.7 | async-start | bytes 8388608
  688.5 19.5 %slice-start.3 = ((s8[6291456]{0:T(1024)(128)(4,1)}), s8[2097152]{0:T(1024)(128)(4,1)S(1)}, s32[]{:S(2)}) async-start(s8[6291456]{0:T(1024)(128)(4,1)} %bitcast.263), calls=%async_computation.8 | async-start | bytes 4194304
  691.5 16.5 %copy-start.5 = (bf16[1024,1536]{1,0:T(8,128)(2,1)S(1)}, bf16[1024,1536]{1,0:T(8,128)(2,1)}, u32[]{:S(2)}) copy-start(bf16[1024,1536]{1,0:T(8,128)(2,1)} %dynamic-slice_bitcast_fusion) | copy-start | bytes 9437188
  691.6 16.5 %copy-start.52 = (f32[1536]{0:T(1024)S(1)}, f32[1536]{0:T(1024)}, u32[]{:S(2)}) copy-start(f32[1536]{0:T(1024)} %copy-done.51) | copy-start | bytes 18436
  691.7 11.3 %collective-permute-start.23 = (bf16[2,2,64,768]{3,2,0,1:T(8,128)(2,1)S(1)}, bf16[2,2,64,768]{3,2,0,1:T(8,128)(2,1)S(1)}, u32[]{:S(2)}, u32[]{:S(2)}) collective-permute-start(bf16[2,2,64,768]{3,2,0,1:T(8,128)(2,1)S(1)} %fusion.36), channel_id=1, source_target_pairs={{0,4},{2,6},{4,0},{6,2},{8,12},{10,14},{12,8},{14,10},{16,20},{18,... | collective-permute-start | bytes 1179656 | tf_op jit(solution)/shard_map/ppermute | solution.py:488
  703.1 15.6 %copy-start.12 = (f32[2,64,1408]{2,1,0:T(8,128)S(1)}, f32[2,64,1408]{2,1,0:T(8,128)}, u32[]{:S(2)}) copy-start(f32[2,64,1408]{2,1,0:T(8,128)} %dynamic-slice_bitcast_fusion.5) | copy-start | bytes 2162692
  716.7 9.2 %collective-permute-start.24 = (bf16[2,64,1152]{2,1,0:T(8,128)(2,1)S(1)}, bf16[2,64,1152]{2,1,0:T(8,128)(2,1)S(1)}, u32[]{:S(2)}, u32[]{:S(2)}) collective-permute-start(bf16[2,64,1152]{2,1,0:T(8,128)(2,1)S(1)} %fusion.49), channel_id=1, source_target_pairs={{0,8},{2,10},{4,12},{6,14},{8,0},{10,2},{12,4},{14,6},{16,24},{18,... | collective-permute-start | bytes 884744 | tf_op jit(solution)/shard_map/ppermute | solution.py:488
  726.0 11.6 %collective-permute-start.25 = (bf16[64,2560]{1,0:T(8,128)(2,1)S(1)}, bf16[64,2560]{1,0:T(8,128)(2,1)S(1)}, u32[]{:S(2)}, u32[]{:S(2)}) collective-permute-start(bf16[64,2560]{1,0:T(8,128)(2,1)S(1)} %fusion.48), channel_id=1, source_target_pairs={{0,16},{2,18},{4,20},{6,22},{8,24},{10,26},{12,28},{14,30},{16,0},... | collective-permute-start | bytes 983048 | tf_op jit(solution)/shard_map/ppermute | solution.py:488
  742.3 4.5 collective-permute-start.27
  752.7 7.9 %collective-permute-start.29 = (bf16[64,2048]{1,0:T(8,128)(2,1)S(1)}, bf16[64,2048]{1,0:T(8,128)(2,1)}, u32[]{:S(2)}, u32[]{:S(2)}) collective-permute-start(bf16[64,2048]{1,0:T(8,128)(2,1)S(1)} %bitcast.293), channel_id=1, source_target_pairs={{0,1},{1,0},{2,3},{3,2},{4,5},{5,4},{6,7},{7,6},{8,9},{9,8},{10,11... | collective-permute-start | bytes 786440 | tf_op jit(solution)/shard_map/ppermute | solution.py:488
  755.4 8.6 %collective-permute-start.28 = (bf16[64,2048]{1,0:T(8,128)(2,1)S(1)}, bf16[64,2048]{1,0:T(8,128)(2,1)S(1)}, u32[]{:S(2)}, u32[]{:S(2)}) collective-permute-start(bf16[64,2048]{1,0:T(8,128)(2,1)S(1)} %bitcast.292), channel_id=1, source_target_pairs={{0,1},{1,0},{2,3},{3,2},{4,5},{5,4},{6,7},{7,6},{8,9},{9,8},{10,11... | collective-permute-start | bytes 786440 | tf_op jit(solution)/shard_map/ppermute | solution.py:488
  (51 other events, 290.5 us)
Sparse Core Ops, SparseCore 0:
  10.9 47.8 all-gather.4
  62.3 123.4 all-gather.6
  218.7 79.3 all-gather.8
  422.4 148.1 reduce-scatter.1

commit v3 on v2

--- a/solution.py
+++ b/solution.py
@@ -448,7 +448,7 @@
     )
     part = pl.BlockSpec((rows, block), lambda i: (0, i))
     owners = (blocks // 2, 2, dim // blocks)
-    half = pl.BlockSpec(owners + (block,), lambda i: (0, 0, 0, i))
+    half = pl.BlockSpec((None, *owners, block), lambda i: (i // per, 0, 0, 0, i % per))
     once = pl.BlockSpec((rows, dim), lambda i: (0, 0), pipeline_mode=pl.Buffered(1))
     return pl.pallas_call(
         functools.partial(feed_back_kernel, rows, ch, blocks),
@@ -465,8 +465,8 @@
         out_shape=[
             jax.ShapeDtypeStruct((1, every), f32),
             jax.ShapeDtypeStruct((rows, dim), f32),
-            jax.ShapeDtypeStruct(owners + (every,), low),
-            jax.ShapeDtypeStruct(owners + (every,), f32),
+            jax.ShapeDtypeStruct((groups, *owners, units), low),
+            jax.ShapeDtypeStruct((groups, *owners, units), f32),
         ],
         scratch_shapes=[
             pltpu.VMEM((dim, rows), low),
@@ -529,20 +529,11 @@
 
 
 def over_chips(value):
-    dp = lax.axis_size("dp")
-    groups = [[i for i in range(dp) if i % 2 == core] for core in range(2)]
+    size = lax.axis_size("mp") * lax.axis_size("dp")
+    groups = [[i for i in range(size) if i % 2 == core] for core in range(2)]
     return lax.psum_scatter(
-        value, "dp", scatter_dimension=0, axis_index_groups=groups, tiled=True
-    )
-
-
-def over_mp(value):
-    steps = bits_of(lax.axis_size("mp"))
-    rows, _, width = value.shape
-    value = value.reshape((rows,) + (2,) * steps + (width,))
-    for step in range(steps):
-        value = halve(value, "mp", step, steps - step)
-    return value
+        value, ("mp", "dp"), scatter_dimension=0, axis_index_groups=groups, tiled=True
+    )
 
 
 def over_mp_relative(blocks):
@@ -671,7 +662,7 @@
                 part = after(part, grad_rel[0][j])
             grad_rel[pair][j] = part if j == 0 else swap(part, "mp", j)
         summed_late = after(summed_low, piece) if j == mp - 1 else summed_late
-    feed_part = over_chips(feed_low.reshape(-1, mp * units))
+    feed_part = over_chips(feed_low.reshape(-1, units))
     out_part = core_first(core_halves(summed_late.T), attended_all)
 
     slot = lax.broadcasted_iota(jnp.int32, (dp * mp, heads_local), 0)
@@ -735,6 +726,9 @@
         grads_low, head_sums = attention_backward(
             probs, grad_now, attended_t, totals, queries, values_all, keys_t, pair, at
         )
+        if pair == pairs - 1 and pair > 0:
+            kept = [rows_of[pair - 1] for rows_of in got_rows]
+            grads_low, head_sums = lax.optimization_barrier((grads_low, head_sums, *kept))[:2]
         bias_pieces.append(head_sums)
         if pair > 0:
             qkv_pieces.append(own_piece(pair - 1, grads_low))
@@ -752,8 +746,9 @@
     qkv_pieces.append(own_piece(pairs - 1))
     while waiting:
         early = add_step(early)
-    parts = feed_part.astype(jnp.float32).reshape(2, -1, mp, units)
-    up_sum, down_sum = over_mp(parts[0]), over_mp(parts[1])
+    feed_rows = feed_part.shape[0] // 2
+    up_sum = feed_part[:feed_rows].astype(jnp.float32)
+    down_sum = feed_part[feed_rows:].astype(jnp.float32)
     gain_sum = early[: 2 * dim].reshape(2, dim)
     late_biases = early[2 * dim : 6 * dim].reshape(4, dim)
     unit_sum = early[6 * dim : 6 * dim + units * mp]

time: 779 us -> 765 us (0.982)
  waiting for transfers between devices: 50.7 us -> 38.4 us
    ppermute x35 -> x33, waiting for transfers between devices: 40.2 us -> 27.9 us  [swap(): return lax.ppermute(value, axis_name, [(i, i ^ mask) for i in range(size)])]
    ppermute x35 -> x33, starting transfers between devices: 29.9 us -> 29.6 us  [swap(): return lax.ppermute(value, axis_name, [(i, i ^ mask) for i in range(size)])]
  transfers between devices with their start and end apart: 39 -> 37, of which waited for: 11 -> 8; matrix products, arithmetic and copies ran while one was open for 29% -> 29% of each run, Pallas kernels for 49% -> 50%
where the time goes in v3:
time: 765 us; the launch traced here: 760 us
  Pallas kernels  440 us (58%)
  other arithmetic  91.9 us (12%)
  local copies, waits for them, and re-layouts  77.4 us (10%)
  matrix products  66.7 us (9%)
  waiting for transfers between devices  38.4 us (5%)
  starting transfers between devices  30 us (4%)
  between operations  15.1 us (2%)
    pallas_call x4, Pallas kernels, attention_backward(): pl.pallas_call(functools.partial(backward_kernel, bq, ch, tokens), grid=(...  184 us
    pallas_call x2, Pallas kernels, attention_forward(): pl.pallas_call(functools.partial(forward_kernel, bq, ch, tokens), grid=(c...  126 us
    pallas_call x1, Pallas kernels, feed_back(): pl.pallas_call(functools.partial(feed_back_kernel, rows, ch, blocks), gri...  63.8 us
    pallas_call x1, Pallas kernels, feed_forward(): pl.pallas_call(functools.partial(feed_kernel, rows, ch), grid=(groups * p...  47.5 us
    ppermute x33, starting transfers between devices, swap(): return lax.ppermute(value, axis_name, [(i, i ^ mask) for i in range(size)])  29.6 us
    ppermute x33, waiting for transfers between devices, swap(): return lax.ppermute(value, axis_name, [(i, i ^ mask) for i in range(size)])  27.9 us
    dot_general x4, matrix products, times_transposed(): lax.dot_general(left_side, right_side, (((1,), (1,)), ((), ())), preferre...  26.1 us
    pallas_call x1, Pallas kernels, project(): pl.pallas_call(functools.partial(project_kernel, pairs), grid=(tokens //...  19.4 us
  transfers between devices with their start and end apart: 37, of which 8 were waited for; matrix products, arithmetic and copies ran while one was open for 29% of the time, Pallas kernels for 50%

profile of v3, /device:TPU:0, one launch (start us, length us, event | category | flops | bytes accessed | tf_op | source)
XLA Modules:
  0.0 759.5 jit_solution(12476858743354564539)
XLA Ops:
  14.1 5.2 dynamic-slice_bitcast_fusion.1
  19.4 9.7 %pad_maximum_fusion = (bf16[3072,1024]{1,0:T(8,128)(2,1)}, bf16[1024,3072]{0,1:T(8,128)(2,1)}) fusion(bf16[1536,1024]{1,0:T(8,128)(2,1)} %get-tuple-element.195, bf16[1536,1024]{1,0:T(8,128)(2,1)S(1)} %get-tuple-element.196), kind=kLoop, calls=%fused_computation.10 | loop fusion | flops 12582912 | bytes 18874368 | tf_op jit(solution)/shard_map/concatenate | solution.py:593
  29.1 8.6 %copy.69 = bf16[1024,3072]{1,0:T(8,128)(2,1)} copy(bf16[1024,3072]{0,1:T(8,128)(2,1)} %get-tuple-element.192) | data formatting | bytes 12582912 | tf_op jit(solution)/shard_map/transpose | solution.py:602
  37.8 6.5 constant_dynamic-slice_fusion.10
  46.2 2.1 select_convert_fusion.marks
  48.3 10.5 %all-gather.5.cloned.1.call-done.weights = bf16[1024,1536]{1,0:T(8,128)(2,1)} async-done(((bf16[64,1536]{1,0:T(8,128)(2,1)}), bf16[1024,1536]{1,0:T(8,128)(2,1)}) %all-gather.5.cloned.1.call-update) | async-done | bytes 3145744 | tf_op jit(solution)/shard_map/all_gather | solution.py:597
  60.3 19.4 %project.1 = (bf16[3072,512]{1,0:T(8,128)(2,1)}, bf16[512,3072]{1,0:T(8,128)(2,1)}, bf16[4,3072,256]{2,1,0:T(8,128)(2,1)}, bf16[512,3072]{1,0:T(8,128)(2,1)}, bf...) custom-call(bf16[3072,1024]{1,0:T(8,128)(2,1)} %get-tuple-element.191.x, ...), custom_call_target="tpu_custom_call" | custom-call | flops 603979776 | bytes 1048576 | tf_op jit(solution)/shard_map/project/pallas_call | solution.py:91
  79.7 90.8 %attend.2 = (bf16[3,2,6,3072,512]{4,3,2,1,0:T(8,128)(2,1)}, f32[384,3072]{1,0:T(8,128)}, bf16[3072,384]{1,0:T(8,128)(2,1)}, f32[3,2,3072]{2,1,0:T(2,128)}, f32[3,2,128]{2,1,0:T(2,128)}) custom-call(bf16[4,3072,256]{2,1,0:T(8,128)(2,1)} %get-tuple-element.76.k_cur.k_nxt, bf16[4,3072,256]{2,1,0:T(8,128)(2,1)} %get-tuple-element.76.k_cur.k_nxt, ...), custom_call_target="tpu_custom_call" | custom-call | flops 3623878656 | bytes 1048576 | tf_op jit(solution)/shard_map/attend/pallas_call | solution.py:198
  170.5 3.3 fusion.102
  175.3 34.8 %attend.3 = (bf16[1,2,6,3072,512]{4,3,2,1,0:T(8,128)(2,1)}, f32[128,3072]{1,0:T(8,128)}, bf16[3072,128]{1,0:T(8,128)(2,1)}, f32[1,2,3072]{2,1,0:T(2,128)}, f32[1,2,128]{2,1,0:T(2,128)}) custom-call(bf16[4,3072,256]{2,1,0:T(8,128)(2,1)} %get-tuple-element.76.k_cur.k_nxt, bf16[4,3072,256]{2,1,0:T(8,128)(2,1)} %get-tuple-element.76.k_cur.k_nxt, ...), custom_call_target="tpu_custom_call" | custom-call | flops 1207959552 | bytes 1048576 | tf_op jit(solution)/shard_map/attend/pallas_call | solution.py:198
  210.1 1.9 fusion.105
  215.0 3.0 slice.228
  218.2 1.8 dynamic-slice_bitcast_fusion.4
  220.0 3.2 collective-permute-done.1
  223.2 5.7 fusion.109
  229.7 1.9 copy-done
  231.6 2.9 fusion.4.x.normed
  234.5 47.5 %feed.1 = (bf16[1536,4096]{1,0:T(8,128)(2,1)}, bf16[1536,4096]{1,0:T(8,128)(2,1)}, f32[1536,1024]{1,0:T(8,128)}) custom-call(bf16[1536,1024]{1,0:T(8,128)(2,1)} %fusion.4.x.normed, bf16[2,1024,4608]{2,1,0:T(8,128)(2,1)} %bitcast.221, bf16[2,1024,4608]{2,1,0:T(8,128)(2,1)} %bitcast.222, f32[1,4096]{1,0:T(1,128)} %bitcast.263), custom_call_target="tpu_custom_call" | custom-call | flops 1610612736 | bytes 1048576 | tf_op jit(solution)/shard_map/feed/pallas_call | solution.py:378
  282.0 5.9 fusion.97
  289.8 3.2 fusion.3
  293.0 4.3 fusion.96
  297.3 2.6 copy-done.1
  299.9 2.2 add_reduce_fusion.1
  302.2 63.8 %feed_back.1 = (f32[1,4096]{1,0:T(1,128)}, f32[1536,1024]{1,0:T(8,128)}, bf16[2,8,2,64,2048]{4,3,2,1,0:T(8,128)(2,1)}, f32[2,8,2,64,2048]{4,3,2,1,0:T(8,128)}) custom-call(s32[1]{0:T(128)} %bitcast.18.core, bf16[1536,1024]{1,0:T(8,128)(2,1)} %get-tuple-element.84.x, bf16[1536,1024]{1,0:T(8,128)(2,1)} %fusion.4.x.normed, bf16[2,1024,4608]{2,1,0:T(8,128)(2,1)} %bitcast.223, ...), custom_call_target="tpu_custom_call" | custom-call | flops 3221225472 | bytes 1048576 | tf_op jit(solution)/shard_map/feed_back/pallas_call | solution.py:453
  367.0 8.1 %multiply_reduce_fusion = (f32[1024]{0:T(1024)S(1)}, f32[1536]{0:T(1024)S(1)}, f32[1024]{0:T(1024)S(1)}, f32[1536,1024]{1,0:T(8,128)S(1)}) fusion(f32[1536,1024]{1,0:T(8,128)} %copy-done, f32[1536]{0:T(1024)S(1)} %fusion.80, f32[1536]{0:T(1024)S(1)} %broadcast_multiply_fusion.1, f32[1024]{0:T(1024)S(1)} %bitcast.260, f32[1536,1024]{1,0:T(8,128)} %get-tuple-element.87, ...), kind=kLoop, calls=%fused_computation.12 | loop fusion | flops 15725056 | bytes 25202688 | tf_op jit(solution)/shard_map/transpose(jvp())/reduce_sum | solution.py:28
  376.3 2.8 fusion.95
  379.8 2.0 copy-done.2
  385.9 1.8 convolution_convert_fusion
  390.3 2.9 copy.71
  393.3 2.2 constant_dynamic-slice_fusion.9
  395.6 3.8 convolution_convert_fusion.2
  399.4 1.8 convolution_convert_fusion.1
  403.8 1.9 dynamic-slice_bitcast_fusion
  408.8 1.9 pad_maximum_fusion.6.grad
  410.7 4.7 convert_add_fusion
  415.5 8.5 %add_convert_fusion = bf16[2,8,2,64,2048]{4,3,2,1,0:T(8,128)(2,1)} fusion(f32[2,8,2,64,2048]{4,3,2,1,0:T(8,128)S(1)} %bitcast.232, bf16[2,8,2,64,2048]{4,3,2,1,0:T(8,128)(2,1)} %collective-permute-done.3), kind=kLoop, calls=%fused_computation | loop fusion | flops 12582912 | bytes 33554432 | tf_op jit(solution)/shard_map/convert_element_type | solution.py:653
  424.0 46.1 %attend_back.4 = (bf16[3072,384]{1,0:T(8,128)(2,1)}, f32[2,128]{1,0:T(2,128)}) custom-call(bf16[3,2,6,3072,512]{4,3,2,1,0:T(8,128)(2,1)} %get-tuple-element.88.p_ref, bf16[3072,128]{1,0:T(8,128)(2,1)} %pad_maximum_fusion.6.grad, f32[384,3072]{1,0:T(8,128)} %get-tuple-element.96.out_t, f32[3,2,3072]{2,1,0:T(2,128)} %get-tuple-element.97.totals, ...), custom_call_target="tpu_custom_call" | custom-call | flops 2415919104 | bytes 1048576 | tf_op jit(solution)/shard_map/attend_back/pallas_call | solution.py:301
  470.2 4.4 convolution_convert_fusion.6
  478.7 45.7 %attend_back.5 = (bf16[3072,384]{1,0:T(8,128)(2,1)}, f32[2,128]{1,0:T(2,128)}) custom-call(bf16[3,2,6,3072,512]{4,3,2,1,0:T(8,128)(2,1)} %get-tuple-element.88.p_ref, bf16[3072,128]{1,0:T(8,128)(2,1)} %pad_maximum_fusion.7.grad, f32[384,3072]{1,0:T(8,128)} %get-tuple-element.96.out_t, f32[3,2,3072]{2,1,0:T(2,128)} %get-tuple-element.97.totals, ...), custom_call_target="tpu_custom_call" | custom-call | flops 2415919104 | bytes 1048576 | tf_op jit(solution)/shard_map/attend_back/pallas_call | solution.py:301
  524.4 3.5 fusion.100
  528.0 4.4 convolution_convert_fusion.5
  532.6 1.9 pad_maximum_fusion.8.grad
  535.3 1.9 collective-permute-start.13
  537.3 2.1 collective-permute-done.13
  539.4 1.9 collective-permute-start.14
  542.0 1.9 convert_add_fusion.4
  546.3 45.9 %attend_back.6 = (bf16[3072,384]{1,0:T(8,128)(2,1)}, f32[2,128]{1,0:T(2,128)}) custom-call(bf16[3,2,6,3072,512]{4,3,2,1,0:T(8,128)(2,1)} %get-tuple-element.88.p_ref, bf16[3072,128]{1,0:T(8,128)(2,1)} %pad_maximum_fusion.8.grad, f32[384,3072]{1,0:T(8,128)} %get-tuple-element.96.out_t, f32[3,2,3072]{2,1,0:T(2,128)} %get-tuple-element.97.totals, ...), custom_call_target="tpu_custom_call" | custom-call | flops 2415919104 | bytes 1048576 | tf_op jit(solution)/shard_map/attend_back/pallas_call | solution.py:301
  593.4 3.7 convert_add_fusion.3
  600.1 2.1 collective-permute-start.19
  602.3 2.6 convolution_convert_fusion.4
  604.8 1.9 pad_maximum_fusion.9.grad
  610.3 45.9 %attend_back.7 = (bf16[3072,384]{1,0:T(8,128)(2,1)}, f32[2,128]{1,0:T(2,128)}) custom-call(bf16[1,2,6,3072,512]{4,3,2,1,0:T(8,128)(2,1)} %get-tuple-element.113.p_ref, bf16[3072,128]{1,0:T(8,128)(2,1)} %pad_maximum_fusion.9.grad, f32[128,3072]{1,0:T(8,128)} %get-tuple-element.122.out_t, f32[1,2,3072]{2,1,0:T(2,128)} %get-tuple-element.123.totals, ...), custom_call_target="tpu_custom_call" | custom-call | flops 2415919104 | bytes 1048576 | tf_op jit(solution)/shard_map/attend_back/pallas_call | solution.py:301
  667.8 5.3 convolution_convert_fusion.3
  675.7 7.1 fusion.5
  683.0 8.7 %add_add_fusion.2 = f32[1536,1024]{1,0:T(8,128)S(1)} fusion(f32[1536,1024]{1,0:T(8,128)} %fusion.5, f32[1536,1024]{1,0:T(8,128)S(1)} %bitcast.230, bf16[1536,384]{1,0:T(8,128)(2,1)} %collective-permute-done.17, bf16[1536,384]{1,0:T(8,128)(2,1)} %collective-permute-done.14, bf16[1536,384]{1,0:T(8,128)(2,1)} %collective-permute-done.10, ...), kind=kOutput, calls=%fused_computation.11 | convolution fusion | flops 3639214080 | bytes 24780800 | tf_op jit(solution)/shard_map/dot_general | solution.py:32
  697.4 3.5 convert_add_fusion.2
  702.2 2.8 convolution_add_fusion.1
  705.3 1.9 collective-permute-start.23
  708.3 7.1 collective-permute-done.23
  718.0 4.6 collective-permute-done.24
  724.4 4.6 convolution_add_fusion
  729.1 8.5 %collective-permute-done.25 = bf16[64,2560]{1,0:T(8,128)(2,1)S(1)} collective-permute-done((bf16[64,2560]{1,0:T(8,128)(2,1)S(1)}, bf16[64,2560]{1,0:T(8,128)(2,1)S(1)}, u32[]{:S(2)}, u32[]{:S(2)}) %collective-permute-start.25) | collective-permute-done | bytes 327712 | tf_op jit(solution)/shard_map/ppermute | solution.py:488
  742.6 2.2 fusion.51
  748.2 3.2 fusion.56
  (332 shorter events, 85.7 us)
Async XLA Ops:
  7.2 51.6 %all-gather.5.cloned.1.call-start = ((), (), s32[]{:S(2)}) async-start(), calls=%async_computation.1 | async-start | bytes 3342336 | tf_op jit(solution)/shard_map/all_gather | solution.py:597
  9.4 205.6 %all-gather.7.cloned.1.call-start = ((), (), s32[]{:S(2)}) async-start(), calls=%async_computation.2 | async-start | bytes 19464192 | tf_op jit(solution)/shard_map/all_gather | solution.py:614
  44.3 14.8 %slice-start.10 = ((f32[6,1024]{1,0:T(8,128)}), f32[2,1024]{1,0:T(2,128)S(1)}, s32[]{:S(2)}) async-start(f32[6,1024]{1,0:T(8,128)} %param.25), calls=%async_computation.15 | async-start | bytes 16384 | tf_op jit(solution)/shard_map/slice | solution.py:608
  44.3 15.4 %copy-start.46 = (f32[2,4096]{1,0:T(2,128)S(1)}, f32[2,4096]{1,0:T(2,128)}, u32[]{:S(2)}) copy-start(f32[2,4096]{1,0:T(2,128)} %param.33) | copy-start | bytes 98308
  58.8 243.3 %all-gather.9.cloned.1.call-start = ((), (), s32[]{:S(2)}) async-start(), calls=%async_computation.4 | async-start | bytes 9437184 | tf_op jit(solution)/shard_map/all_gather | solution.py:616
  173.8 49.3 %collective-permute-start = (bf16[1536,384]{1,0:T(8,128)(2,1)}, bf16[1536,384]{1,0:T(8,128)(2,1)}, u32[]{:S(2)}, u32[]{:S(2)}) collective-permute-start(bf16[1536,384]{1,0:T(8,128)(2,1)} %get-tuple-element.208), channel_id=1, source_target_pairs={{0,1},{1,0},{2,3},{3,2},{4,5},{5,4},{6,7},{7,6},{8,9},{9,8},{10,11... | collective-permute-start | bytes 3538952 | tf_op jit(solution)/shard_map/ppermute | solution.py:488
  212.0 11.1 %copy-start.36 = (bf16[1536,128]{1,0:T(8,128)(2,1)}, bf16[1536,128]{1,0:T(8,128)(2,1)S(1)}, u32[]{:S(2)}) copy-start(bf16[1536,128]{1,0:T(8,128)(2,1)S(1)} %get-tuple-element.230) | copy-start | bytes 1179652
  212.0 11.1 %collective-permute-start.1 = (bf16[1536,128]{1,0:T(8,128)(2,1)}, bf16[1536,128]{1,0:T(8,128)(2,1)}, u32[]{:S(2)}, u32[]{:S(2)}) collective-permute-start(bf16[1536,128]{1,0:T(8,128)(2,1)} %get-tuple-element.231), channel_id=1, source_target_pairs={{0,1},{1,0},{2,3},{3,2},{4,5},{5,4},{6,7},{7,6},{8,9},{9,8},{10,11... | collective-permute-start | bytes 1179656 | tf_op jit(solution)/shard_map/ppermute | solution.py:488
  218.1 530.1 %reduce-scatter.2.cloned.1.call-start = ((), (), s32[]{:S(2)}) async-start(), calls=%async_computation.3 | async-start | bytes 8912896 | tf_op jit(solution)/shard_map/reduce_scatter | solution.py:534
  220.0 8.9 %copy-start.29 = (bf16[1024,512]{1,0:T(8,128)(2,1)}, bf16[1024,512]{1,0:T(8,128)(2,1)S(1)}, u32[]{:S(2)}) copy-start(bf16[1024,512]{1,0:T(8,128)(2,1)S(1)} %get-tuple-element.209) | copy-start | bytes 3145732
  220.0 8.9 %copy-start.31 = (bf16[1024,512]{1,0:T(8,128)(2,1)}, bf16[1024,512]{1,0:T(8,128)(2,1)S(1)}, u32[]{:S(2)}) copy-start(bf16[1024,512]{1,0:T(8,128)(2,1)S(1)} %get-tuple-element.210) | copy-start | bytes 3145732
  234.5 47.5 %copy-start.51 = (f32[1,1024]{1,0:T(1,128)S(1)}, f32[1,1024]{1,0:T(1,128)}, u32[]{:S(2)}) copy-start(f32[1,1024]{1,0:T(1,128)} %get-tuple-element.245) | copy-start | bytes 12292
  302.1 63.8 %copy-start.42 = (f32[2,6,1024]{2,0,1:T(2,128)S(1)}, f32[2,6,1024]{2,0,1:T(2,128)}, u32[]{:S(2)}) copy-start(f32[2,6,1024]{2,0,1:T(2,128)} %param.32) | copy-start | bytes 147460
  302.1 64.5 %copy-start.53 = (f32[3,2,128]{2,1,0:T(2,128)S(1)}, f32[3,2,128]{2,1,0:T(2,128)}, u32[]{:S(2)}) copy-start(f32[3,2,128]{2,1,0:T(2,128)} %get-tuple-element.93) | copy-start | bytes 9220
  302.1 64.5 %copy-start.57 = (f32[1,2,128]{2,1,0:T(2,128)S(1)}, f32[1,2,128]{2,1,0:T(2,128)}, u32[]{:S(2)}) copy-start(f32[1,2,128]{2,1,0:T(2,128)} %get-tuple-element.94) | copy-start | bytes 3076
  302.1 64.6 %copy-start.58 = (pred[32]{0:T(512)(128)(4,1)S(1)}, pred[32]{0:T(512)(128)(4,1)}, u32[]{:S(2)}) copy-start(pred[32]{0:T(512)(128)(4,1)} %iota_compare_fusion.2) | copy-start | bytes 100
  365.9 49.5 %collective-permute-start.3 = (bf16[2,8,2,64,2048]{4,3,2,1,0:T(8,128)(2,1)}, bf16[2,8,2,64,2048]{4,3,2,1,0:T(8,128)(2,1)}, u32[]{:S(2)}, u32[]{:S(2)}) collective-permute-start(bf16[2,8,2,64,2048]{4,3,2,1,0:T(8,128)(2,1)} %get-tuple-element.90), channel_id=1, source_target_pairs={{0,2},{2,0},{4,6},{6,4},{8,10},{10,8},{12,14},{14,12},{16,18},{18,... | collective-permute-start | bytes 25165832 | tf_op jit(solution)/shard_map/ppermute | solution.py:488
  366.9 9.3 %slice-start = ((s8[6291456]{0:T(1024)(128)(4,1)}), s8[4194304]{0:T(1024)(128)(4,1)S(1)}, s32[]{:S(2)}) async-start(s8[6291456]{0:T(1024)(128)(4,1)} %bitcast.225), calls=%async_computation.5 | async-start | bytes 8388608
  367.0 9.3 %slice-start.1 = ((s8[6291456]{0:T(1024)(128)(4,1)}), s8[2097152]{0:T(1024)(128)(4,1)S(1)}, s32[]{:S(2)}) async-start(s8[6291456]{0:T(1024)(128)(4,1)} %bitcast.225), calls=%async_computation.6 | async-start | bytes 4194304
  385.3 17.0 %collective-permute-start.5 = (f32[10496]{0:T(1024)}, f32[10496]{0:T(1024)}, u32[]{:S(2)}, u32[]{:S(2)}) collective-permute-start(f32[10496]{0:T(1024)} %constant_dynamic-update-slice_fusion.7), channel_id=1, source_target_pairs={{0,1},{1,0},{2,3},{3,2},{4,5},{5,4},{6,7},{7,6},{8,9},{9,8},{10,11... | collective-permute-start | bytes 125960 | tf_op jit(solution)/shard_map/ppermute | solution.py:488
  388.8 17.4 %collective-permute-start.2 = (bf16[1536,128]{1,0:T(8,128)(2,1)}, bf16[1536,128]{1,0:T(8,128)(2,1)}, u32[]{:S(2)}, u32[]{:S(2)}) collective-permute-start(bf16[1536,128]{1,0:T(8,128)(2,1)} %get-tuple-element.224), channel_id=1, source_target_pairs={{0,1},{1,0},{2,3},{3,2},{4,5},{5,4},{6,7},{7,6},{8,9},{9,8},{10,11... | collective-permute-start | bytes 1179656 | tf_op jit(solution)/shard_map/ppermute | solution.py:488
  393.3 10.5 %slice-start.8 = ((s8[6291456]{0:T(1024)(128)(4,1)}), s8[4194304]{0:T(1024)(128)(4,1)S(1)}, s32[]{:S(2)}) async-start(s8[6291456]{0:T(1024)(128)(4,1)} %bitcast.250), calls=%async_computation.13 | async-start | bytes 8388608
  395.6 8.2 %slice-start.9 = ((s8[6291456]{0:T(1024)(128)(4,1)}), s8[2097152]{0:T(1024)(128)(4,1)S(1)}, s32[]{:S(2)}) async-start(s8[6291456]{0:T(1024)(128)(4,1)} %bitcast.250), calls=%async_computation.14 | async-start | bytes 4194304
  399.3 11.4 %collective-permute-start.4 = (bf16[512,1024]{1,0:T(8,128)(2,1)S(1)}, bf16[512,1024]{1,0:T(8,128)(2,1)S(1)}, u32[]{:S(2)}, u32[]{:S(2)}) collective-permute-start(bf16[512,1024]{1,0:T(8,128)(2,1)S(1)} %convolution_convert_fusion.2), channel_id=1, source_target_pairs={{0,2},{2,0},{4,6},{6,4},{8,10},{10,8},{12,14},{14,12},{16,18},{18,... | collective-permute-start | bytes 3145736 | tf_op jit(solution)/shard_map/ppermute | solution.py:488
  399.4 16.0 %slice-start.4 = ((s8[16777216]{0:T(1024)(128)(4,1)}), s8[4194304]{0:T(1024)(128)(4,1)S(1)}, s32[]{:S(2)}) async-start(s8[16777216]{0:T(1024)(128)(4,1)} %bitcast.231), calls=%async_computation.9 | async-start | bytes 8388608
  399.4 16.0 %slice-start.5 = ((s8[16777216]{0:T(1024)(128)(4,1)}), s8[4194304]{0:T(1024)(128)(4,1)S(1)}, s32[]{:S(2)}) async-start(s8[16777216]{0:T(1024)(128)(4,1)} %bitcast.231), calls=%async_computation.10 | async-start | bytes 8388608
  403.2 12.2 %slice-start.6 = ((s8[16777216]{0:T(1024)(128)(4,1)}), s8[4194304]{0:T(1024)(128)(4,1)S(1)}, s32[]{:S(2)}) async-start(s8[16777216]{0:T(1024)(128)(4,1)} %bitcast.231), calls=%async_computation.11 | async-start | bytes 8388608
  403.2 2.4 collective-permute-start.7
  406.3 70.5 %collective-permute-start.6 = (bf16[1536,128]{1,0:T(8,128)(2,1)S(1)}, bf16[1536,128]{1,0:T(8,128)(2,1)S(1)}, u32[]{:S(2)}, u32[]{:S(2)}) collective-permute-start(bf16[1536,128]{1,0:T(8,128)(2,1)S(1)} %get-tuple-element.103), channel_id=1, source_target_pairs={{0,1},{1,0},{2,3},{3,2},{4,5},{5,4},{6,7},{7,6},{8,9},{9,8},{10,11... | collective-permute-start | bytes 1179656 | tf_op jit(solution)/shard_map/ppermute | solution.py:488
  406.8 125.6 %collective-permute-start.8 = (bf16[1536,128]{1,0:T(8,128)(2,1)}, bf16[1536,128]{1,0:T(8,128)(2,1)}, u32[]{:S(2)}, u32[]{:S(2)}) collective-permute-start(bf16[1536,128]{1,0:T(8,128)(2,1)} %get-tuple-element.107), channel_id=1, source_target_pairs={{0,1},{1,0},{2,3},{3,2},{4,5},{5,4},{6,7},{7,6},{8,9},{9,8},{10,11... | collective-permute-start | bytes 1179656 | tf_op jit(solution)/shard_map/ppermute | solution.py:488
  408.3 196.5 %collective-permute-start.12 = (bf16[1536,128]{1,0:T(8,128)(2,1)}, bf16[1536,128]{1,0:T(8,128)(2,1)}, u32[]{:S(2)}, u32[]{:S(2)}) collective-permute-start(bf16[1536,128]{1,0:T(8,128)(2,1)} %get-tuple-element.115), channel_id=1, source_target_pairs={{0,1},{1,0},{2,3},{3,2},{4,5},{5,4},{6,7},{7,6},{8,9},{9,8},{10,11... | collective-permute-start | bytes 1179656 | tf_op jit(solution)/shard_map/ppermute | solution.py:488
  424.0 46.1 %copy-start.7 = (bf16[8,1,64,3072]{3,2,1,0:T(8,128)(2,1)S(1)}, bf16[8,1,64,3072]{3,2,1,0:T(8,128)(2,1)}, u32[]{:S(2)}) copy-start(bf16[8,1,64,3072]{3,2,1,0:T(8,128)(2,1)} %get-tuple-element.194) | copy-start | bytes 9437188
  474.5 60.0 %collective-permute-start.9 = (f32[10496]{0:T(1024)}, f32[10496]{0:T(1024)S(1)}, u32[]{:S(2)}, u32[]{:S(2)}) collective-permute-start(f32[10496]{0:T(1024)} %add.361), channel_id=1, source_target_pairs={{0,4},{2,6},{4,0},{6,2},{8,12},{10,14},{12,8},{14,10},{16,20},{18,... | collective-permute-start | bytes 125960 | tf_op jit(solution)/shard_map/ppermute | solution.py:488
  475.5 66.4 %collective-permute-start.11 = (bf16[512,384]{1,0:T(8,128)(2,1)}, bf16[512,384]{1,0:T(8,128)(2,1)S(1)}, u32[]{:S(2)}, u32[]{:S(2)}) collective-permute-start(bf16[512,384]{1,0:T(8,128)(2,1)} %convolution_convert_fusion.6), channel_id=1, source_target_pairs={{0,2},{2,0},{4,6},{6,4},{8,10},{10,8},{12,14},{14,12},{16,18},{18,... | collective-permute-start | bytes 1179656 | tf_op jit(solution)/shard_map/ppermute | solution.py:488
  476.8 69.5 %collective-permute-start.10 = (bf16[1536,384]{1,0:T(8,128)(2,1)S(1)}, bf16[1536,384]{1,0:T(8,128)(2,1)}, u32[]{:S(2)}, u32[]{:S(2)}) collective-permute-start(bf16[1536,384]{1,0:T(8,128)(2,1)S(1)} %get-tuple-element.202), channel_id=1, source_target_pairs={{0,1},{1,0},{2,3},{3,2},{4,5},{5,4},{6,7},{7,6},{8,9},{9,8},{10,11... | collective-permute-start | bytes 3538952 | tf_op jit(solution)/shard_map/ppermute | solution.py:488
  528.0 9.3 %copy-start.55 = (f32[2,128]{1,0:T(2,128)S(1)}, f32[2,128]{1,0:T(2,128)}, u32[]{:S(2)}) copy-start(f32[2,128]{1,0:T(2,128)} %get-tuple-element.133) | copy-start | bytes 3076
  528.0 14.0 %copy-start.6 = (bf16[8,1,64,3072]{3,2,1,0:T(8,128)(2,1)S(1)}, bf16[8,1,64,3072]{3,2,1,0:T(8,128)(2,1)}, u32[]{:S(2)}) copy-start(bf16[8,1,64,3072]{3,2,1,0:T(8,128)(2,1)} %get-tuple-element.193) | copy-start | bytes 9437188
  528.0 14.0 %copy-start.15 = (bf16[3072,384]{1,0:T(8,128)(2,1)S(1)}, bf16[3072,384]{1,0:T(8,128)(2,1)}, u32[]{:S(2)}) copy-start(bf16[3072,384]{1,0:T(8,128)(2,1)} %get-tuple-element.101) | copy-start | bytes 7077892
  532.4 61.1 %collective-permute-start.15 = (bf16[512,384]{1,0:T(8,128)(2,1)}, bf16[512,384]{1,0:T(8,128)(2,1)}, u32[]{:S(2)}, u32[]{:S(2)}) collective-permute-start(bf16[512,384]{1,0:T(8,128)(2,1)} %convolution_convert_fusion.5), channel_id=1, source_target_pairs={{0,2},{2,0},{4,6},{6,4},{8,10},{10,8},{12,14},{14,12},{16,18},{18,... | collective-permute-start | bytes 1179656 | tf_op jit(solution)/shard_map/ppermute | solution.py:488
  535.3 4.1 collective-permute-start.13
  539.4 69.0 %collective-permute-start.14 = (bf16[1536,384]{1,0:T(8,128)(2,1)}, bf16[1536,384]{1,0:T(8,128)(2,1)}, u32[]{:S(2)}, u32[]{:S(2)}) collective-permute-start(bf16[1536,384]{1,0:T(8,128)(2,1)} %get-tuple-element.204), channel_id=1, source_target_pairs={{0,1},{1,0},{2,3},{3,2},{4,5},{5,4},{6,7},{7,6},{8,9},{9,8},{10,11... | collective-permute-start | bytes 3538952 | tf_op jit(solution)/shard_map/ppermute | solution.py:488
  545.0 53.1 %collective-permute-start.16 = (bf16[2,2,64,1408]{3,2,0,1:T(8,128)(2,1)}, bf16[2,2,64,1408]{3,2,0,1:T(8,128)(2,1)}, u32[]{:S(2)}, u32[]{:S(2)}) collective-permute-start(bf16[2,2,64,1408]{3,2,0,1:T(8,128)(2,1)} %fusion.25), channel_id=1, source_target_pairs={{0,4},{2,6},{4,0},{6,2},{8,12},{10,14},{12,8},{14,10},{16,20},{18,... | collective-permute-start | bytes 2162696 | tf_op jit(solution)/shard_map/ppermute | solution.py:488
  592.2 65.5 %collective-permute-start.26 = (f32[10496]{0:T(1024)}, f32[10496]{0:T(1024)}, u32[]{:S(2)}, u32[]{:S(2)}) collective-permute-start(f32[10496]{0:T(1024)} %add.365), channel_id=1, source_target_pairs={{0,16},{2,18},{4,20},{6,22},{8,24},{10,26},{12,28},{14,30},{16,0},... | collective-permute-start | bytes 125960 | tf_op jit(solution)/shard_map/ppermute | solution.py:488
  593.4 8.8 %copy-start.11 = (bf16[3072,384]{1,0:T(8,128)(2,1)S(1)}, bf16[3072,384]{1,0:T(8,128)(2,1)}, u32[]{:S(2)}) copy-start(bf16[3072,384]{1,0:T(8,128)(2,1)} %get-tuple-element.112) | copy-start | bytes 7077892
  597.2 110.0 %collective-permute-start.20 = (bf16[2,2,64,384]{3,2,0,1:T(8,128)(2,1)S(1)}, bf16[2,2,64,384]{3,2,0,1:T(8,128)(2,1)}, u32[]{:S(2)}, u32[]{:S(2)}) collective-permute-start(bf16[2,2,64,384]{3,2,0,1:T(8,128)(2,1)S(1)} %fusion.60), channel_id=1, source_target_pairs={{0,4},{2,6},{4,0},{6,2},{8,12},{10,14},{12,8},{14,10},{16,20},{18,... | collective-permute-start | bytes 589832 | tf_op jit(solution)/shard_map/ppermute | solution.py:488
  600.1 92.7 %collective-permute-start.19 = (bf16[2,64,1408]{2,1,0:T(8,128)(2,1)}, bf16[2,64,1408]{2,1,0:T(8,128)(2,1)}, u32[]{:S(2)}, u32[]{:S(2)}) collective-permute-start(bf16[2,64,1408]{2,1,0:T(8,128)(2,1)} %fusion.52), channel_id=1, source_target_pairs={{0,8},{2,10},{4,12},{6,14},{8,0},{10,2},{12,4},{14,6},{16,24},{18,... | collective-permute-start | bytes 1081352 | tf_op jit(solution)/shard_map/ppermute | solution.py:488
  604.8 92.6 %collective-permute-start.21 = (bf16[512,384]{1,0:T(8,128)(2,1)}, bf16[512,384]{1,0:T(8,128)(2,1)}, u32[]{:S(2)}, u32[]{:S(2)}) collective-permute-start(bf16[512,384]{1,0:T(8,128)(2,1)} %convolution_convert_fusion.4), channel_id=1, source_target_pairs={{0,2},{2,0},{4,6},{6,4},{8,10},{10,8},{12,14},{14,12},{16,18},{18,... | collective-permute-start | bytes 1179656 | tf_op jit(solution)/shard_map/ppermute | solution.py:488
  608.4 56.6 %collective-permute-start.17 = (bf16[1536,384]{1,0:T(8,128)(2,1)}, bf16[1536,384]{1,0:T(8,128)(2,1)}, u32[]{:S(2)}, u32[]{:S(2)}) collective-permute-start(bf16[1536,384]{1,0:T(8,128)(2,1)} %get-tuple-element.206), channel_id=1, source_target_pairs={{0,1},{1,0},{2,3},{3,2},{4,5},{5,4},{6,7},{7,6},{8,9},{9,8},{10,11... | collective-permute-start | bytes 3538952 | tf_op jit(solution)/shard_map/ppermute | solution.py:488
  610.3 46.9 %copy-start.54 = (f32[2,128]{1,0:T(2,128)S(1)}, f32[2,128]{1,0:T(2,128)}, u32[]{:S(2)}) copy-start(f32[2,128]{1,0:T(2,128)} %get-tuple-element.134) | copy-start | bytes 3076
  666.9 15.9 %collective-permute-start.28 = (f32[2,1024]{1,0:T(2,128)S(1)}, f32[2,1024]{1,0:T(2,128)S(1)}, u32[]{:S(2)}, u32[]{:S(2)}) collective-permute-start(f32[2,1024]{1,0:T(2,128)S(1)} %constant_dynamic-update-slice_fusion.6), channel_id=1, source_target_pairs={{0,1},{1,0},{2,3},{3,2},{4,5},{5,4},{6,7},{7,6},{8,9},{9,8},{10,11... | collective-permute-start | bytes 24584 | tf_op jit(solution)/shard_map/ppermute | solution.py:488
  673.1 29.2 %collective-permute-start.22 = (bf16[512,384]{1,0:T(8,128)(2,1)}, bf16[512,384]{1,0:T(8,128)(2,1)}, u32[]{:S(2)}, u32[]{:S(2)}) collective-permute-start(bf16[512,384]{1,0:T(8,128)(2,1)} %convolution_convert_fusion.3), channel_id=1, source_target_pairs={{0,2},{2,0},{4,6},{6,4},{8,10},{10,8},{12,14},{14,12},{16,18},{18,... | collective-permute-start | bytes 1179656 | tf_op jit(solution)/shard_map/ppermute | solution.py:488
  673.1 9.9 %slice-start.2 = ((s8[6291456]{0:T(1024)(128)(4,1)}), s8[4194304]{0:T(1024)(128)(4,1)S(1)}, s32[]{:S(2)}) async-start(s8[6291456]{0:T(1024)(128)(4,1)} %bitcast.229), calls=%async_computation.7 | async-start | bytes 8388608
  675.7 7.3 copy-start.5
  675.7 7.3 copy-start.44
  682.9 8.8 %collective-permute-start.29 = (f32[2,1024]{1,0:T(2,128)S(1)}, f32[2,1024]{1,0:T(2,128)S(1)}, u32[]{:S(2)}, u32[]{:S(2)}) collective-permute-start(f32[2,1024]{1,0:T(2,128)S(1)} %constant_dynamic-update-slice_fusion.5), channel_id=1, source_target_pairs={{0,2},{2,0},{4,6},{6,4},{8,10},{10,8},{12,14},{14,12},{16,18},{18,... | collective-permute-start | bytes 24584 | tf_op jit(solution)/shard_map/ppermute | solution.py:488
  691.7 32.8 %collective-permute-start.18 = (bf16[1536,384]{1,0:T(8,128)(2,1)}, bf16[1536,384]{1,0:T(8,128)(2,1)S(1)}, u32[]{:S(2)}, u32[]{:S(2)}) collective-permute-start(bf16[1536,384]{1,0:T(8,128)(2,1)} %get-tuple-element.199), channel_id=1, source_target_pairs={{0,1},{1,0},{2,3},{3,2},{4,5},{5,4},{6,7},{7,6},{8,9},{9,8},{10,11... | collective-permute-start | bytes 3538952 | tf_op jit(solution)/shard_map/ppermute | solution.py:488
  692.9 3.7 collective-permute-start.30
  696.6 4.3 collective-permute-start.31
  701.0 7.2 collective-permute-start.32
  705.2 12.2 %copy-start.41 = (f32[6,1024]{1,0:T(8,128)S(1)}, f32[6,1024]{1,0:T(8,128)}, u32[]{:S(2)}) copy-start(f32[6,1024]{1,0:T(8,128)} %param.25) | copy-start | bytes 73732
  705.3 10.1 %collective-permute-start.23 = (bf16[2,2,64,768]{3,2,0,1:T(8,128)(2,1)S(1)}, bf16[2,2,64,768]{3,2,0,1:T(8,128)(2,1)S(1)}, u32[]{:S(2)}, u32[]{:S(2)}) collective-permute-start(bf16[2,2,64,768]{3,2,0,1:T(8,128)(2,1)S(1)} %fusion.42), channel_id=1, source_target_pairs={{0,4},{2,6},{4,0},{6,2},{8,12},{10,14},{12,8},{14,10},{16,20},{18,... | collective-permute-start | bytes 1179656 | tf_op jit(solution)/shard_map/ppermute | solution.py:488
  715.5 7.1 collective-permute-start.24
  722.7 14.8 %collective-permute-start.25 = (bf16[64,2560]{1,0:T(8,128)(2,1)S(1)}, bf16[64,2560]{1,0:T(8,128)(2,1)S(1)}, u32[]{:S(2)}, u32[]{:S(2)}) collective-permute-start(bf16[64,2560]{1,0:T(8,128)(2,1)S(1)} %fusion.54), channel_id=1, source_target_pairs={{0,16},{2,18},{4,20},{6,22},{8,24},{10,26},{12,28},{14,30},{16,0},... | collective-permute-start | bytes 983048 | tf_op jit(solution)/shard_map/ppermute | solution.py:488
  742.4 4.3 collective-permute-start.27
  (43 other events, 187.4 us)
Sparse Core Ops, SparseCore 0:
  10.9 47.8 all-gather.4
  62.3 123.4 all-gather.6
  218.2 79.6 all-gather.8
  424.1 198.7 reduce-scatter.1

commit v4 on v3

--- a/solution.py
+++ b/solution.py
@@ -386,9 +386,73 @@
             jax.ShapeDtypeStruct((rows, dim), f32),
         ],
         compiler_params=kernel_params(),
-        cost_estimate=brief(4 * rows * dim * every),
+        cost_estimate=pl.CostEstimate(
+            flops=4 * rows * dim * every, bytes_accessed=8 * dim * every, transcendentals=0
+        ),
         name="feed",
     )(x, weights, weights, bias)
+
+
+def norm_parts(values):
+    center = values - jnp.mean(values, axis=-1, keepdims=True)
+    scale = lax.rsqrt(jnp.mean(center * center, axis=-1, keepdims=True) + 1e-05)
+    return center * scale, scale
+
+
+def norm_pull(normal, scale, gain, cotangent):
+    grad = cotangent * gain
+    mean = jnp.mean(grad, axis=-1, keepdims=True)
+    along = jnp.mean(grad * normal, axis=-1, keepdims=True)
+    return scale * (grad - mean - normal * along)
+
+
+def add_sums(sums, *values):
+    @pl.when(pl.program_id(0) == 0)
+    def _():
+        sums[...] = jnp.zeros_like(sums)
+
+    for at, value in enumerate(values):
+        sums[at : at + 1, :] += jnp.sum(value, axis=0, keepdims=True)
+
+
+def second_norm_kernel(normed, fed, cotangent, lines, result, grad_ref, low_ref, sums):
+    normal, scale = norm_parts(normed[...] + fed[...] + lines[2:3, :])
+    result[...] = (normal * lines[0:1, :] + lines[1:2, :]).astype(low)
+    cotangent = cotangent[...].astype(f32)
+    grad = norm_pull(normal, scale, lines[0:1, :], cotangent)
+    grad_ref[...] = grad
+    low_ref[...] = grad.astype(low)
+    add_sums(sums, cotangent * normal, cotangent, grad)
+
+
+def first_norm_kernel(summed, fed, total_grad, lines, grad_ref, low_ref, sums):
+    normal, scale = norm_parts(summed[...])
+    cotangent = fed[...] + total_grad[...]
+    grad = norm_pull(normal, scale, lines[0:1, :], cotangent)
+    grad_ref[...] = grad
+    low_ref[...] = grad.astype(low)
+    add_sums(sums, cotangent * normal, cotangent, grad)
+
+
+def norm_call(kernel, arrays, lines, kinds, name):
+    rows, dim = arrays[0].shape
+    block = 256 if rows % 256 == 0 else 128
+    part = pl.BlockSpec((block, dim), lambda i: (i, 0))
+    return pl.pallas_call(
+        kernel,
+        grid=(rows // block,),
+        in_specs=[part] * len(arrays) + [pl.BlockSpec(lines.shape, lambda i: (0, 0))],
+        out_specs=[part] * len(kinds) + [pl.BlockSpec((3, dim), lambda i: (0, 0))],
+        out_shape=[
+            *[jax.ShapeDtypeStruct((rows, dim), kind) for kind in kinds],
+            jax.ShapeDtypeStruct((3, dim), f32),
+        ],
+        compiler_params=kernel_params(),
+        cost_estimate=pl.CostEstimate(
+            flops=32 * rows * dim, bytes_accessed=36 * rows * dim, transcendentals=0
+        ),
+        name=name,
+    )(*arrays, lines)
 
 
 def feed_back_kernel(
@@ -613,7 +677,6 @@
     weight_set = after(weight_set, qkv_full, key_marks, query_marks, *input_halves)
     weights_all = lax.all_gather(weight_set, ("mp", "dp"), axis=0, tiled=True)
     weights_all = weights_all.reshape(mp, dim, -1)
-    qkv_all = lax.all_gather(after(qkv_full, weights_all), "mp", axis=0, tiled=False)
     own_core = (dp_me & 1).astype(jnp.int32).reshape(1)
 
     calls = [(0, pairs - 1), (pairs - 1, 1)] if pairs > 1 else [(0, 1)]
@@ -623,11 +686,18 @@
         probs, attended_t, attended, totals, maxima = attention_forward(
             key_rows, queries_t, query_marks, values_t, first, count, block
         )
+        if first > 0:
+            came = [parts[0] for parts in attended_rel[1:]]
+            attended, maxima = lax.optimization_barrier((attended, maxima, *came))[:2]
         saved.append((probs, attended_t, totals))
+        query_marks = after(query_marks, attended)
         tops.append(maxima)
         for j in range(mp):
             piece = attended[j * rows : (j + 1) * rows]
             attended_rel[j].append(piece if j == 0 else swap(piece, "mp", j))
+    qkv_all = lax.all_gather(
+        after(qkv_full, weights_all, totals), "mp", axis=0, tiled=False
+    )
     head_max = jnp.max(jnp.concatenate(tops).reshape(heads_local, PAIR), axis=1)
     head_max = head_max * HEAD_DIM ** (-0.5)
     attended_all = jnp.concatenate([piece for parts in attended_rel for piece in parts], axis=1)
@@ -635,24 +705,31 @@
     out_rel = [pick(weights_all[:, :, 2 * units :], me ^ j, 0) for j in range(mp)]
     branch = times_transposed(attended_all, jnp.concatenate(out_rel, axis=1))
     summed = inputs[:rows].astype(jnp.float32) + branch + bias_rows[2]
-    normed, first_norm_pull = jax.vjp(norm_rows, summed, norm_gains[0], bias_rows[4])
+    normed = norm_rows(summed, norm_gains[0], bias_rows[4])
     normed_low = normed.astype(low)
     hidden_low, slope, ffn_out = feed_forward(
         normed_low, weights_all, up_bias[None], units
     )
-    total = normed + ffn_out + bias_rows[3]
-    result, second_norm_pull = jax.vjp(norm_rows, total, norm_gains[1], bias_rows[5])
-    total_grad, second_gain_grad, second_shift_grad = second_norm_pull(
-        out_cotangent.astype(jnp.float32)
-    )
-    total_low = total_grad.astype(low)
+    second_lines = jnp.stack([norm_gains[1], bias_rows[5], bias_rows[3]])
+    result, total_grad, total_low, second_sums = norm_call(
+        second_norm_kernel,
+        [normed, ffn_out, out_cotangent],
+        second_lines,
+        [low, jnp.float32, low],
+        "second_norm",
+    )
     total_low = after(total_low, qkv_all)
     up_bias_grad, feed_grad, sent, own = feed_back(
         own_core, dp, total_low, normed_low, weights_all, slope, hidden_low, units
     )
     feed_low = (own + swap(sent, "dp", 1).astype(jnp.float32)).astype(low)
-    summed_grad, first_gain_grad, first_shift_grad = first_norm_pull(feed_grad + total_grad)
-    summed_low = summed_grad.astype(low)
+    summed_grad, summed_low, first_sums = norm_call(
+        first_norm_kernel,
+        [summed, feed_grad, total_grad],
+        norm_gains[:1],
+        [jnp.float32, low],
+        "first_norm",
+    )
     grad_rel = [[None] * mp for _ in range(pairs)]
     for j in reversed(range(mp)):
         piece = jnp.dot(summed_low, out_rel[j], preferred_element_type=jnp.float32).astype(low)
@@ -667,18 +744,8 @@
 
     slot = lax.broadcasted_iota(jnp.int32, (dp * mp, heads_local), 0)
     slots = jnp.where(slot == dp_me * mp + me, head_max[None], 0.0)
-    early = jnp.concatenate(
-        [
-            first_gain_grad,
-            second_gain_grad,
-            jnp.sum(summed_grad, axis=0),
-            jnp.sum(total_grad, axis=0),
-            first_shift_grad,
-            second_shift_grad,
-            up_bias_grad.reshape(-1),
-            slots.reshape(-1),
-        ]
-    )
+    slots = jnp.pad(slots.reshape(-1), (0, -slots.size % dim)).reshape(-1, dim)
+    early = jnp.concatenate([first_sums, second_sums, up_bias_grad.reshape(-1, dim), slots])
     waiting = sum_steps()
 
     def add_step(value, *others):
@@ -749,11 +816,6 @@
     feed_rows = feed_part.shape[0] // 2
     up_sum = feed_part[:feed_rows].astype(jnp.float32)
     down_sum = feed_part[feed_rows:].astype(jnp.float32)
-    gain_sum = early[: 2 * dim].reshape(2, dim)
-    late_biases = early[2 * dim : 6 * dim].reshape(4, dim)
-    unit_sum = early[6 * dim : 6 * dim + units * mp]
-    group_max = jnp.max(early[6 * dim + units * mp :].reshape(dp, mp, heads_local), axis=0)
-    local_max = pick(group_max, me, 0)
 
     input_grad = summed_grad + times_transposed(
         jnp.concatenate(own_rows, axis=1), qkv_full
@@ -770,6 +832,13 @@
     most_grad = input_grad
     for got, others in last_parts:
         input_grad = input_grad + times_transposed(got, others)
+    early = after(early, most_grad)
+    gain_sum = jnp.stack([early[0], early[3]])
+    late_biases = jnp.stack([early[2], early[5], early[1], early[4]])
+    unit_sum = early[6 : 6 + units * mp // dim].reshape(-1)
+    group_max = early[6 + units * mp // dim :].reshape(-1)[: dp * mp * heads_local]
+    group_max = jnp.max(group_max.reshape(dp, mp, heads_local), axis=0)
+    local_max = pick(group_max, me, 0)
     fresh = qkv_pieces[chained:]
     fresh = [out_part, *fresh] if chained == 0 else fresh
     summing = by_bits(jnp.concatenate(fresh, axis=1))

time: 765 us -> 759 us (level)
  other arithmetic: 91.9 us -> 64.2 us
  Pallas kernels: 440 us -> 466 us
  local copies, waits for them, and re-layouts: 77.4 us -> 61.3 us
    reduce_sum x7 -> x0, other arithmetic: 27.1 us -> none  [the longest x3 13 us: norm_rows(): center = values - jnp.mean(values, axis=-1, keepdims=True)]
    pallas_call x0 -> x2, Pallas kernels: none -> 26.5 us  [norm_call(): pl.pallas_call(kernel, grid=(rows // block,), in_specs=[part] * len(array...]
    unnamed x150 -> x145, local copies, waits for them, and re-layouts: 15.1 us -> 6.75 us
  transfers between devices with their start and end apart: 37 -> 37, of which waited for: 8 -> 8; matrix products, arithmetic and copies ran while one was open for 29% -> 25% of each run, Pallas kernels for 50% -> 53%
where the time goes in v4:
time: 759 us; the launch traced here: 753 us
  Pallas kernels  466 us (61%)
  matrix products  73 us (10%)
  other arithmetic  64.2 us (8%)
  local copies, waits for them, and re-layouts  61.3 us (8%)
  waiting for transfers between devices  42 us (6%)
  starting transfers between devices  30.4 us (4%)
  between operations  15.5 us (2%)
    pallas_call x4, Pallas kernels, attention_backward(): pl.pallas_call(functools.partial(backward_kernel, bq, ch, tokens), grid=(...  184 us
    pallas_call x2, Pallas kernels, attention_forward(): pl.pallas_call(functools.partial(forward_kernel, bq, ch, tokens), grid=(c...  125 us
    pallas_call x1, Pallas kernels, feed_back(): pl.pallas_call(functools.partial(feed_back_kernel, rows, ch, blocks), gri...  63.9 us
    pallas_call x1, Pallas kernels, feed_forward(): pl.pallas_call(functools.partial(feed_kernel, rows, ch), grid=(groups * p...  47.3 us
    dot_general x4, matrix products, times_transposed(): lax.dot_general(left_side, right_side, (((1,), (1,)), ((), ())), preferre...  31.9 us
    ppermute x33, waiting for transfers between devices, swap(): return lax.ppermute(value, axis_name, [(i, i ^ mask) for i in range(size)])  31.6 us
    ppermute x33, starting transfers between devices, swap(): return lax.ppermute(value, axis_name, [(i, i ^ mask) for i in range(size)])  30 us
    pallas_call x2, Pallas kernels, norm_call(): pl.pallas_call(kernel, grid=(rows // block,), in_specs=[part] * len(array...  26.5 us
  transfers between devices with their start and end apart: 37, of which 8 were waited for; matrix products, arithmetic and copies ran while one was open for 25% of the time, Pallas kernels for 53%

profile of v4, /device:TPU:0, one launch (start us, length us, event | category | flops | bytes accessed | tf_op | source)
XLA Modules:
  0.0 752.6 jit_solution(2587857517201886605)
XLA Ops:
  14.1 5.2 dynamic-slice_bitcast_fusion.1
  19.4 9.7 %pad_maximum_fusion = (bf16[3072,1024]{1,0:T(8,128)(2,1)}, bf16[1024,3072]{0,1:T(8,128)(2,1)}) fusion(bf16[1536,1024]{1,0:T(8,128)(2,1)} %get-tuple-element.214, bf16[1536,1024]{1,0:T(8,128)(2,1)S(1)} %get-tuple-element.215), kind=kLoop, calls=%fused_computation.1 | loop fusion | flops 12582912 | bytes 18874368 | tf_op jit(solution)/shard_map/concatenate | solution.py:657
  29.1 8.7 %copy.68 = bf16[1024,3072]{1,0:T(8,128)(2,1)} copy(bf16[1024,3072]{0,1:T(8,128)(2,1)} %get-tuple-element.211) | data formatting | bytes 12582912 | tf_op jit(solution)/shard_map/transpose | solution.py:666
  37.8 6.6 constant_dynamic-slice_fusion.10
  46.3 2.1 select_convert_fusion.marks
  48.4 10.4 %all-gather.5.cloned.1.call-done.weights = bf16[1024,1536]{1,0:T(8,128)(2,1)} async-done(((bf16[64,1536]{1,0:T(8,128)(2,1)}), bf16[1024,1536]{1,0:T(8,128)(2,1)}) %all-gather.5.cloned.1.call-update) | async-done | bytes 3145744 | tf_op jit(solution)/shard_map/all_gather | solution.py:661
  59.7 19.4 %project.1 = (bf16[3072,512]{1,0:T(8,128)(2,1)}, bf16[512,3072]{1,0:T(8,128)(2,1)}, bf16[4,3072,256]{2,1,0:T(8,128)(2,1)}, bf16[512,3072]{1,0:T(8,128)(2,1)}, bf...) custom-call(bf16[3072,1024]{1,0:T(8,128)(2,1)} %get-tuple-element.210.x, ...), custom_call_target="tpu_custom_call" | custom-call | flops 603979776 | bytes 1048576 | tf_op jit(solution)/shard_map/project/pallas_call | solution.py:91
  79.1 90.8 %attend.2 = (bf16[3,2,6,3072,512]{4,3,2,1,0:T(8,128)(2,1)}, f32[384,3072]{1,0:T(8,128)}, bf16[3072,384]{1,0:T(8,128)(2,1)}, f32[3,2,3072]{2,1,0:T(2,128)}, f32[3,2,128]{2,1,0:T(2,128)}) custom-call(bf16[4,3072,256]{2,1,0:T(8,128)(2,1)} %get-tuple-element.87.k_cur.k_nxt, bf16[4,3072,256]{2,1,0:T(8,128)(2,1)} %get-tuple-element.87.k_cur.k_nxt, ...), custom_call_target="tpu_custom_call" | custom-call | flops 3623878656 | bytes 1048576 | tf_op jit(solution)/shard_map/attend/pallas_call | solution.py:198
  169.9 3.3 fusion.99
  173.2 1.5 collective-permute-start
  174.6 34.7 %attend.3 = (bf16[1,2,6,3072,512]{4,3,2,1,0:T(8,128)(2,1)}, f32[128,3072]{1,0:T(8,128)}, bf16[3072,128]{1,0:T(8,128)(2,1)}, f32[1,2,3072]{2,1,0:T(2,128)}, f32[1,2,128]{2,1,0:T(2,128)}) custom-call(bf16[4,3072,256]{2,1,0:T(8,128)(2,1)} %get-tuple-element.87.k_cur.k_nxt, bf16[4,3072,256]{2,1,0:T(8,128)(2,1)} %get-tuple-element.87.k_cur.k_nxt, ...), custom_call_target="tpu_custom_call" | custom-call | flops 1207959552 | bytes 1048576 | tf_op jit(solution)/shard_map/attend/pallas_call | solution.py:198
  212.6 2.0 slice.237
  214.8 10.7 %collective-permute-done.1 = bf16[1536,128]{1,0:T(8,128)(2,1)S(1)} collective-permute-done((bf16[1536,128]{1,0:T(8,128)(2,1)S(1)}, bf16[1536,128]{1,0:T(8,128)(2,1)S(1)}, u32[]{:S(2)}, u32[]{:S(2)}) %collective-permute-start.1) | collective-permute-done | bytes 393248 | tf_op jit(solution)/shard_map/ppermute | solution.py:552
  225.6 5.5 fusion.106
  231.9 1.8 copy-done
  233.7 4.8 fusion.94
  238.5 47.3 %feed.1 = (bf16[1536,4096]{1,0:T(8,128)(2,1)}, bf16[1536,4096]{1,0:T(8,128)(2,1)}, f32[1536,1024]{1,0:T(8,128)}) custom-call(bf16[1536,1024]{1,0:T(8,128)(2,1)} %get-tuple-element.208.x.normed, bf16[2,1024,4608]{2,1,0:T(8,128)(2,1)} %bitcast.265, bf16[2,1024,4608]{2,1,0:T(8,128)(2,1)} %bitcast.266, f32[1,4096]{1,0:T(1,128)} %bitcast.304), custom_call_target="tpu_custom_call" | custom-call | flops 25769803776 | bytes 33554432 | tf_op jit(solution)/shard_map/feed/pallas_call | solution.py:378
  285.8 13.7 %second_norm.1 = (bf16[1536,1024]{1,0:T(8,128)(2,1)}, f32[1536,1024]{1,0:T(8,128)}, bf16[1536,1024]{1,0:T(8,128)(2,1)}, f32[3,1024]{1,0:T(4,128)}) custom-call(f32[1536,1024]{1,0:T(8,128)} %get-tuple-element.209.normed, f32[1536,1024]{1,0:T(8,128)} %get-tuple-element.96.fed, bf16[1536,1024]{1,0:T(8,128)(2,1)} %cotangent.1, f32[3,1024]{1,0:T(4,128)} %pad_maximum_fusion.16.lines), custom_call_target="tpu_custom_call" | custom-call | flops 50331648 | bytes 56623104 | tf_op jit(solution)/shard_map/second_norm/pallas_call | solution.py:441
  299.5 63.9 %feed_back.1 = (f32[1,4096]{1,0:T(1,128)}, f32[1536,1024]{1,0:T(8,128)}, bf16[2,8,2,64,2048]{4,3,2,1,0:T(8,128)(2,1)}, f32[2,8,2,64,2048]{4,3,2,1,0:T(8,128)}) custom-call(s32[1]{0:T(128)} %bitcast.15.core, bf16[1536,1024]{1,0:T(8,128)(2,1)} %get-tuple-element.101.x, bf16[1536,1024]{1,0:T(8,128)(2,1)} %get-tuple-element.208.x.normed, ...), custom_call_target="tpu_custom_call" | custom-call | flops 3221225472 | bytes 1048576 | tf_op jit(solution)/shard_map/feed_back/pallas_call | solution.py:517
  365.6 1.4 reduce.16
  367.0 12.8 %first_norm.1 = (f32[1536,1024]{1,0:T(8,128)}, bf16[1536,1024]{1,0:T(8,128)(2,1)}, f32[3,1024]{1,0:T(4,128)}) custom-call(f32[1536,1024]{1,0:T(8,128)} %copy-done, f32[1536,1024]{1,0:T(8,128)} %get-tuple-element.104.fed, f32[1536,1024]{1,0:T(8,128)} %get-tuple-element.105.total_grad, f32[1,1024]{1,0:T(1,128)} %copy-done.42), custom_call_target="tpu_custom_call" | custom-call | flops 50331648 | bytes 56623104 | tf_op jit(solution)/shard_map/first_norm/pallas_call | solution.py:441
  382.1 3.7 convolution_convert_fusion
  388.1 3.4 copy.70
  393.0 3.6 convolution_convert_fusion.2
  396.7 1.9 convolution_convert_fusion.1
  401.0 1.9 dynamic-slice_bitcast_fusion
  406.5 1.9 pad_maximum_fusion.6.grad
  408.4 4.6 convert_add_fusion
  413.1 8.5 %add_convert_fusion = bf16[2,8,2,64,2048]{4,3,2,1,0:T(8,128)(2,1)} fusion(f32[2,8,2,64,2048]{4,3,2,1,0:T(8,128)S(1)} %bitcast.272, bf16[2,8,2,64,2048]{4,3,2,1,0:T(8,128)(2,1)} %collective-permute-done.3), kind=kLoop, calls=%fused_computation | loop fusion | flops 12582912 | bytes 33554432 | tf_op jit(solution)/shard_map/convert_element_type | solution.py:725
  421.6 46.0 %attend_back.4 = (bf16[3072,384]{1,0:T(8,128)(2,1)}, f32[2,128]{1,0:T(2,128)}) custom-call(bf16[3,2,6,3072,512]{4,3,2,1,0:T(8,128)(2,1)} %get-tuple-element.107.p_ref, bf16[3072,128]{1,0:T(8,128)(2,1)} %pad_maximum_fusion.6.grad, f32[384,3072]{1,0:T(8,128)} %get-tuple-element.118.out_t, f32[3,2,3072]{2,1,0:T(2,128)} %get-tuple-element.119.totals, ...), custom_call_target="tpu_custom_call" | custom-call | flops 2415919104 | bytes 1048576 | tf_op jit(solution)/shard_map/attend_back/pallas_call | solution.py:301
  467.6 4.3 convolution_convert_fusion.6
  475.4 46.0 %attend_back.5 = (bf16[3072,384]{1,0:T(8,128)(2,1)}, f32[2,128]{1,0:T(2,128)}) custom-call(bf16[3,2,6,3072,512]{4,3,2,1,0:T(8,128)(2,1)} %get-tuple-element.107.p_ref, bf16[3072,128]{1,0:T(8,128)(2,1)} %pad_maximum_fusion.7.grad, f32[384,3072]{1,0:T(8,128)} %get-tuple-element.118.out_t, f32[3,2,3072]{2,1,0:T(2,128)} %get-tuple-element.119.totals, ...), custom_call_target="tpu_custom_call" | custom-call | flops 2415919104 | bytes 1048576 | tf_op jit(solution)/shard_map/attend_back/pallas_call | solution.py:301
  521.4 3.5 fusion.97
  524.9 4.4 convolution_convert_fusion.5
  529.5 1.9 pad_maximum_fusion.8.grad
  532.2 2.1 collective-permute-start.13
  534.3 3.2 collective-permute-done.13
  538.9 1.9 convert_add_fusion.4
  542.0 1.9 collective-permute-start.16
  544.0 45.9 %attend_back.6 = (bf16[3072,384]{1,0:T(8,128)(2,1)}, f32[2,128]{1,0:T(2,128)}) custom-call(bf16[3,2,6,3072,512]{4,3,2,1,0:T(8,128)(2,1)} %get-tuple-element.107.p_ref, bf16[3072,128]{1,0:T(8,128)(2,1)} %pad_maximum_fusion.8.grad, f32[384,3072]{1,0:T(8,128)} %get-tuple-element.118.out_t, f32[3,2,3072]{2,1,0:T(2,128)} %get-tuple-element.119.totals, ...), custom_call_target="tpu_custom_call" | custom-call | flops 2415919104 | bytes 1048576 | tf_op jit(solution)/shard_map/attend_back/pallas_call | solution.py:301
  590.9 3.5 convert_add_fusion.3
  599.1 1.5 collective-permute-start.17
  600.6 1.9 pad_maximum_fusion.9.grad
  602.5 2.6 convolution_convert_fusion.4
  605.9 45.8 %attend_back.7 = (bf16[3072,384]{1,0:T(8,128)(2,1)}, f32[2,128]{1,0:T(2,128)}) custom-call(bf16[1,2,6,3072,512]{4,3,2,1,0:T(8,128)(2,1)} %get-tuple-element.135.p_ref, bf16[3072,128]{1,0:T(8,128)(2,1)} %pad_maximum_fusion.9.grad, f32[128,3072]{1,0:T(8,128)} %get-tuple-element.144.out_t, f32[1,2,3072]{2,1,0:T(2,128)} %get-tuple-element.99.totals, ...), custom_call_target="tpu_custom_call" | custom-call | flops 2415919104 | bytes 1048576 | tf_op jit(solution)/shard_map/attend_back/pallas_call | solution.py:301
  653.1 4.3 convolution_convert_fusion.3
  660.0 7.2 fusion
  667.3 11.3 %add_add_fusion = f32[1536,1024]{1,0:T(8,128)} fusion(f32[1536,1024]{1,0:T(8,128)S(1)} %bitcast.309, f32[1536,1024]{1,0:T(8,128)} %fusion, bf16[1536,384]{1,0:T(8,128)(2,1)} %collective-permute-done.17, bf16[1536,384]{1,0:T(8,128)(2,1)} %collective-permute-done.14, bf16[1536,384]{1,0:T(8,128)(2,1)} %collective-permute-done.10, ...), kind=kOutput, calls=%fused_computation.2 | convolution fusion | flops 3637641216 | bytes 24772608 | tf_op jit(solution)/shard_map/dot_general | solution.py:32
  682.7 1.5 collective-permute-start.18
  684.3 4.6 convert_add_fusion.2
  689.0 1.7 collective-permute-start.30
  692.7 1.7 collective-permute-start.31
  694.4 1.8 convolution_add_fusion.1
  696.4 2.0 collective-permute-start.23
  699.2 1.7 collective-permute-start.32
  701.5 2.3 collective-permute-done.32
  704.4 3.1 collective-permute-done.23
  711.1 5.5 collective-permute-done.24
  716.6 1.7 collective-permute-start.25
  718.4 7.9 %convolution_add_fusion = f32[1536,1024]{1,0:T(8,128)} fusion(f32[1536,1024]{1,0:T(8,128)} %add_add_fusion, bf16[1536,384]{1,0:T(8,128)(2,1)} %collective-permute-done.18, bf16[1024,1536]{1,0:T(8,128)(2,1)} %dynamic-slice_bitcast_fusion), kind=kOutput, calls=%fused_computation.14 | convolution fusion | flops 1209532416 | bytes 14548992 | tf_op jit(solution)/shard_map/dot_general | solution.py:32
  726.3 5.7 collective-permute-done.25
  736.2 2.4 fusion.46
  741.0 3.2 fusion.51
  744.2 1.5 pad_maximum_fusion.4
  (316 shorter events, 64.1 us)
Async XLA Ops:
  7.2 51.6 %all-gather.5.cloned.1.call-start = ((), (), s32[]{:S(2)}) async-start(), calls=%async_computation.1 | async-start | bytes 3342336 | tf_op jit(solution)/shard_map/all_gather | solution.py:661
  9.4 200.0 %all-gather.7.cloned.1.call-start = ((), (), s32[]{:S(2)}) async-start(), calls=%async_computation.2 | async-start | bytes 19464192 | tf_op jit(solution)/shard_map/all_gather | solution.py:678
  44.4 14.7 %slice-start.6 = ((f32[6,1024]{1,0:T(8,128)}), f32[2,1024]{1,0:T(2,128)S(1)}, s32[]{:S(2)}) async-start(f32[6,1024]{1,0:T(8,128)} %param.25), calls=%async_computation.11 | async-start | bytes 16384 | tf_op jit(solution)/shard_map/slice | solution.py:672
  58.8 240.7 %all-gather.9.cloned.1.call-start = ((), (), s32[]{:S(2)}) async-start(), calls=%async_computation.4 | async-start | bytes 9437184 | tf_op jit(solution)/shard_map/all_gather | solution.py:698
  173.2 37.0 %collective-permute-start = (bf16[1536,384]{1,0:T(8,128)(2,1)}, bf16[1536,384]{1,0:T(8,128)(2,1)}, u32[]{:S(2)}, u32[]{:S(2)}) collective-permute-start(bf16[1536,384]{1,0:T(8,128)(2,1)} %get-tuple-element.227), channel_id=1, source_target_pairs={{0,1},{1,0},{2,3},{3,2},{4,5},{5,4},{6,7},{7,6},{8,9},{9,8},{10,11... | collective-permute-start | bytes 3538952 | tf_op jit(solution)/shard_map/ppermute | solution.py:552
  209.4 531.6 %reduce-scatter.2.cloned.1.call-start = ((), (), s32[]{:S(2)}) async-start(), calls=%async_computation.3 | async-start | bytes 8912896 | tf_op jit(solution)/shard_map/reduce_scatter | solution.py:598
  211.3 14.2 %copy-start.32 = (bf16[1536,128]{1,0:T(8,128)(2,1)}, bf16[1536,128]{1,0:T(8,128)(2,1)S(1)}, u32[]{:S(2)}) copy-start(bf16[1536,128]{1,0:T(8,128)(2,1)S(1)} %get-tuple-element.249) | copy-start | bytes 1179652
  211.3 14.2 %collective-permute-start.1 = (bf16[1536,128]{1,0:T(8,128)(2,1)S(1)}, bf16[1536,128]{1,0:T(8,128)(2,1)S(1)}, u32[]{:S(2)}, u32[]{:S(2)}) collective-permute-start(bf16[1536,128]{1,0:T(8,128)(2,1)S(1)} %get-tuple-element.250), channel_id=1, source_target_pairs={{0,1},{1,0},{2,3},{3,2},{4,5},{5,4},{6,7},{7,6},{8,9},{9,8},{10,11... | collective-permute-start | bytes 1179656 | tf_op jit(solution)/shard_map/ppermute | solution.py:552
  212.0 19.9 %copy-start.42 = (f32[1,1024]{1,0:T(1,128)}, f32[1,1024]{1,0:T(1,128)S(1)}, u32[]{:S(2)}) copy-start(f32[1,1024]{1,0:T(1,128)S(1)} %get-tuple-element.287.lines) | copy-start | bytes 12292
  214.6 10.9 %copy-start.21 = (bf16[1536,384]{1,0:T(8,128)(2,1)S(1)}, bf16[1536,384]{1,0:T(8,128)(2,1)}, u32[]{:S(2)}) copy-start(bf16[1536,384]{1,0:T(8,128)(2,1)} %get-tuple-element.226) | copy-start | bytes 3538948
  214.8 16.2 %copy-start.25 = (bf16[1024,512]{1,0:T(8,128)(2,1)}, bf16[1024,512]{1,0:T(8,128)(2,1)S(1)}, u32[]{:S(2)}) copy-start(bf16[1024,512]{1,0:T(8,128)(2,1)S(1)} %get-tuple-element.228) | copy-start | bytes 3145732
  214.8 16.2 %copy-start.27 = (bf16[1024,512]{1,0:T(8,128)(2,1)}, bf16[1024,512]{1,0:T(8,128)(2,1)S(1)}, u32[]{:S(2)}) copy-start(bf16[1024,512]{1,0:T(8,128)(2,1)S(1)} %get-tuple-element.229) | copy-start | bytes 3145732
  299.5 64.6 %copy-start.41 = (f32[2,6,1024]{2,0,1:T(2,128)S(1)}, f32[2,6,1024]{2,0,1:T(2,128)}, u32[]{:S(2)}) copy-start(f32[2,6,1024]{2,0,1:T(2,128)} %param.32) | copy-start | bytes 147460
  299.5 65.2 %copy-start.53 = (f32[3,2,128]{2,1,0:T(2,128)S(1)}, f32[3,2,128]{2,1,0:T(2,128)}, u32[]{:S(2)}) copy-start(f32[3,2,128]{2,1,0:T(2,128)} %get-tuple-element.115) | copy-start | bytes 9220
  299.5 65.2 %copy-start.57 = (f32[1,2,128]{2,1,0:T(2,128)S(1)}, f32[1,2,128]{2,1,0:T(2,128)}, u32[]{:S(2)}) copy-start(f32[1,2,128]{2,1,0:T(2,128)} %get-tuple-element.116) | copy-start | bytes 3076
  363.5 49.6 %collective-permute-start.3 = (bf16[2,8,2,64,2048]{4,3,2,1,0:T(8,128)(2,1)}, bf16[2,8,2,64,2048]{4,3,2,1,0:T(8,128)(2,1)}, u32[]{:S(2)}, u32[]{:S(2)}) collective-permute-start(bf16[2,8,2,64,2048]{4,3,2,1,0:T(8,128)(2,1)} %get-tuple-element.110), channel_id=1, source_target_pairs={{0,2},{2,0},{4,6},{6,4},{8,10},{10,8},{12,14},{14,12},{16,18},{18,... | collective-permute-start | bytes 25165832 | tf_op jit(solution)/shard_map/ppermute | solution.py:552
  367.0 12.8 %copy-start.52 = (f32[3,1024]{1,0:T(4,128)S(1)}, f32[3,1024]{1,0:T(4,128)}, u32[]{:S(2)}) copy-start(f32[3,1024]{1,0:T(4,128)} %get-tuple-element.113) | copy-start | bytes 36868
  367.0 15.0 %copy-start.28 = (bf16[1024,512]{1,0:T(8,128)(2,1)S(1)}, bf16[1024,512]{1,0:T(8,128)(2,1)}, u32[]{:S(2)}) copy-start(bf16[1024,512]{1,0:T(8,128)(2,1)} %copy-done.27) | copy-start | bytes 3145732
  381.2 18.4 %collective-permute-start.5 = (f32[11,1024]{1,0:T(8,128)}, f32[11,1024]{1,0:T(8,128)}, u32[]{:S(2)}, u32[]{:S(2)}) collective-permute-start(f32[11,1024]{1,0:T(8,128)} %pad_maximum_fusion.13), channel_id=1, source_target_pairs={{0,1},{1,0},{2,3},{3,2},{4,5},{5,4},{6,7},{7,6},{8,9},{9,8},{10,11... | collective-permute-start | bytes 135176 | tf_op jit(solution)/shard_map/ppermute | solution.py:552
  386.9 16.7 %collective-permute-start.2 = (bf16[1536,128]{1,0:T(8,128)(2,1)S(1)}, bf16[1536,128]{1,0:T(8,128)(2,1)}, u32[]{:S(2)}, u32[]{:S(2)}) collective-permute-start(bf16[1536,128]{1,0:T(8,128)(2,1)S(1)} %get-tuple-element.243), channel_id=1, source_target_pairs={{0,1},{1,0},{2,3},{3,2},{4,5},{5,4},{6,7},{7,6},{8,9},{9,8},{10,11... | collective-permute-start | bytes 1179656 | tf_op jit(solution)/shard_map/ppermute | solution.py:552
  396.6 11.8 %collective-permute-start.4 = (bf16[512,1024]{1,0:T(8,128)(2,1)S(1)}, bf16[512,1024]{1,0:T(8,128)(2,1)S(1)}, u32[]{:S(2)}, u32[]{:S(2)}) collective-permute-start(bf16[512,1024]{1,0:T(8,128)(2,1)S(1)} %convolution_convert_fusion.2), channel_id=1, source_target_pairs={{0,2},{2,0},{4,6},{6,4},{8,10},{10,8},{12,14},{14,12},{16,18},{18,... | collective-permute-start | bytes 3145736 | tf_op jit(solution)/shard_map/ppermute | solution.py:552
  396.7 16.3 %slice-start = ((s8[16777216]{0:T(1024)(128)(4,1)}), s8[4194304]{0:T(1024)(128)(4,1)S(1)}, s32[]{:S(2)}) async-start(s8[16777216]{0:T(1024)(128)(4,1)} %bitcast.271), calls=%async_computation.5 | async-start | bytes 8388608
  396.7 16.3 %slice-start.1 = ((s8[16777216]{0:T(1024)(128)(4,1)}), s8[4194304]{0:T(1024)(128)(4,1)S(1)}, s32[]{:S(2)}) async-start(s8[16777216]{0:T(1024)(128)(4,1)} %bitcast.271), calls=%async_computation.6 | async-start | bytes 8388608
  400.5 12.6 %slice-start.2 = ((s8[16777216]{0:T(1024)(128)(4,1)}), s8[4194304]{0:T(1024)(128)(4,1)S(1)}, s32[]{:S(2)}) async-start(s8[16777216]{0:T(1024)(128)(4,1)} %bitcast.271), calls=%async_computation.7 | async-start | bytes 8388608
  400.5 2.5 collective-permute-start.7
  403.6 69.6 %collective-permute-start.6 = (bf16[1536,128]{1,0:T(8,128)(2,1)}, bf16[1536,128]{1,0:T(8,128)(2,1)S(1)}, u32[]{:S(2)}, u32[]{:S(2)}) collective-permute-start(bf16[1536,128]{1,0:T(8,128)(2,1)} %get-tuple-element.125), channel_id=1, source_target_pairs={{0,1},{1,0},{2,3},{3,2},{4,5},{5,4},{6,7},{7,6},{8,9},{9,8},{10,11... | collective-permute-start | bytes 1179656 | tf_op jit(solution)/shard_map/ppermute | solution.py:552
  404.5 124.8 %collective-permute-start.8 = (bf16[1536,128]{1,0:T(8,128)(2,1)}, bf16[1536,128]{1,0:T(8,128)(2,1)}, u32[]{:S(2)}, u32[]{:S(2)}) collective-permute-start(bf16[1536,128]{1,0:T(8,128)(2,1)} %get-tuple-element.129), channel_id=1, source_target_pairs={{0,1},{1,0},{2,3},{3,2},{4,5},{5,4},{6,7},{7,6},{8,9},{9,8},{10,11... | collective-permute-start | bytes 1179656 | tf_op jit(solution)/shard_map/ppermute | solution.py:552
  405.7 193.5 %collective-permute-start.12 = (bf16[1536,128]{1,0:T(8,128)(2,1)}, bf16[1536,128]{1,0:T(8,128)(2,1)}, u32[]{:S(2)}, u32[]{:S(2)}) collective-permute-start(bf16[1536,128]{1,0:T(8,128)(2,1)} %get-tuple-element.137), channel_id=1, source_target_pairs={{0,1},{1,0},{2,3},{3,2},{4,5},{5,4},{6,7},{7,6},{8,9},{9,8},{10,11... | collective-permute-start | bytes 1179656 | tf_op jit(solution)/shard_map/ppermute | solution.py:552
  421.6 46.0 %copy-start.6 = (bf16[8,1,64,3072]{3,2,1,0:T(8,128)(2,1)S(1)}, bf16[8,1,64,3072]{3,2,1,0:T(8,128)(2,1)}, u32[]{:S(2)}) copy-start(bf16[8,1,64,3072]{3,2,1,0:T(8,128)(2,1)} %get-tuple-element.213) | copy-start | bytes 9437188
  471.9 59.5 %collective-permute-start.9 = (f32[11,1024]{1,0:T(8,128)}, f32[11,1024]{1,0:T(8,128)S(1)}, u32[]{:S(2)}, u32[]{:S(2)}) collective-permute-start(f32[11,1024]{1,0:T(8,128)} %add.326), channel_id=1, source_target_pairs={{0,4},{2,6},{4,0},{6,2},{8,12},{10,14},{12,8},{14,10},{16,20},{18,... | collective-permute-start | bytes 135176 | tf_op jit(solution)/shard_map/ppermute | solution.py:552
  471.9 67.0 %collective-permute-start.11 = (bf16[512,384]{1,0:T(8,128)(2,1)}, bf16[512,384]{1,0:T(8,128)(2,1)S(1)}, u32[]{:S(2)}, u32[]{:S(2)}) collective-permute-start(bf16[512,384]{1,0:T(8,128)(2,1)} %convolution_convert_fusion.6), channel_id=1, source_target_pairs={{0,2},{2,0},{4,6},{6,4},{8,10},{10,8},{12,14},{14,12},{16,18},{18,... | collective-permute-start | bytes 1179656 | tf_op jit(solution)/shard_map/ppermute | solution.py:552
  473.3 70.8 %collective-permute-start.10 = (bf16[1536,384]{1,0:T(8,128)(2,1)S(1)}, bf16[1536,384]{1,0:T(8,128)(2,1)}, u32[]{:S(2)}, u32[]{:S(2)}) collective-permute-start(bf16[1536,384]{1,0:T(8,128)(2,1)S(1)} %get-tuple-element.221), channel_id=1, source_target_pairs={{0,1},{1,0},{2,3},{3,2},{4,5},{5,4},{6,7},{7,6},{8,9},{9,8},{10,11... | collective-permute-start | bytes 3538952 | tf_op jit(solution)/shard_map/ppermute | solution.py:552
  524.9 14.0 %copy-start.4 = (bf16[8,1,64,3072]{3,2,1,0:T(8,128)(2,1)S(1)}, bf16[8,1,64,3072]{3,2,1,0:T(8,128)(2,1)}, u32[]{:S(2)}) copy-start(bf16[8,1,64,3072]{3,2,1,0:T(8,128)(2,1)} %get-tuple-element.212) | copy-start | bytes 9437188
  524.9 14.1 %copy-start.14 = (bf16[3072,384]{1,0:T(8,128)(2,1)S(1)}, bf16[3072,384]{1,0:T(8,128)(2,1)}, u32[]{:S(2)}) copy-start(bf16[3072,384]{1,0:T(8,128)(2,1)} %get-tuple-element.123) | copy-start | bytes 7077892
  529.3 61.7 %collective-permute-start.15 = (bf16[512,384]{1,0:T(8,128)(2,1)}, bf16[512,384]{1,0:T(8,128)(2,1)}, u32[]{:S(2)}, u32[]{:S(2)}) collective-permute-start(bf16[512,384]{1,0:T(8,128)(2,1)} %convolution_convert_fusion.5), channel_id=1, source_target_pairs={{0,2},{2,0},{4,6},{6,4},{8,10},{10,8},{12,14},{14,12},{16,18},{18,... | collective-permute-start | bytes 1179656 | tf_op jit(solution)/shard_map/ppermute | solution.py:552
  532.2 5.3 collective-permute-start.13
  537.5 67.6 %collective-permute-start.14 = (bf16[1536,384]{1,0:T(8,128)(2,1)}, bf16[1536,384]{1,0:T(8,128)(2,1)}, u32[]{:S(2)}, u32[]{:S(2)}) collective-permute-start(bf16[1536,384]{1,0:T(8,128)(2,1)} %get-tuple-element.223), channel_id=1, source_target_pairs={{0,1},{1,0},{2,3},{3,2},{4,5},{5,4},{6,7},{7,6},{8,9},{9,8},{10,11... | collective-permute-start | bytes 3538952 | tf_op jit(solution)/shard_map/ppermute | solution.py:552
  542.0 53.2 %collective-permute-start.16 = (bf16[2,2,64,1408]{3,2,0,1:T(8,128)(2,1)}, bf16[2,2,64,1408]{3,2,0,1:T(8,128)(2,1)}, u32[]{:S(2)}, u32[]{:S(2)}) collective-permute-start(bf16[2,2,64,1408]{3,2,0,1:T(8,128)(2,1)} %fusion.20), channel_id=1, source_target_pairs={{0,4},{2,6},{4,0},{6,2},{8,12},{10,14},{12,8},{14,10},{16,20},{18,... | collective-permute-start | bytes 2162696 | tf_op jit(solution)/shard_map/ppermute | solution.py:552
  589.9 61.8 %collective-permute-start.26 = (f32[11,1024]{1,0:T(8,128)S(1)}, f32[11,1024]{1,0:T(8,128)S(1)}, u32[]{:S(2)}, u32[]{:S(2)}) collective-permute-start(f32[11,1024]{1,0:T(8,128)S(1)} %add.330), channel_id=1, source_target_pairs={{0,16},{2,18},{4,20},{6,22},{8,24},{10,26},{12,28},{14,30},{16,0},... | collective-permute-start | bytes 135176 | tf_op jit(solution)/shard_map/ppermute | solution.py:552
  595.2 95.5 %collective-permute-start.20 = (bf16[2,2,64,384]{3,2,0,1:T(8,128)(2,1)}, bf16[2,2,64,384]{3,2,0,1:T(8,128)(2,1)}, u32[]{:S(2)}, u32[]{:S(2)}) collective-permute-start(bf16[2,2,64,384]{3,2,0,1:T(8,128)(2,1)} %fusion.55), channel_id=1, source_target_pairs={{0,4},{2,6},{4,0},{6,2},{8,12},{10,14},{12,8},{14,10},{16,20},{18,... | collective-permute-start | bytes 589832 | tf_op jit(solution)/shard_map/ppermute | solution.py:552
  597.3 84.0 %collective-permute-start.19 = (bf16[2,64,1408]{2,1,0:T(8,128)(2,1)}, bf16[2,64,1408]{2,1,0:T(8,128)(2,1)}, u32[]{:S(2)}, u32[]{:S(2)}) collective-permute-start(bf16[2,64,1408]{2,1,0:T(8,128)(2,1)} %fusion.47), channel_id=1, source_target_pairs={{0,8},{2,10},{4,12},{6,14},{8,0},{10,2},{12,4},{14,6},{16,24},{18,... | collective-permute-start | bytes 1081352 | tf_op jit(solution)/shard_map/ppermute | solution.py:552
  599.1 52.7 %collective-permute-start.17 = (bf16[1536,384]{1,0:T(8,128)(2,1)}, bf16[1536,384]{1,0:T(8,128)(2,1)}, u32[]{:S(2)}, u32[]{:S(2)}) collective-permute-start(bf16[1536,384]{1,0:T(8,128)(2,1)} %get-tuple-element.225), channel_id=1, source_target_pairs={{0,1},{1,0},{2,3},{3,2},{4,5},{5,4},{6,7},{7,6},{8,9},{9,8},{10,11... | collective-permute-start | bytes 3538952 | tf_op jit(solution)/shard_map/ppermute | solution.py:552
  605.1 79.2 %collective-permute-start.21 = (bf16[512,384]{1,0:T(8,128)(2,1)}, bf16[512,384]{1,0:T(8,128)(2,1)}, u32[]{:S(2)}, u32[]{:S(2)}) collective-permute-start(bf16[512,384]{1,0:T(8,128)(2,1)} %convolution_convert_fusion.4), channel_id=1, source_target_pairs={{0,2},{2,0},{4,6},{6,4},{8,10},{10,8},{12,14},{14,12},{16,18},{18,... | collective-permute-start | bytes 1179656 | tf_op jit(solution)/shard_map/ppermute | solution.py:552
  605.9 45.8 %copy-start.48 = (f32[2,512]{1,0:T(2,128)S(1)}, f32[2,512]{1,0:T(2,128)}, u32[]{:S(2)}) copy-start(f32[2,512]{1,0:T(2,128)} %copy-done.47) | copy-start | bytes 12292
  605.9 45.8 %copy-start.54 = (f32[2,128]{1,0:T(2,128)S(1)}, f32[2,128]{1,0:T(2,128)}, u32[]{:S(2)}) copy-start(f32[2,128]{1,0:T(2,128)} %get-tuple-element.156) | copy-start | bytes 3076
  652.5 31.7 %collective-permute-start.28 = (f32[2,1024]{1,0:T(2,128)S(1)}, f32[2,1024]{1,0:T(2,128)S(1)}, u32[]{:S(2)}, u32[]{:S(2)}) collective-permute-start(f32[2,1024]{1,0:T(2,128)S(1)} %constant_dynamic-update-slice_fusion.5), channel_id=1, source_target_pairs={{0,1},{1,0},{2,3},{3,2},{4,5},{5,4},{6,7},{7,6},{8,9},{9,8},{10,11... | collective-permute-start | bytes 24584 | tf_op jit(solution)/shard_map/ppermute | solution.py:552
  657.4 37.0 %collective-permute-start.22 = (bf16[512,384]{1,0:T(8,128)(2,1)}, bf16[512,384]{1,0:T(8,128)(2,1)S(1)}, u32[]{:S(2)}, u32[]{:S(2)}) collective-permute-start(bf16[512,384]{1,0:T(8,128)(2,1)} %convolution_convert_fusion.3), channel_id=1, source_target_pairs={{0,2},{2,0},{4,6},{6,4},{8,10},{10,8},{12,14},{14,12},{16,18},{18,... | collective-permute-start | bytes 1179656 | tf_op jit(solution)/shard_map/ppermute | solution.py:552
  667.2 12.1 %copy-start.40 = (f32[2,2,1024]{2,1,0:T(2,128)S(1)}, f32[2,2,1024]{2,1,0:T(2,128)}, u32[]{:S(2)}) copy-start(f32[2,2,1024]{2,1,0:T(2,128)} %param.31) | copy-start | bytes 49156
  667.2 12.0 %copy-start.45 = (f32[2,1024]{1,0:T(2,128)S(1)}, f32[2,1024]{1,0:T(2,128)}, u32[]{:S(2)}) copy-start(f32[2,1024]{1,0:T(2,128)} %param.24) | copy-start | bytes 24580
  667.3 12.7 %copy-start.46 = (f32[2,4096]{1,0:T(2,128)S(1)}, f32[2,4096]{1,0:T(2,128)}, u32[]{:S(2)}) copy-start(f32[2,4096]{1,0:T(2,128)} %param.33) | copy-start | bytes 98308
  667.3 12.8 %copy-start.51 = (f32[4096]{0:T(1024)S(1)}, f32[4096]{0:T(1024)}, u32[]{:S(2)}) copy-start(f32[4096]{0:T(1024)} %param.26) | copy-start | bytes 49156
  667.3 16.9 %copy-start.50 = (f32[2,512]{1,0:T(2,128)S(1)}, f32[2,512]{1,0:T(2,128)}, u32[]{:S(2)}) copy-start(f32[2,512]{1,0:T(2,128)} %copy-done.49) | copy-start | bytes 12292
  682.7 35.7 %collective-permute-start.18 = (bf16[1536,384]{1,0:T(8,128)(2,1)}, bf16[1536,384]{1,0:T(8,128)(2,1)}, u32[]{:S(2)}, u32[]{:S(2)}) collective-permute-start(bf16[1536,384]{1,0:T(8,128)(2,1)} %get-tuple-element.218), channel_id=1, source_target_pairs={{0,1},{1,0},{2,3},{3,2},{4,5},{5,4},{6,7},{7,6},{8,9},{9,8},{10,11... | collective-permute-start | bytes 3538952 | tf_op jit(solution)/shard_map/ppermute | solution.py:552
  684.2 10.2 %copy-start.5 = (bf16[8,1,64,3072]{3,2,1,0:T(8,128)(2,1)S(1)}, bf16[8,1,64,3072]{3,2,1,0:T(8,128)(2,1)}, u32[]{:S(2)}) copy-start(bf16[8,1,64,3072]{3,2,1,0:T(8,128)(2,1)} %get-tuple-element.212) | copy-start | bytes 9437188
  684.2 10.2 %copy-start.12 = (bf16[3072,384]{1,0:T(8,128)(2,1)S(1)}, bf16[3072,384]{1,0:T(8,128)(2,1)}, u32[]{:S(2)}) copy-start(bf16[3072,384]{1,0:T(8,128)(2,1)} %get-tuple-element.147) | copy-start | bytes 7077892
  684.3 4.7 collective-permute-start.29
  689.0 3.7 collective-permute-start.30
  692.7 6.4 collective-permute-start.31
  696.4 14.0 %copy-start.38 = (f32[6,1024]{1,0:T(8,128)S(1)}, f32[6,1024]{1,0:T(8,128)}, u32[]{:S(2)}) copy-start(f32[6,1024]{1,0:T(8,128)} %param.25) | copy-start | bytes 73732
  696.4 11.0 %collective-permute-start.23 = (bf16[2,2,64,768]{3,2,0,1:T(8,128)(2,1)S(1)}, bf16[2,2,64,768]{3,2,0,1:T(8,128)(2,1)}, u32[]{:S(2)}, u32[]{:S(2)}) collective-permute-start(bf16[2,2,64,768]{3,2,0,1:T(8,128)(2,1)S(1)} %fusion.37), channel_id=1, source_target_pairs={{0,4},{2,6},{4,0},{6,2},{8,12},{10,14},{12,8},{14,10},{16,20},{18,... | collective-permute-start | bytes 1179656 | tf_op jit(solution)/shard_map/ppermute | solution.py:552
  699.2 4.6 collective-permute-start.32
  708.6 7.9 %collective-permute-start.24 = (bf16[2,64,1152]{2,1,0:T(8,128)(2,1)S(1)}, bf16[2,64,1152]{2,1,0:T(8,128)(2,1)S(1)}, u32[]{:S(2)}, u32[]{:S(2)}) collective-permute-start(bf16[2,64,1152]{2,1,0:T(8,128)(2,1)S(1)} %fusion.50), channel_id=1, source_target_pairs={{0,8},{2,10},{4,12},{6,14},{8,0},{10,2},{12,4},{14,6},{16,24},{18,... | collective-permute-start | bytes 884744 | tf_op jit(solution)/shard_map/ppermute | solution.py:552
  716.6 15.3 %collective-permute-start.25 = (bf16[64,2560]{1,0:T(8,128)(2,1)S(1)}, bf16[64,2560]{1,0:T(8,128)(2,1)S(1)}, u32[]{:S(2)}, u32[]{:S(2)}) collective-permute-start(bf16[64,2560]{1,0:T(8,128)(2,1)S(1)} %fusion.49), channel_id=1, source_target_pairs={{0,16},{2,18},{4,20},{6,22},{8,24},{10,26},{12,28},{14,30},{16,0},... | collective-permute-start | bytes 983048 | tf_op jit(solution)/shard_map/ppermute | solution.py:552
  735.1 4.4 collective-permute-start.27
  (43 other events, 198.2 us)
Sparse Core Ops, SparseCore 0:
  10.9 47.8 all-gather.4
  62.3 123.4 all-gather.6
  209.6 80.6 all-gather.8
  421.7 198.1 reduce-scatter.1

commit v5 on v4

--- a/solution.py
+++ b/solution.py
@@ -860,8 +860,13 @@
         column_start,
         1,
     )
-    for name, mask in sum_steps():
-        head_biases = head_biases + swap(head_biases, name, mask)
+    for name in ("mp", "dp"):
+        bits = bits_of(lax.axis_size(name))
+        for first in range(0, bits, 2):
+            masks = [mask << first for mask in range(1, 1 << min(2, bits - first))]
+            got = [swap(head_biases, name, mask) for mask in masks]
+            head_biases = head_biases + got[0]
+            head_biases = head_biases + (got[1] + got[2]) if len(got) == 3 else head_biases
     bias_sum = jnp.concatenate([head_biases, late_biases], axis=0)
 
     grad_scale = lax.rsqrt(jnp.float32(tokens * dp))

time: 759 us -> 763 us (level)
    ppermute x33 -> x35, waiting for transfers between devices: 31.6 us -> 33.1 us  [swap(): return lax.ppermute(value, axis_name, [(i, i ^ mask) for i in range(size)])]
    ppermute x33 -> x35, starting transfers between devices: 30 us -> 31.4 us  [swap(): return lax.ppermute(value, axis_name, [(i, i ^ mask) for i in range(size)])]
  transfers between devices with their start and end apart: 37 -> 39, of which waited for: 8 -> 10; matrix products, arithmetic and copies ran while one was open for 25% -> 25% of each run, Pallas kernels for 53% -> 53%
where the time goes in v5:
time: 763 us; the launch traced here: 757 us
  Pallas kernels  466 us (61%)
  matrix products  73.1 us (10%)
  other arithmetic  64.1 us (8%)
  local copies, waits for them, and re-layouts  62.2 us (8%)
  waiting for transfers between devices  43.6 us (6%)
  starting transfers between devices  31.7 us (4%)
  between operations  15.4 us (2%)
    pallas_call x4, Pallas kernels, attention_backward(): pl.pallas_call(functools.partial(backward_kernel, bq, ch, tokens), grid=(...  184 us
    pallas_call x2, Pallas kernels, attention_forward(): pl.pallas_call(functools.partial(forward_kernel, bq, ch, tokens), grid=(c...  126 us
    pallas_call x1, Pallas kernels, feed_back(): pl.pallas_call(functools.partial(feed_back_kernel, rows, ch, blocks), gri...  64 us
    pallas_call x1, Pallas kernels, feed_forward(): pl.pallas_call(functools.partial(feed_kernel, rows, ch), grid=(groups * p...  47.4 us
    ppermute x35, waiting for transfers between devices, swap(): return lax.ppermute(value, axis_name, [(i, i ^ mask) for i in range(size)])  33.1 us
    dot_general x4, matrix products, times_transposed(): lax.dot_general(left_side, right_side, (((1,), (1,)), ((), ())), preferre...  31.9 us
    ppermute x35, starting transfers between devices, swap(): return lax.ppermute(value, axis_name, [(i, i ^ mask) for i in range(size)])  31.4 us
    pallas_call x2, Pallas kernels, norm_call(): pl.pallas_call(kernel, grid=(rows // block,), in_specs=[part] * len(array...  26.5 us
  transfers between devices with their start and end apart: 39, of which 10 were waited for; matrix products, arithmetic and copies ran while one was open for 25% of the time, Pallas kernels for 53%

profile of v5, /device:TPU:0, one launch (start us, length us, event | category | flops | bytes accessed | tf_op | source)
XLA Modules:
  0.0 756.6 jit_solution(9632512748832364718)
XLA Ops:
  10.0 1.4 reduce.15
  14.1 5.2 dynamic-slice_bitcast_fusion.1
  19.4 9.7 %pad_maximum_fusion = (bf16[3072,1024]{1,0:T(8,128)(2,1)}, bf16[1024,3072]{0,1:T(8,128)(2,1)}) fusion(bf16[1536,1024]{1,0:T(8,128)(2,1)} %get-tuple-element.214, bf16[1536,1024]{1,0:T(8,128)(2,1)S(1)} %get-tuple-element.215), kind=kLoop, calls=%fused_computation.1 | loop fusion | flops 12582912 | bytes 18874368 | tf_op jit(solution)/shard_map/concatenate | solution.py:657
  29.1 8.7 %copy.68 = bf16[1024,3072]{1,0:T(8,128)(2,1)} copy(bf16[1024,3072]{0,1:T(8,128)(2,1)} %get-tuple-element.211) | data formatting | bytes 12582912 | tf_op jit(solution)/shard_map/transpose | solution.py:666
  37.8 6.6 constant_dynamic-slice_fusion.10
  46.3 2.1 select_convert_fusion.marks
  48.4 10.4 %all-gather.5.cloned.1.call-done.weights = bf16[1024,1536]{1,0:T(8,128)(2,1)} async-done(((bf16[64,1536]{1,0:T(8,128)(2,1)}), bf16[1024,1536]{1,0:T(8,128)(2,1)}) %all-gather.5.cloned.1.call-update) | async-done | bytes 3145744 | tf_op jit(solution)/shard_map/all_gather | solution.py:661
  59.7 19.4 %project.1 = (bf16[3072,512]{1,0:T(8,128)(2,1)}, bf16[512,3072]{1,0:T(8,128)(2,1)}, bf16[4,3072,256]{2,1,0:T(8,128)(2,1)}, bf16[512,3072]{1,0:T(8,128)(2,1)}, bf...) custom-call(bf16[3072,1024]{1,0:T(8,128)(2,1)} %get-tuple-element.210.x, ...), custom_call_target="tpu_custom_call" | custom-call | flops 603979776 | bytes 1048576 | tf_op jit(solution)/shard_map/project/pallas_call | solution.py:91
  79.1 90.8 %attend.2 = (bf16[3,2,6,3072,512]{4,3,2,1,0:T(8,128)(2,1)}, f32[384,3072]{1,0:T(8,128)}, bf16[3072,384]{1,0:T(8,128)(2,1)}, f32[3,2,3072]{2,1,0:T(2,128)}, f32[3,2,128]{2,1,0:T(2,128)}) custom-call(bf16[4,3072,256]{2,1,0:T(8,128)(2,1)} %get-tuple-element.87.k_cur.k_nxt, bf16[4,3072,256]{2,1,0:T(8,128)(2,1)} %get-tuple-element.87.k_cur.k_nxt, ...), custom_call_target="tpu_custom_call" | custom-call | flops 3623878656 | bytes 1048576 | tf_op jit(solution)/shard_map/attend/pallas_call | solution.py:198
  169.9 3.3 fusion.99
  173.2 1.5 collective-permute-start
  174.6 34.7 %attend.3 = (bf16[1,2,6,3072,512]{4,3,2,1,0:T(8,128)(2,1)}, f32[128,3072]{1,0:T(8,128)}, bf16[3072,128]{1,0:T(8,128)(2,1)}, f32[1,2,3072]{2,1,0:T(2,128)}, f32[1,2,128]{2,1,0:T(2,128)}) custom-call(bf16[4,3072,256]{2,1,0:T(8,128)(2,1)} %get-tuple-element.87.k_cur.k_nxt, bf16[4,3072,256]{2,1,0:T(8,128)(2,1)} %get-tuple-element.87.k_cur.k_nxt, ...), custom_call_target="tpu_custom_call" | custom-call | flops 1207959552 | bytes 1048576 | tf_op jit(solution)/shard_map/attend/pallas_call | solution.py:198
  212.5 2.0 slice.237
  214.8 10.8 %collective-permute-done.1 = bf16[1536,128]{1,0:T(8,128)(2,1)S(1)} collective-permute-done((bf16[1536,128]{1,0:T(8,128)(2,1)S(1)}, bf16[1536,128]{1,0:T(8,128)(2,1)S(1)}, u32[]{:S(2)}, u32[]{:S(2)}) %collective-permute-start.1) | collective-permute-done | bytes 393248 | tf_op jit(solution)/shard_map/ppermute | solution.py:552
  225.6 5.5 fusion.106
  231.9 1.9 copy-done
  233.7 4.8 fusion.94
  238.5 47.4 %feed.1 = (bf16[1536,4096]{1,0:T(8,128)(2,1)}, bf16[1536,4096]{1,0:T(8,128)(2,1)}, f32[1536,1024]{1,0:T(8,128)}) custom-call(bf16[1536,1024]{1,0:T(8,128)(2,1)} %get-tuple-element.208.x.normed, bf16[2,1024,4608]{2,1,0:T(8,128)(2,1)} %bitcast.265, bf16[2,1024,4608]{2,1,0:T(8,128)(2,1)} %bitcast.266, f32[1,4096]{1,0:T(1,128)} %bitcast.304), custom_call_target="tpu_custom_call" | custom-call | flops 25769803776 | bytes 33554432 | tf_op jit(solution)/shard_map/feed/pallas_call | solution.py:378
  285.9 13.7 %second_norm.1 = (bf16[1536,1024]{1,0:T(8,128)(2,1)}, f32[1536,1024]{1,0:T(8,128)}, bf16[1536,1024]{1,0:T(8,128)(2,1)}, f32[3,1024]{1,0:T(4,128)}) custom-call(f32[1536,1024]{1,0:T(8,128)} %get-tuple-element.209.normed, f32[1536,1024]{1,0:T(8,128)} %get-tuple-element.96.fed, bf16[1536,1024]{1,0:T(8,128)(2,1)} %cotangent.1, f32[3,1024]{1,0:T(4,128)} %pad_maximum_fusion.16.lines), custom_call_target="tpu_custom_call" | custom-call | flops 50331648 | bytes 56623104 | tf_op jit(solution)/shard_map/second_norm/pallas_call | solution.py:441
  299.7 64.0 %feed_back.1 = (f32[1,4096]{1,0:T(1,128)}, f32[1536,1024]{1,0:T(8,128)}, bf16[2,8,2,64,2048]{4,3,2,1,0:T(8,128)(2,1)}, f32[2,8,2,64,2048]{4,3,2,1,0:T(8,128)}) custom-call(s32[1]{0:T(128)} %bitcast.15.core, bf16[1536,1024]{1,0:T(8,128)(2,1)} %get-tuple-element.101.x, bf16[1536,1024]{1,0:T(8,128)(2,1)} %get-tuple-element.208.x.normed, ...), custom_call_target="tpu_custom_call" | custom-call | flops 3221225472 | bytes 1048576 | tf_op jit(solution)/shard_map/feed_back/pallas_call | solution.py:517
  365.9 1.4 reduce.16
  367.3 12.8 %first_norm.1 = (f32[1536,1024]{1,0:T(8,128)}, bf16[1536,1024]{1,0:T(8,128)(2,1)}, f32[3,1024]{1,0:T(4,128)}) custom-call(f32[1536,1024]{1,0:T(8,128)} %copy-done, f32[1536,1024]{1,0:T(8,128)} %get-tuple-element.104.fed, f32[1536,1024]{1,0:T(8,128)} %get-tuple-element.105.total_grad, f32[1,1024]{1,0:T(1,128)} %copy-done.43), custom_call_target="tpu_custom_call" | custom-call | flops 50331648 | bytes 56623104 | tf_op jit(solution)/shard_map/first_norm/pallas_call | solution.py:441
  380.1 1.4 pad_maximum_fusion.13
  382.3 3.7 convolution_convert_fusion
  388.4 3.4 copy.70
  393.2 3.6 convolution_convert_fusion.2
  397.0 1.9 convolution_convert_fusion.1
  401.3 1.9 dynamic-slice_bitcast_fusion
  406.7 1.9 pad_maximum_fusion.6.grad
  408.6 4.6 convert_add_fusion
  413.3 8.5 %add_convert_fusion = bf16[2,8,2,64,2048]{4,3,2,1,0:T(8,128)(2,1)} fusion(f32[2,8,2,64,2048]{4,3,2,1,0:T(8,128)S(1)} %bitcast.272, bf16[2,8,2,64,2048]{4,3,2,1,0:T(8,128)(2,1)} %collective-permute-done.3), kind=kLoop, calls=%fused_computation | loop fusion | flops 12582912 | bytes 33554432 | tf_op jit(solution)/shard_map/convert_element_type | solution.py:725
  421.8 46.0 %attend_back.4 = (bf16[3072,384]{1,0:T(8,128)(2,1)}, f32[2,128]{1,0:T(2,128)}) custom-call(bf16[3,2,6,3072,512]{4,3,2,1,0:T(8,128)(2,1)} %get-tuple-element.107.p_ref, bf16[3072,128]{1,0:T(8,128)(2,1)} %pad_maximum_fusion.6.grad, f32[384,3072]{1,0:T(8,128)} %get-tuple-element.118.out_t, f32[3,2,3072]{2,1,0:T(2,128)} %get-tuple-element.119.totals, ...), custom_call_target="tpu_custom_call" | custom-call | flops 2415919104 | bytes 1048576 | tf_op jit(solution)/shard_map/attend_back/pallas_call | solution.py:301
  467.8 4.3 convolution_convert_fusion.6
  475.7 46.0 %attend_back.5 = (bf16[3072,384]{1,0:T(8,128)(2,1)}, f32[2,128]{1,0:T(2,128)}) custom-call(bf16[3,2,6,3072,512]{4,3,2,1,0:T(8,128)(2,1)} %get-tuple-element.107.p_ref, bf16[3072,128]{1,0:T(8,128)(2,1)} %pad_maximum_fusion.7.grad, f32[384,3072]{1,0:T(8,128)} %get-tuple-element.118.out_t, f32[3,2,3072]{2,1,0:T(2,128)} %get-tuple-element.119.totals, ...), custom_call_target="tpu_custom_call" | custom-call | flops 2415919104 | bytes 1048576 | tf_op jit(solution)/shard_map/attend_back/pallas_call | solution.py:301
  521.7 3.4 fusion.97
  525.1 4.4 convolution_convert_fusion.5
  529.7 1.9 pad_maximum_fusion.8.grad
  532.5 2.0 collective-permute-start.13
  534.5 3.2 collective-permute-done.13
  537.7 1.4 collective-permute-start.14
  539.1 1.9 convert_add_fusion.4
  542.1 2.0 collective-permute-start.16
  544.3 45.9 %attend_back.6 = (bf16[3072,384]{1,0:T(8,128)(2,1)}, f32[2,128]{1,0:T(2,128)}) custom-call(bf16[3,2,6,3072,512]{4,3,2,1,0:T(8,128)(2,1)} %get-tuple-element.107.p_ref, bf16[3072,128]{1,0:T(8,128)(2,1)} %pad_maximum_fusion.8.grad, f32[384,3072]{1,0:T(8,128)} %get-tuple-element.118.out_t, f32[3,2,3072]{2,1,0:T(2,128)} %get-tuple-element.119.totals, ...), custom_call_target="tpu_custom_call" | custom-call | flops 2415919104 | bytes 1048576 | tf_op jit(solution)/shard_map/attend_back/pallas_call | solution.py:301
  591.1 3.5 convert_add_fusion.3
  599.4 1.5 collective-permute-start.17
  600.9 1.9 pad_maximum_fusion.9.grad
  602.8 2.6 convolution_convert_fusion.4
  606.2 45.7 %attend_back.7 = (bf16[3072,384]{1,0:T(8,128)(2,1)}, f32[2,128]{1,0:T(2,128)}) custom-call(bf16[1,2,6,3072,512]{4,3,2,1,0:T(8,128)(2,1)} %get-tuple-element.135.p_ref, bf16[3072,128]{1,0:T(8,128)(2,1)} %pad_maximum_fusion.9.grad, f32[128,3072]{1,0:T(8,128)} %get-tuple-element.144.out_t, f32[1,2,3072]{2,1,0:T(2,128)} %get-tuple-element.99.totals, ...), custom_call_target="tpu_custom_call" | custom-call | flops 2415919104 | bytes 1048576 | tf_op jit(solution)/shard_map/attend_back/pallas_call | solution.py:301
  654.1 4.3 convolution_convert_fusion.3
  661.1 7.2 fusion
  668.4 11.3 %add_add_fusion = f32[1536,1024]{1,0:T(8,128)} fusion(f32[1536,1024]{1,0:T(8,128)S(1)} %bitcast.309, f32[1536,1024]{1,0:T(8,128)} %fusion, bf16[1536,384]{1,0:T(8,128)(2,1)} %collective-permute-done.17, bf16[1536,384]{1,0:T(8,128)(2,1)} %collective-permute-done.14, bf16[1536,384]{1,0:T(8,128)(2,1)} %collective-permute-done.10, ...), kind=kOutput, calls=%fused_computation.2 | convolution fusion | flops 3637641216 | bytes 24772608 | tf_op jit(solution)/shard_map/dot_general | solution.py:32
  682.1 1.5 collective-permute-start.18
  684.7 4.6 convert_add_fusion.2
  694.9 1.7 collective-permute-done.30
  696.6 3.3 collective-permute-start.34
  701.0 1.8 convolution_add_fusion.1
  705.0 8.2 %collective-permute-done.23 = bf16[2,2,64,768]{3,2,0,1:T(8,128)(2,1)} collective-permute-done((bf16[2,2,64,768]{3,2,0,1:T(8,128)(2,1)S(1)}, bf16[2,2,64,768]{3,2,0,1:T(8,128)(2,1)}, u32[]{:S(2)}, u32[]{:S(2)}) %collective-permute-start.23) | collective-permute-done | bytes 393248 | tf_op jit(solution)/shard_map/ppermute | solution.py:552
  717.6 3.7 collective-permute-done.24
  721.4 2.7 collective-permute-start.25
  724.1 7.9 %convolution_add_fusion = f32[1536,1024]{1,0:T(8,128)} fusion(f32[1536,1024]{1,0:T(8,128)} %add_add_fusion, bf16[1536,384]{1,0:T(8,128)(2,1)} %collective-permute-done.18, bf16[1024,1536]{1,0:T(8,128)(2,1)} %dynamic-slice_bitcast_fusion), kind=kOutput, calls=%fused_computation.14 | convolution fusion | flops 1209532416 | bytes 14548992 | tf_op jit(solution)/shard_map/dot_general | solution.py:32
  732.0 4.1 collective-permute-done.25
  740.1 2.4 fusion.46
  745.0 3.2 fusion.51
  748.2 1.5 pad_maximum_fusion.4
  (320 shorter events, 65.5 us)
Async XLA Ops:
  7.2 51.6 %all-gather.5.cloned.1.call-start = ((), (), s32[]{:S(2)}) async-start(), calls=%async_computation.1 | async-start | bytes 3342336 | tf_op jit(solution)/shard_map/all_gather | solution.py:661
  9.4 200.0 %all-gather.7.cloned.1.call-start = ((), (), s32[]{:S(2)}) async-start(), calls=%async_computation.2 | async-start | bytes 19464192 | tf_op jit(solution)/shard_map/all_gather | solution.py:678
  44.4 14.7 %slice-start.6 = ((f32[6,1024]{1,0:T(8,128)}), f32[2,1024]{1,0:T(2,128)S(1)}, s32[]{:S(2)}) async-start(f32[6,1024]{1,0:T(8,128)} %param.25), calls=%async_computation.11 | async-start | bytes 16384 | tf_op jit(solution)/shard_map/slice | solution.py:672
  58.8 240.8 %all-gather.9.cloned.1.call-start = ((), (), s32[]{:S(2)}) async-start(), calls=%async_computation.4 | async-start | bytes 9437184 | tf_op jit(solution)/shard_map/all_gather | solution.py:698
  173.2 37.0 %collective-permute-start = (bf16[1536,384]{1,0:T(8,128)(2,1)}, bf16[1536,384]{1,0:T(8,128)(2,1)}, u32[]{:S(2)}, u32[]{:S(2)}) collective-permute-start(bf16[1536,384]{1,0:T(8,128)(2,1)} %get-tuple-element.227), channel_id=1, source_target_pairs={{0,1},{1,0},{2,3},{3,2},{4,5},{5,4},{6,7},{7,6},{8,9},{9,8},{10,11... | collective-permute-start | bytes 3538952 | tf_op jit(solution)/shard_map/ppermute | solution.py:552
  209.5 535.6 %reduce-scatter.2.cloned.1.call-start = ((), (), s32[]{:S(2)}) async-start(), calls=%async_computation.3 | async-start | bytes 8912896 | tf_op jit(solution)/shard_map/reduce_scatter | solution.py:598
  211.3 14.2 %copy-start.33 = (bf16[1536,128]{1,0:T(8,128)(2,1)}, bf16[1536,128]{1,0:T(8,128)(2,1)S(1)}, u32[]{:S(2)}) copy-start(bf16[1536,128]{1,0:T(8,128)(2,1)S(1)} %get-tuple-element.249) | copy-start | bytes 1179652
  211.4 14.2 %collective-permute-start.1 = (bf16[1536,128]{1,0:T(8,128)(2,1)S(1)}, bf16[1536,128]{1,0:T(8,128)(2,1)S(1)}, u32[]{:S(2)}, u32[]{:S(2)}) collective-permute-start(bf16[1536,128]{1,0:T(8,128)(2,1)S(1)} %get-tuple-element.250), channel_id=1, source_target_pairs={{0,1},{1,0},{2,3},{3,2},{4,5},{5,4},{6,7},{7,6},{8,9},{9,8},{10,11... | collective-permute-start | bytes 1179656 | tf_op jit(solution)/shard_map/ppermute | solution.py:552
  211.9 20.0 %copy-start.43 = (f32[1,1024]{1,0:T(1,128)}, f32[1,1024]{1,0:T(1,128)S(1)}, u32[]{:S(2)}) copy-start(f32[1,1024]{1,0:T(1,128)S(1)} %get-tuple-element.287.lines) | copy-start | bytes 12292
  214.7 16.3 %copy-start.26 = (bf16[1024,512]{1,0:T(8,128)(2,1)}, bf16[1024,512]{1,0:T(8,128)(2,1)S(1)}, u32[]{:S(2)}) copy-start(bf16[1024,512]{1,0:T(8,128)(2,1)S(1)} %get-tuple-element.228) | copy-start | bytes 3145732
  214.8 16.3 %copy-start.28 = (bf16[1024,512]{1,0:T(8,128)(2,1)}, bf16[1024,512]{1,0:T(8,128)(2,1)S(1)}, u32[]{:S(2)}) copy-start(bf16[1024,512]{1,0:T(8,128)(2,1)S(1)} %get-tuple-element.229) | copy-start | bytes 3145732
  299.6 64.7 %copy-start.42 = (f32[2,6,1024]{2,0,1:T(2,128)S(1)}, f32[2,6,1024]{2,0,1:T(2,128)}, u32[]{:S(2)}) copy-start(f32[2,6,1024]{2,0,1:T(2,128)} %param.32) | copy-start | bytes 147460
  299.6 65.4 %copy-start.54 = (f32[3,2,128]{2,1,0:T(2,128)S(1)}, f32[3,2,128]{2,1,0:T(2,128)}, u32[]{:S(2)}) copy-start(f32[3,2,128]{2,1,0:T(2,128)} %get-tuple-element.115) | copy-start | bytes 9220
  299.6 65.3 %copy-start.58 = (f32[1,2,128]{2,1,0:T(2,128)S(1)}, f32[1,2,128]{2,1,0:T(2,128)}, u32[]{:S(2)}) copy-start(f32[1,2,128]{2,1,0:T(2,128)} %get-tuple-element.116) | copy-start | bytes 3076
  363.6 49.6 %collective-permute-start.3 = (bf16[2,8,2,64,2048]{4,3,2,1,0:T(8,128)(2,1)}, bf16[2,8,2,64,2048]{4,3,2,1,0:T(8,128)(2,1)}, u32[]{:S(2)}, u32[]{:S(2)}) collective-permute-start(bf16[2,8,2,64,2048]{4,3,2,1,0:T(8,128)(2,1)} %get-tuple-element.110), channel_id=1, source_target_pairs={{0,2},{2,0},{4,6},{6,4},{8,10},{10,8},{12,14},{14,12},{16,18},{18,... | collective-permute-start | bytes 25165832 | tf_op jit(solution)/shard_map/ppermute | solution.py:552
  367.3 12.8 %copy-start.53 = (f32[3,1024]{1,0:T(4,128)S(1)}, f32[3,1024]{1,0:T(4,128)}, u32[]{:S(2)}) copy-start(f32[3,1024]{1,0:T(4,128)} %get-tuple-element.113) | copy-start | bytes 36868
  367.3 15.0 %copy-start.29 = (bf16[1024,512]{1,0:T(8,128)(2,1)S(1)}, bf16[1024,512]{1,0:T(8,128)(2,1)}, u32[]{:S(2)}) copy-start(bf16[1024,512]{1,0:T(8,128)(2,1)} %copy-done.28) | copy-start | bytes 3145732
  381.5 18.4 %collective-permute-start.5 = (f32[11,1024]{1,0:T(8,128)}, f32[11,1024]{1,0:T(8,128)}, u32[]{:S(2)}, u32[]{:S(2)}) collective-permute-start(f32[11,1024]{1,0:T(8,128)} %pad_maximum_fusion.13), channel_id=1, source_target_pairs={{0,1},{1,0},{2,3},{3,2},{4,5},{5,4},{6,7},{7,6},{8,9},{9,8},{10,11... | collective-permute-start | bytes 135176 | tf_op jit(solution)/shard_map/ppermute | solution.py:552
  387.1 16.8 %collective-permute-start.2 = (bf16[1536,128]{1,0:T(8,128)(2,1)S(1)}, bf16[1536,128]{1,0:T(8,128)(2,1)}, u32[]{:S(2)}, u32[]{:S(2)}) collective-permute-start(bf16[1536,128]{1,0:T(8,128)(2,1)S(1)} %get-tuple-element.243), channel_id=1, source_target_pairs={{0,1},{1,0},{2,3},{3,2},{4,5},{5,4},{6,7},{7,6},{8,9},{9,8},{10,11... | collective-permute-start | bytes 1179656 | tf_op jit(solution)/shard_map/ppermute | solution.py:552
  396.9 11.8 %collective-permute-start.4 = (bf16[512,1024]{1,0:T(8,128)(2,1)S(1)}, bf16[512,1024]{1,0:T(8,128)(2,1)S(1)}, u32[]{:S(2)}, u32[]{:S(2)}) collective-permute-start(bf16[512,1024]{1,0:T(8,128)(2,1)S(1)} %convolution_convert_fusion.2), channel_id=1, source_target_pairs={{0,2},{2,0},{4,6},{6,4},{8,10},{10,8},{12,14},{14,12},{16,18},{18,... | collective-permute-start | bytes 3145736 | tf_op jit(solution)/shard_map/ppermute | solution.py:552
  397.0 16.3 %slice-start = ((s8[16777216]{0:T(1024)(128)(4,1)}), s8[4194304]{0:T(1024)(128)(4,1)S(1)}, s32[]{:S(2)}) async-start(s8[16777216]{0:T(1024)(128)(4,1)} %bitcast.271), calls=%async_computation.5 | async-start | bytes 8388608
  397.0 16.3 %slice-start.1 = ((s8[16777216]{0:T(1024)(128)(4,1)}), s8[4194304]{0:T(1024)(128)(4,1)S(1)}, s32[]{:S(2)}) async-start(s8[16777216]{0:T(1024)(128)(4,1)} %bitcast.271), calls=%async_computation.6 | async-start | bytes 8388608
  400.7 12.5 %slice-start.2 = ((s8[16777216]{0:T(1024)(128)(4,1)}), s8[4194304]{0:T(1024)(128)(4,1)S(1)}, s32[]{:S(2)}) async-start(s8[16777216]{0:T(1024)(128)(4,1)} %bitcast.271), calls=%async_computation.7 | async-start | bytes 8388608
  400.8 2.5 collective-permute-start.7
  403.9 69.6 %collective-permute-start.6 = (bf16[1536,128]{1,0:T(8,128)(2,1)}, bf16[1536,128]{1,0:T(8,128)(2,1)S(1)}, u32[]{:S(2)}, u32[]{:S(2)}) collective-permute-start(bf16[1536,128]{1,0:T(8,128)(2,1)} %get-tuple-element.125), channel_id=1, source_target_pairs={{0,1},{1,0},{2,3},{3,2},{4,5},{5,4},{6,7},{7,6},{8,9},{9,8},{10,11... | collective-permute-start | bytes 1179656 | tf_op jit(solution)/shard_map/ppermute | solution.py:552
  404.7 124.8 %collective-permute-start.8 = (bf16[1536,128]{1,0:T(8,128)(2,1)}, bf16[1536,128]{1,0:T(8,128)(2,1)}, u32[]{:S(2)}, u32[]{:S(2)}) collective-permute-start(bf16[1536,128]{1,0:T(8,128)(2,1)} %get-tuple-element.129), channel_id=1, source_target_pairs={{0,1},{1,0},{2,3},{3,2},{4,5},{5,4},{6,7},{7,6},{8,9},{9,8},{10,11... | collective-permute-start | bytes 1179656 | tf_op jit(solution)/shard_map/ppermute | solution.py:552
  405.9 193.4 %collective-permute-start.12 = (bf16[1536,128]{1,0:T(8,128)(2,1)}, bf16[1536,128]{1,0:T(8,128)(2,1)}, u32[]{:S(2)}, u32[]{:S(2)}) collective-permute-start(bf16[1536,128]{1,0:T(8,128)(2,1)} %get-tuple-element.137), channel_id=1, source_target_pairs={{0,1},{1,0},{2,3},{3,2},{4,5},{5,4},{6,7},{7,6},{8,9},{9,8},{10,11... | collective-permute-start | bytes 1179656 | tf_op jit(solution)/shard_map/ppermute | solution.py:552
  421.8 46.0 %copy-start.6 = (bf16[8,1,64,3072]{3,2,1,0:T(8,128)(2,1)S(1)}, bf16[8,1,64,3072]{3,2,1,0:T(8,128)(2,1)}, u32[]{:S(2)}) copy-start(bf16[8,1,64,3072]{3,2,1,0:T(8,128)(2,1)} %get-tuple-element.213) | copy-start | bytes 9437188
  472.1 59.5 %collective-permute-start.9 = (f32[11,1024]{1,0:T(8,128)}, f32[11,1024]{1,0:T(8,128)S(1)}, u32[]{:S(2)}, u32[]{:S(2)}) collective-permute-start(f32[11,1024]{1,0:T(8,128)} %add.332), channel_id=1, source_target_pairs={{0,4},{2,6},{4,0},{6,2},{8,12},{10,14},{12,8},{14,10},{16,20},{18,... | collective-permute-start | bytes 135176 | tf_op jit(solution)/shard_map/ppermute | solution.py:552
  472.1 66.9 %collective-permute-start.11 = (bf16[512,384]{1,0:T(8,128)(2,1)}, bf16[512,384]{1,0:T(8,128)(2,1)S(1)}, u32[]{:S(2)}, u32[]{:S(2)}) collective-permute-start(bf16[512,384]{1,0:T(8,128)(2,1)} %convolution_convert_fusion.6), channel_id=1, source_target_pairs={{0,2},{2,0},{4,6},{6,4},{8,10},{10,8},{12,14},{14,12},{16,18},{18,... | collective-permute-start | bytes 1179656 | tf_op jit(solution)/shard_map/ppermute | solution.py:552
  473.5 70.8 %collective-permute-start.10 = (bf16[1536,384]{1,0:T(8,128)(2,1)S(1)}, bf16[1536,384]{1,0:T(8,128)(2,1)}, u32[]{:S(2)}, u32[]{:S(2)}) collective-permute-start(bf16[1536,384]{1,0:T(8,128)(2,1)S(1)} %get-tuple-element.221), channel_id=1, source_target_pairs={{0,1},{1,0},{2,3},{3,2},{4,5},{5,4},{6,7},{7,6},{8,9},{9,8},{10,11... | collective-permute-start | bytes 3538952 | tf_op jit(solution)/shard_map/ppermute | solution.py:552
  525.1 14.0 %copy-start.4 = (bf16[8,1,64,3072]{3,2,1,0:T(8,128)(2,1)S(1)}, bf16[8,1,64,3072]{3,2,1,0:T(8,128)(2,1)}, u32[]{:S(2)}) copy-start(bf16[8,1,64,3072]{3,2,1,0:T(8,128)(2,1)} %get-tuple-element.212) | copy-start | bytes 9437188
  525.1 14.0 %copy-start.15 = (bf16[3072,384]{1,0:T(8,128)(2,1)S(1)}, bf16[3072,384]{1,0:T(8,128)(2,1)}, u32[]{:S(2)}) copy-start(bf16[3072,384]{1,0:T(8,128)(2,1)} %get-tuple-element.123) | copy-start | bytes 7077892
  529.5 61.6 %collective-permute-start.15 = (bf16[512,384]{1,0:T(8,128)(2,1)}, bf16[512,384]{1,0:T(8,128)(2,1)}, u32[]{:S(2)}, u32[]{:S(2)}) collective-permute-start(bf16[512,384]{1,0:T(8,128)(2,1)} %convolution_convert_fusion.5), channel_id=1, source_target_pairs={{0,2},{2,0},{4,6},{6,4},{8,10},{10,8},{12,14},{14,12},{16,18},{18,... | collective-permute-start | bytes 1179656 | tf_op jit(solution)/shard_map/ppermute | solution.py:552
  532.5 5.1 collective-permute-start.13
  537.7 67.7 %collective-permute-start.14 = (bf16[1536,384]{1,0:T(8,128)(2,1)}, bf16[1536,384]{1,0:T(8,128)(2,1)}, u32[]{:S(2)}, u32[]{:S(2)}) collective-permute-start(bf16[1536,384]{1,0:T(8,128)(2,1)} %get-tuple-element.223), channel_id=1, source_target_pairs={{0,1},{1,0},{2,3},{3,2},{4,5},{5,4},{6,7},{7,6},{8,9},{9,8},{10,11... | collective-permute-start | bytes 3538952 | tf_op jit(solution)/shard_map/ppermute | solution.py:552
  542.1 53.2 %collective-permute-start.16 = (bf16[2,2,64,1408]{3,2,0,1:T(8,128)(2,1)}, bf16[2,2,64,1408]{3,2,0,1:T(8,128)(2,1)}, u32[]{:S(2)}, u32[]{:S(2)}) collective-permute-start(bf16[2,2,64,1408]{3,2,0,1:T(8,128)(2,1)} %fusion.20), channel_id=1, source_target_pairs={{0,4},{2,6},{4,0},{6,2},{8,12},{10,14},{12,8},{14,10},{16,20},{18,... | collective-permute-start | bytes 2162696 | tf_op jit(solution)/shard_map/ppermute | solution.py:552
  590.1 62.7 %collective-permute-start.26 = (f32[11,1024]{1,0:T(8,128)S(1)}, f32[11,1024]{1,0:T(8,128)S(1)}, u32[]{:S(2)}, u32[]{:S(2)}) collective-permute-start(f32[11,1024]{1,0:T(8,128)S(1)} %add.336), channel_id=1, source_target_pairs={{0,16},{2,18},{4,20},{6,22},{8,24},{10,26},{12,28},{14,30},{16,0},... | collective-permute-start | bytes 135176 | tf_op jit(solution)/shard_map/ppermute | solution.py:552
  595.4 86.7 %collective-permute-start.20 = (bf16[2,2,64,384]{3,2,0,1:T(8,128)(2,1)}, bf16[2,2,64,384]{3,2,0,1:T(8,128)(2,1)}, u32[]{:S(2)}, u32[]{:S(2)}) collective-permute-start(bf16[2,2,64,384]{3,2,0,1:T(8,128)(2,1)} %fusion.55), channel_id=1, source_target_pairs={{0,4},{2,6},{4,0},{6,2},{8,12},{10,14},{12,8},{14,10},{16,20},{18,... | collective-permute-start | bytes 589832 | tf_op jit(solution)/shard_map/ppermute | solution.py:552
  597.5 92.5 %collective-permute-start.19 = (bf16[2,64,1408]{2,1,0:T(8,128)(2,1)}, bf16[2,64,1408]{2,1,0:T(8,128)(2,1)}, u32[]{:S(2)}, u32[]{:S(2)}) collective-permute-start(bf16[2,64,1408]{2,1,0:T(8,128)(2,1)} %fusion.47), channel_id=1, source_target_pairs={{0,8},{2,10},{4,12},{6,14},{8,0},{10,2},{12,4},{14,6},{16,24},{18,... | collective-permute-start | bytes 1081352 | tf_op jit(solution)/shard_map/ppermute | solution.py:552
  599.4 53.5 %collective-permute-start.17 = (bf16[1536,384]{1,0:T(8,128)(2,1)}, bf16[1536,384]{1,0:T(8,128)(2,1)}, u32[]{:S(2)}, u32[]{:S(2)}) collective-permute-start(bf16[1536,384]{1,0:T(8,128)(2,1)} %get-tuple-element.225), channel_id=1, source_target_pairs={{0,1},{1,0},{2,3},{3,2},{4,5},{5,4},{6,7},{7,6},{8,9},{9,8},{10,11... | collective-permute-start | bytes 3538952 | tf_op jit(solution)/shard_map/ppermute | solution.py:552
  605.4 79.3 %collective-permute-start.21 = (bf16[512,384]{1,0:T(8,128)(2,1)}, bf16[512,384]{1,0:T(8,128)(2,1)}, u32[]{:S(2)}, u32[]{:S(2)}) collective-permute-start(bf16[512,384]{1,0:T(8,128)(2,1)} %convolution_convert_fusion.4), channel_id=1, source_target_pairs={{0,2},{2,0},{4,6},{6,4},{8,10},{10,8},{12,14},{14,12},{16,18},{18,... | collective-permute-start | bytes 1179656 | tf_op jit(solution)/shard_map/ppermute | solution.py:552
  606.2 46.6 %copy-start.49 = (f32[2,512]{1,0:T(2,128)S(1)}, f32[2,512]{1,0:T(2,128)}, u32[]{:S(2)}) copy-start(f32[2,512]{1,0:T(2,128)} %copy-done.48) | copy-start | bytes 12292
  606.2 46.6 %copy-start.55 = (f32[2,128]{1,0:T(2,128)S(1)}, f32[2,128]{1,0:T(2,128)}, u32[]{:S(2)}) copy-start(f32[2,128]{1,0:T(2,128)} %get-tuple-element.156) | copy-start | bytes 3076
  653.6 38.1 %collective-permute-start.28 = (f32[2,1024]{1,0:T(2,128)S(1)}, f32[2,1024]{1,0:T(2,128)S(1)}, u32[]{:S(2)}, u32[]{:S(2)}) collective-permute-start(f32[2,1024]{1,0:T(2,128)S(1)} %constant_dynamic-update-slice_fusion.5), channel_id=1, source_target_pairs={{0,1},{1,0},{2,3},{3,2},{4,5},{5,4},{6,7},{7,6},{8,9},{9,8},{10,11... | collective-permute-start | bytes 24584 | tf_op jit(solution)/shard_map/ppermute | solution.py:552
  658.5 42.5 %collective-permute-start.22 = (bf16[512,384]{1,0:T(8,128)(2,1)}, bf16[512,384]{1,0:T(8,128)(2,1)S(1)}, u32[]{:S(2)}, u32[]{:S(2)}) collective-permute-start(bf16[512,384]{1,0:T(8,128)(2,1)} %convolution_convert_fusion.3), channel_id=1, source_target_pairs={{0,2},{2,0},{4,6},{6,4},{8,10},{10,8},{12,14},{14,12},{16,18},{18,... | collective-permute-start | bytes 1179656 | tf_op jit(solution)/shard_map/ppermute | solution.py:552
  668.3 12.4 %copy-start.41 = (f32[2,2,1024]{2,1,0:T(2,128)S(1)}, f32[2,2,1024]{2,1,0:T(2,128)}, u32[]{:S(2)}) copy-start(f32[2,2,1024]{2,1,0:T(2,128)} %param.31) | copy-start | bytes 49156
  668.4 13.0 %copy-start.47 = (f32[2,4096]{1,0:T(2,128)S(1)}, f32[2,4096]{1,0:T(2,128)}, u32[]{:S(2)}) copy-start(f32[2,4096]{1,0:T(2,128)} %param.33) | copy-start | bytes 98308
  668.4 13.1 %copy-start.52 = (f32[4096]{0:T(1024)S(1)}, f32[4096]{0:T(1024)}, u32[]{:S(2)}) copy-start(f32[4096]{0:T(1024)} %param.26) | copy-start | bytes 49156
  668.4 15.3 %copy-start.21 = (f32[2,2,64,384]{3,2,0,1:T(8,128)S(1)}, f32[2,2,64,384]{3,2,0,1:T(8,128)}, u32[]{:S(2)}) copy-start(f32[2,2,64,384]{3,2,0,1:T(8,128)} %copy_bitcast_fusion.1) | copy-start | bytes 1179652
  682.1 42.0 %collective-permute-start.18 = (bf16[1536,384]{1,0:T(8,128)(2,1)}, bf16[1536,384]{1,0:T(8,128)(2,1)}, u32[]{:S(2)}, u32[]{:S(2)}) collective-permute-start(bf16[1536,384]{1,0:T(8,128)(2,1)} %get-tuple-element.218), channel_id=1, source_target_pairs={{0,1},{1,0},{2,3},{3,2},{4,5},{5,4},{6,7},{7,6},{8,9},{9,8},{10,11... | collective-permute-start | bytes 3538952 | tf_op jit(solution)/shard_map/ppermute | solution.py:552
  684.7 16.3 %copy-start.5 = (bf16[8,1,64,3072]{3,2,1,0:T(8,128)(2,1)S(1)}, bf16[8,1,64,3072]{3,2,1,0:T(8,128)(2,1)}, u32[]{:S(2)}) copy-start(bf16[8,1,64,3072]{3,2,1,0:T(8,128)(2,1)} %get-tuple-element.212) | copy-start | bytes 9437188
  684.7 16.3 %copy-start.12 = (bf16[3072,384]{1,0:T(8,128)(2,1)S(1)}, bf16[3072,384]{1,0:T(8,128)(2,1)}, u32[]{:S(2)}) copy-start(bf16[3072,384]{1,0:T(8,128)(2,1)} %get-tuple-element.147) | copy-start | bytes 7077892
  691.7 3.1 collective-permute-start.31
  692.9 3.7 collective-permute-start.30
  693.4 3.2 collective-permute-start.29
  696.6 7.1 collective-permute-start.34
  699.8 4.5 collective-permute-start.33
  700.1 4.3 collective-permute-start.32
  703.0 14.0 %copy-start.39 = (f32[6,1024]{1,0:T(8,128)S(1)}, f32[6,1024]{1,0:T(8,128)}, u32[]{:S(2)}) copy-start(f32[6,1024]{1,0:T(8,128)} %param.25) | copy-start | bytes 73732
  703.0 10.1 %collective-permute-start.23 = (bf16[2,2,64,768]{3,2,0,1:T(8,128)(2,1)S(1)}, bf16[2,2,64,768]{3,2,0,1:T(8,128)(2,1)}, u32[]{:S(2)}, u32[]{:S(2)}) collective-permute-start(bf16[2,2,64,768]{3,2,0,1:T(8,128)(2,1)S(1)} %fusion.37), channel_id=1, source_target_pairs={{0,4},{2,6},{4,0},{6,2},{8,12},{10,14},{12,8},{14,10},{16,20},{18,... | collective-permute-start | bytes 1179656 | tf_op jit(solution)/shard_map/ppermute | solution.py:552
  714.3 7.0 collective-permute-start.24
  721.4 14.7 %collective-permute-start.25 = (bf16[64,2560]{1,0:T(8,128)(2,1)S(1)}, bf16[64,2560]{1,0:T(8,128)(2,1)S(1)}, u32[]{:S(2)}, u32[]{:S(2)}) collective-permute-start(bf16[64,2560]{1,0:T(8,128)(2,1)S(1)} %fusion.49), channel_id=1, source_target_pairs={{0,16},{2,18},{4,20},{6,22},{8,24},{10,26},{12,28},{14,30},{16,0},... | collective-permute-start | bytes 983048 | tf_op jit(solution)/shard_map/ppermute | solution.py:552
  739.3 4.3 collective-permute-start.27
  (46 other events, 219.3 us)
Sparse Core Ops, SparseCore 0:
  10.9 47.8 all-gather.4
  62.3 123.4 all-gather.6
  209.6 80.6 all-gather.8
  421.9 198.1 reduce-scatter.1
